TPU v7x, 32 devices: a whole 2x2x4 slice. The times are simulated.
32 devices in a mesh: lon: 4 (over z), lat: 4 (over x, core), mp: 2 (over y).
Axes of the slice: x: 2, y: 2, z: 4, core: 2. Of those that a mesh axis runs over, the one named last changes fastest.
Arguments:
- fields: bfloat16 [160, 32, 2240], P('lat', 'lon', 'mp'), may hold values from -6 to 6
- shift_offsets: int32 [20], replicated, may hold values from 1 to 7, as said below
- w_embed: bfloat16 [2240, 1536], P('mp'), may hold values from -0.125 to 0.125
- w_qkv: bfloat16 [1536, 3, 768], P(None, None, 'mp'), may hold values from -0.15625 to 0.15625
- w_proj: bfloat16 [768, 1536], P('mp'), may hold values from -0.21875 to 0.21875
- w_head: bfloat16 [1536, 1120], P('mp'), may hold values from -0.15625 to 0.15625
- log_scale: float32 [12], P('mp'), may hold values from 1.6 to 5.3
- bias_table: float32 [12, 225], P('mp'), may hold values from -130 to 130
- cotangent: bfloat16 [160, 32, 1120], P(('lat', 'mp'), 'lon'), may hold values from -0.3125 to 0.3125
Outputs:
- prediction: bfloat16 [160, 32, 1120], P(('lat', 'mp'), 'lon')
- grad_qkv: float32 [1536, 3, 768], P(('lon', 'lat'), None, 'mp')
- grad_proj: float32 [768, 1536], P('mp', ('lon', 'lat'))
Inputs may be any that keep to these rules, and one draw needn't show every extreme that they name: `shift_offsets`: in every draw some row of windows has the shift 7.
All inputs are finite; a program needn't handle non-finite values.
Results may differ from a plain program's by a relative error of at most 0.035.
Values may be sent and summed in bfloat16 or wider, within the bound.
No kernel may reach another device: no remote copies, remote signals or barrier semaphores. Data moves between devices by JAX's collectives and lax.ppermute only.
A program may use at most 128 MiB of HBM per device.

v0:
```python
import jax
import jax.numpy as jnp
from jax import lax
from jax.sharding import PartitionSpec as P

HD = 64
WIN = 8


eps = 1e-06
scale_cap = 4.605170185988092


def passed_along(value, axis, steps):
    count = lax.axis_size(axis)
    pairs = [(source, (source + steps) % count) for source in range(count)]
    return lax.ppermute(value, axis, pairs)


def offset_onehot(window):
    span = window * window
    places = jnp.arange(span, dtype=jnp.int32)
    across = places // window
    along = places % window
    code = (across[:, None] - across[None, :] + window - 1) * (2 * window - 1) + (
        along[:, None] - along[None, :] + window - 1
    )
    entries = jnp.arange((2 * window - 1) ** 2, dtype=jnp.int32)
    return (code[:, :, None] == entries[None, None, :]).astype(jnp.float32)


def window_attention(query_rows, key_rows, value_rows, scales, biases):
    query_f = query_rows.astype(jnp.float32)
    key_f = key_rows.astype(jnp.float32)
    value_f = value_rows.astype(jnp.float32)
    query_n = query_f * lax.rsqrt(jnp.sum(query_f * query_f, -1, keepdims=True) + eps)
    key_n = key_f * lax.rsqrt(jnp.sum(key_f * key_f, -1, keepdims=True) + eps)
    scores = (
        jnp.einsum("wihd,wjhd->whij", query_n, key_n) * scales[None, :, None, None] + biases[None]
    )
    top = jnp.max(scores, -1, keepdims=True)
    weights = jnp.exp(scores - top)
    probs = (weights / jnp.sum(weights, -1, keepdims=True)).astype(jnp.bfloat16)
    return jnp.einsum("whij,wjhd->wihd", probs.astype(jnp.float32), value_f)


def to_windows(grid, window):
    height, breadth, channels = grid.shape
    blocks = grid.reshape(height // window, window, breadth // window, window, channels)
    return blocks.transpose(0, 2, 1, 3, 4).reshape(-1, window * window, channels)


def from_windows(blocks, height, breadth, window):
    channels = blocks.shape[2]
    grid = blocks.reshape(height // window, breadth // window, window, window, channels)
    return grid.transpose(0, 2, 1, 3, 4).reshape(height, breadth, channels)


def roll_left(grid, offsets, window):
    rim = passed_along(grid[:, : window - 1], "lon", -1)
    wide = jnp.concatenate([grid, rim], axis=1)
    blocks = wide.reshape(offsets.shape[0], window, wide.shape[1], wide.shape[2])
    moved = jax.vmap(
        lambda block, amount: lax.dynamic_slice_in_dim(block, amount, grid.shape[1], 1)
    )(blocks, offsets)
    return moved.reshape(grid.shape)


def roll_right(grid, offsets, window):
    rim = passed_along(grid[:, grid.shape[1] - window + 1 :], "lon", 1)
    wide = jnp.concatenate([rim, grid], axis=1)
    blocks = wide.reshape(offsets.shape[0], window, wide.shape[1], wide.shape[2])
    moved = jax.vmap(
        lambda block, amount: lax.dynamic_slice_in_dim(block, window - 1 - amount, grid.shape[1], 1)
    )(blocks, offsets)
    return moved.reshape(grid.shape)


def local(fields, shift_offsets, w_embed, w_qkv, w_proj, w_head, log_scale, bias_table, cotangent):
    height, breadth = (fields.shape[0], fields.shape[1])
    count = height * breadth
    span = WIN * WIN
    count_win = count // span
    model_width = w_embed.shape[1]
    heads_here = w_qkv.shape[2] // HD
    groups = height // WIN
    offsets = lax.dynamic_slice_in_dim(shift_offsets, lax.axis_index("lat") * groups, groups)
    embed_term = jnp.dot(fields.reshape(count, -1), w_embed, preferred_element_type=jnp.float32)
    embedded = (
        lax.psum_scatter(embed_term, "mp", scatter_dimension=1, tiled=True)
        .astype(jnp.bfloat16)
        .reshape(height, breadth, -1)
    )
    rolled = roll_left(embedded, offsets, WIN)
    all_channels = lax.all_gather(rolled, "mp", axis=2, tiled=True)
    win_tokens = to_windows(all_channels, WIN).reshape(count, model_width)
    qkv = jnp.dot(win_tokens, w_qkv.reshape(model_width, -1), preferred_element_type=jnp.float32)
    qkv = qkv.astype(jnp.bfloat16).reshape(count_win, span, 3, heads_here, HD)
    scales = jnp.exp(jnp.minimum(log_scale, scale_cap))
    biases = jnp.einsum(
        "ije,he->hij", offset_onehot(WIN), bias_table, precision=lax.Precision.HIGHEST
    )

    def attend(query_rows, key_rows, value_rows):
        return window_attention(query_rows, key_rows, value_rows, scales, biases)

    out_f, pullback = jax.vjp(attend, qkv[:, :, 0], qkv[:, :, 1], qkv[:, :, 2])
    attended = out_f.astype(jnp.bfloat16).reshape(count, -1)
    proj_term = jnp.dot(attended, w_proj, preferred_element_type=jnp.float32)
    mixed = lax.psum_scatter(proj_term, "mp", scatter_dimension=1, tiled=True).astype(jnp.bfloat16)
    mixed_grid = from_windows(mixed.reshape(count_win, span, -1), height, breadth, WIN)
    restored = roll_right(mixed_grid, offsets, WIN)
    merged = (
        (embedded.astype(jnp.float32) + restored.astype(jnp.float32))
        .astype(jnp.bfloat16)
        .reshape(count, -1)
    )
    prediction = lax.psum_scatter(
        jnp.dot(merged, w_head, preferred_element_type=jnp.float32),
        "mp",
        scatter_dimension=0,
        tiled=True,
    ).astype(jnp.bfloat16)
    prediction = prediction.reshape(height // lax.axis_size("mp"), breadth, -1)
    upstream = lax.dot_general(
        lax.all_gather(cotangent.reshape(-1, cotangent.shape[2]), "mp", axis=0, tiled=True),
        w_head,
        (((1,), (1,)), ((), ())),
        preferred_element_type=jnp.float32,
    )
    upstream = upstream.astype(jnp.bfloat16).reshape(height, breadth, -1)
    upstream_rolled = to_windows(roll_left(upstream, offsets, WIN), WIN).reshape(count, -1)
    piece = lax.all_gather(upstream_rolled, "mp", axis=1, tiled=True)
    d_total = lax.dot_general(
        piece, w_proj, (((1,), (1,)), ((), ())), preferred_element_type=jnp.float32
    )
    block_grad = lax.dot_general(
        attended, piece, (((0,), (0,)), ((), ())), preferred_element_type=jnp.float32
    )
    d_attended = d_total
    d_attended = d_attended.astype(jnp.bfloat16).reshape(count_win, span, heads_here, HD)
    d_query, d_key, d_value = pullback(d_attended.astype(jnp.float32))
    d_qkv = jnp.stack([d_query, d_key, d_value], 2).reshape(count, -1)
    cycle_size = lax.axis_size("lon")
    band_size = lax.axis_size("lat")
    term = lax.dot_general(
        win_tokens, d_qkv, (((0,), (0,)), ((), ())), preferred_element_type=jnp.float32
    )
    grad_qkv = lax.psum_scatter(
        term.reshape(
            model_width // (cycle_size * band_size) * lax.axis_size(("lon", "lat")), 3, -1
        ),
        ("lon", "lat"),
        scatter_dimension=0,
        tiled=True,
    )
    grad_proj = lax.psum_scatter(block_grad, ("lon", "lat"), scatter_dimension=1, tiled=True)
    return (prediction, grad_qkv, grad_proj)


def solution(mesh):
    in_specs = (
        P("lat", "lon", "mp"),
        P(),
        P("mp", None),
        P(None, None, "mp"),
        P("mp", None),
        P("mp", None),
        P("mp"),
        P("mp", None),
        P(("lat", "mp"), "lon", None),
    )
    out_specs = (
        P(("lat", "mp"), "lon", None),
        P(("lon", "lat"), None, "mp"),
        P("mp", ("lon", "lat")),
    )
    return jax.shard_map(local, mesh=mesh, in_specs=in_specs, out_specs=out_specs, check_vma=False)
```

profile of v0, /device:TPU:0, one launch (start us, length us, event | category | flops | bytes accessed | tf_op | source)
XLA Modules:
  0.0 355.6 jit_solution(18187920089905380395)
XLA Ops:
  7.2 1.9 copy-done
  9.1 3.8 %fusion.17 = f32[320,1536]{1,0:T(8,128)} fusion(bf16[1120,1536]{1,0:T(8,128)(2,1)S(1)} %copy-done, bf16[40,8,1120]{2,1,0:T(8,128)(2,1)} %param.9), kind=kOutput, calls=%fused_computation.51 | convolution fusion | flops 1101004800 | bytes 6123520 | tf_op jit(solution)/shard_map/dot_general | solution.py:88
  13.2 33.1 %reduce-scatter.6.cloned.1.call-done = f32[320,768]{1,0:T(8,128)} async-done(((f32[320,1536]{1,0:T(8,128)}), f32[320,768]{1,0:T(8,128)}) %reduce-scatter.6.cloned.1.call-update) | async-done | bytes 983056 | tf_op jit(solution)/shard_map/reduce_scatter | solution.py:90
  47.5 3.4 collective-permute-start
  50.9 3.2 fusion.6
  54.9 6.2 %copy.34 = bf16[1536,3,384]{0,2,1:T(8,128)(2,1)} copy(bf16[1536,3,384]{2,0,1:T(8,128)(2,1)} %param.12) | data formatting | bytes 7077888 | tf_op args[3]
  62.2 13.3 %all_gather.9 = bf16[40,8,1536]{2,1,0:T(8,128)(2,1)S(1)} all-gather(bf16[40,8,768]{2,1,0:T(8,128)(2,1)S(1)} %bitcast.135), channel_id=1, replica_groups=mesh['lon'=4,'lat'=4,'mp'=2] {'mp'}, dimensions={2}, use_global_device_ids=true | all-gather | bytes 1474560 | tf_op jit(solution)/shard_map/all_gather | solution.py:95
  76.5 4.4 %convolution_convert_fusion = bf16[320,1152]{1,0:T(8,128)(2,1)} fusion(bf16[1536,1152]{0,1:T(8,128)(2,1)} %bitcast.132, bf16[40,8,1536]{2,1,0:T(8,128)(2,1)S(1)} %all_gather.9), kind=kOutput, calls=%fused_computation.5 | convolution fusion | flops 1132830720 | bytes 5259264 | tf_op jit(solution)/shard_map/dot_general | solution.py:97
  80.9 2.6 reshape.212
  83.5 1.5 fusion.49
  84.9 1.5 copy.67
  91.9 1.5 reshape.213
  93.4 3.2 fusion.51
  96.7 30.9 %reduce-scatter.8.cloned.1.call-done = f32[320,768]{1,0:T(8,128)} async-done(((f32[320,1536]{1,0:T(8,128)}), f32[320,768]{1,0:T(8,128)}) %reduce-scatter.8.cloned.1.call-update) | async-done | bytes 983056 | tf_op jit(solution)/shard_map/reduce_scatter | solution.py:110
  129.0 1.5 collective-permute-start.1
  130.7 13.1 %collective-permute-done.1 = bf16[40,7,768]{2,1,0:T(8,128)(2,1)S(1)} collective-permute-done((bf16[40,7,768]{2,1,0:T(8,128)(2,1)S(1)}, bf16[40,7,768]{2,1,0:T(8,128)(2,1)S(1)}, u32[]{:S(2)}, u32[]{:S(2)}) %collective-permute-start.1) | collective-permute-done | bytes 430112 | tf_op jit(solution)/shard_map/ppermute | solution.py:17
  144.9 2.6 gather_fusion.1
  149.1 2.0 fusion.52
  151.1 16.3 %all_gather.10 = bf16[320,1120]{1,0:T(8,128)(2,1)S(1)} all-gather(bf16[160,1120]{1,0:T(8,128)(2,1)} %bitcast.145), channel_id=1, replica_groups=mesh['lon'=4,'lat'=4,'mp'=2] {'mp'}, dimensions={0}, use_global_device_ids=true | all-gather | bytes 1075200 | tf_op jit(solution)/shard_map/all_gather | solution.py:126
  167.5 2.3 convolution_convert_fusion.4
  169.9 8.7 %collective-permute-done.2 = bf16[40,7,768]{2,1,0:T(8,128)(2,1)S(1)} collective-permute-done((bf16[40,7,768]{2,1,0:T(8,128)(2,1)S(1)}, bf16[40,7,768]{2,1,0:T(8,128)(2,1)S(1)}, u32[]{:S(2)}, u32[]{:S(2)}) %collective-permute-start.2) | collective-permute-done | bytes 430112 | tf_op jit(solution)/shard_map/ppermute | solution.py:17
  181.3 9.7 %all_gather.11 = bf16[320,1536]{1,0:T(8,128)(2,1)S(1)} all-gather(bf16[320,768]{1,0:T(8,128)(2,1)S(1)} %bitcast.137), channel_id=1, replica_groups=mesh['lon'=4,'lat'=4,'mp'=2] {'mp'}, dimensions={1}, use_global_device_ids=true | all-gather | bytes 1474560 | tf_op jit(solution)/shard_map/all_gather | solution.py:133
  191.0 2.4 fusion.53
  193.4 2.0 convolution_convert_fusion.5
  196.9 1.9 convert_reduce_fusion
  202.1 1.4 copy.55
  203.5 1.9 reshape.218
  205.5 1.7 copy.56
  207.2 5.1 %fusion.13 = f32[1536,3,384]{2,0,1:T(8,128)} fusion(bf16[3,384,320]{2,1,0:T(8,128)(2,1)S(1)} %bitcast.131, bf16[40,8,1536]{2,1,0:T(8,128)(2,1)S(1)} %copy-done.4), kind=kOutput, calls=%fused_computation.37 | convolution fusion | flops 1132462080 | bytes 8798208 | tf_op jit(solution)/shard_map/dot_general | solution.py:146
  212.4 2.0 convert_bitcast_fusion
  214.4 40.6 %reduce-scatter.14.cloned.1.call-done = f32[384,96]{0,1:T(8,128)} async-done(((f32[384,1536]{0,1:T(8,128)}), f32[384,96]{0,1:T(8,128)}) %reduce-scatter.14.cloned.1.call-update) | async-done | bytes 147472 | tf_op jit(solution)/shard_map/reduce_scatter | solution.py:157
  255.1 93.9 %reduce-scatter.12.cloned.1.call-done = f32[96,3,384]{2,0,1:T(8,128)} async-done(((f32[1536,3,384]{2,0,1:T(8,128)}), f32[96,3,384]{2,0,1:T(8,128)}) %reduce-scatter.12.cloned.1.call-update) | async-done | bytes 442384 | tf_op jit(solution)/shard_map/reduce_scatter | solution.py:149
  (92 shorter events, 21.7 us)
Async XLA Ops:
  7.2 2.0 copy-start
  7.2 39.1 %reduce-scatter.6.cloned.1.call-start = ((), (), s32[]{:S(2)}) async-start(), calls=%async_computation.5 | async-start | bytes 2949120 | tf_op jit(solution)/shard_map/reduce_scatter | solution.py:90
  13.0 37.9 %copy-start.14 = (f32[6,225]{1,0:T(8,128)S(1)}, f32[6,225]{1,0:T(8,128)}, u32[]{:S(2)}) copy-start(f32[6,225]{1,0:T(8,128)} %param.16) | copy-start | bytes 16204
  13.0 114.5 %reduce-scatter.8.cloned.1.call-start = ((), (), s32[]{:S(2)}) async-start(), calls=%async_computation.6 | async-start | bytes 2949120 | tf_op jit(solution)/shard_map/reduce_scatter | solution.py:110
  47.5 13.8 %collective-permute-start = (bf16[40,7,768]{2,1,0:T(8,128)(2,1)S(1)}, bf16[40,7,768]{2,1,0:T(8,128)(2,1)S(1)}, u32[]{:S(2)}, u32[]{:S(2)}) collective-permute-start(bf16[40,7,768]{2,1,0:T(8,128)(2,1)S(1)} %bitcast.142), channel_id=1, source_target_pairs={{0,24},{8,0},{16,8},{24,16},{1,25},{9,1},{17,9},{25,17},{2,26},{10... | collective-permute-start | bytes 1290248 | tf_op jit(solution)/shard_map/ppermute | solution.py:17
  54.9 6.2 %copy-start.13 = (s32[20]{0:T(128)S(1)}, s32[20]{0:T(128)}, u32[]{:S(2)}) copy-start(s32[20]{0:T(128)} %param.10) | copy-start | bytes 244
  54.9 6.2 %copy-start.15 = (f32[6]{0:T(128)S(1)}, f32[6]{0:T(128)}, u32[]{:S(2)}) copy-start(f32[6]{0:T(128)} %param.15) | copy-start | bytes 76
  54.9 6.3 %copy-start.2 = (f32[320,768]{1,0:T(8,128)S(1)}, f32[320,768]{1,0:T(8,128)}, u32[]{:S(2)}) copy-start(f32[320,768]{1,0:T(8,128)} %reduce-scatter.6.cloned.1.call-done) | copy-start | bytes 2949124
  75.6 0.9 copy-start.3
  84.9 3.3 copy-start.6
  86.4 3.0 copy-start.8
  86.6 2.8 copy-start.11
  89.3 1.0 copy-start.9
  96.6 115.8 %reduce-scatter.10.cloned.1.call-start = ((), (), s32[]{:S(2)}) async-start(), calls=%async_computation.7 | async-start | bytes 2211840 | tf_op jit(solution)/shard_map/reduce_scatter | solution.py:118
  127.6 3.0 copy-start.5
  129.0 14.8 %collective-permute-start.1 = (bf16[40,7,768]{2,1,0:T(8,128)(2,1)S(1)}, bf16[40,7,768]{2,1,0:T(8,128)(2,1)S(1)}, u32[]{:S(2)}, u32[]{:S(2)}) collective-permute-start(bf16[40,7,768]{2,1,0:T(8,128)(2,1)S(1)} %slice.40), channel_id=1, source_target_pairs={{0,8},{8,16},{16,24},{24,0},{1,9},{9,17},{17,25},{25,1},{2,10},{10... | collective-permute-start | bytes 1290248 | tf_op jit(solution)/shard_map/ppermute | solution.py:17
  147.5 1.6 copy-start.7
  151.1 104.0 %reduce-scatter.14.cloned.1.call-start = ((), (), s32[]{:S(2)}) async-start(), calls=%async_computation.9 | async-start | bytes 2506752 | tf_op jit(solution)/shard_map/reduce_scatter | solution.py:157
  169.7 8.9 %collective-permute-start.2 = (bf16[40,7,768]{2,1,0:T(8,128)(2,1)S(1)}, bf16[40,7,768]{2,1,0:T(8,128)(2,1)S(1)}, u32[]{:S(2)}, u32[]{:S(2)}) collective-permute-start(bf16[40,7,768]{2,1,0:T(8,128)(2,1)S(1)} %bitcast.143), channel_id=1, source_target_pairs={{0,24},{8,0},{16,8},{24,16},{1,25},{9,1},{17,9},{25,17},{2,26},{10... | collective-permute-start | bytes 1290248 | tf_op jit(solution)/shard_map/ppermute | solution.py:17
  193.4 155.7 %reduce-scatter.12.cloned.1.call-start = ((), (), s32[]{:S(2)}) async-start(), calls=%async_computation.8 | async-start | bytes 7520256 | tf_op jit(solution)/shard_map/reduce_scatter | solution.py:149
  199.2 0.7 copy-start.12
  199.7 1.0 copy-start.10
  203.5 3.7 %copy-start.4 = (bf16[40,8,1536]{2,1,0:T(8,128)(2,1)S(1)}, bf16[40,8,1536]{2,1,0:T(8,128)(2,1)}, u32[]{:S(2)}) copy-start(bf16[40,8,1536]{2,1,0:T(8,128)(2,1)} %copy-done.3) | copy-start | bytes 2949124
  212.4 136.7 %copy-start.1 = (bf16[1120,1536]{1,0:T(8,128)(2,1)S(1)}, bf16[1120,1536]{1,0:T(8,128)(2,1)}, u32[]{:S(2)}) copy-start(bf16[1120,1536]{1,0:T(8,128)(2,1)} %param.11) | copy-start | bytes 10321924
Sparse Core Ops, SparseCore 0:
  13.1 33.0 reduce-scatter.5
  96.7 30.7 reduce-scatter.7
  151.2 27.2 reduce-scatter.9
  193.5 61.5 reduce-scatter.13
  260.0 88.9 reduce-scatter.11
where the time goes:
time: 357 us; the launch traced here: 356 us
  waiting for transfers between devices  221 us (62%)
  blocking collectives  39.4 us (11%)
  local copies, waits for them, and re-layouts  36 us (10%)
  matrix products  32.2 us (9%)
  between operations  14.2 us (4%)
  other arithmetic  8.07 us (2%)
  starting transfers between devices  5.17 us (1%)
    reduce_scatter x1, waiting for transfers between devices, local(): lax.psum_scatter(term.reshape(model_width // (cycle_size * band_size) * l...  93.9 us
    reduce_scatter x1, waiting for transfers between devices, local(): lax.psum_scatter(block_grad, ('lon', 'lat'), scatter_dimension=1, tiled=T...  40.6 us
    reduce_scatter x1, waiting for transfers between devices, local(): lax.psum_scatter(embed_term, 'mp', scatter_dimension=1, tiled=True)  33.1 us
    reduce_scatter x1, waiting for transfers between devices, local(): lax.psum_scatter(proj_term, 'mp', scatter_dimension=1, tiled=True)  30.9 us
    ppermute x3, waiting for transfers between devices, passed_along(): return lax.ppermute(value, axis, pairs)  21.9 us
    all_gather x1, blocking collectives, local(): lax.all_gather(cotangent.reshape(-1, cotangent.shape[2]), 'mp', axis=0, t...  16.3 us
    unnamed x36, local copies, waits for them, and re-layouts  14.2 us
    all_gather x1, blocking collectives, local(): all_channels = lax.all_gather(rolled, 'mp', axis=2, tiled=True)  13.3 us
  transfers between devices with their start and end apart: 8, of which 6 were waited for; matrix products, arithmetic and copies ran while one was open for 11% of the time, Pallas kernels for 0%

commit v1 on v0

v1 whole, which is shorter than its diff:
```python
import functools

import jax
import jax.numpy as jnp
from jax import lax
from jax.experimental import pallas as pl
from jax.experimental.pallas import tpu as pltpu
from jax.sharding import PartitionSpec as P

HD = 64
WIN = 8
SPAN = WIN * WIN
PAIR = 2 * HD

eps = 1e-06
scale_cap = 4.605170185988092

BF = jnp.bfloat16
F32 = jnp.float32
F16 = jnp.float16
TERM_SCALE = 64.0
VMEM_LIMIT = 30 * 1024 * 1024
SMALL_LIMIT = 24 * 1024 * 1024


def moved(value, axis, steps):
    count = lax.axis_size(axis)
    pairs = [(source, (source + steps) % count) for source in range(count)]
    return lax.ppermute(value, axis, pairs)


def swapped(value, axis, bit):
    count = lax.axis_size(axis)
    return lax.ppermute(value, axis, [(source, source ^ bit) for source in range(count)])


def spec(space=pltpu.VMEM):
    return pl.BlockSpec(memory_space=space)


def call(body, out_shape, kinds, micros, scratch=(), limit=VMEM_LIMIT):
    return pl.pallas_call(
        body,
        out_shape=out_shape,
        in_specs=[spec(pltpu.SMEM) if kind == "s" else spec() for kind in kinds],
        out_specs=jax.tree.map(lambda _: spec(), out_shape),
        scratch_shapes=list(scratch),
        compiler_params=pltpu.CompilerParams(vmem_limit_bytes=limit),
        cost_estimate=pl.CostEstimate(flops=int(micros * 1.0e9), bytes_accessed=1, transcendentals=0),
    )


def after(value, *others):
    return lax.optimization_barrier((value,) + others)[0]


def shape(dims, dtype=BF):
    return jax.ShapeDtypeStruct(tuple(dims), dtype)


def dot(a, b, ca=1, cb=0):
    return lax.dot_general(a, b, (((ca,), (cb,)), ((), ())), preferred_element_type=F32)


def rolled_block(own, other, shift):
    size = own.shape[0]
    row = lax.broadcasted_iota(jnp.int32, (size, size), 0)
    col = lax.broadcasted_iota(jnp.int32, (size, size), 1)
    target = (row & (WIN - 1)) + shift
    same = ((row >> 3) == (col >> 3)) & ((col & (WIN - 1)) == (target & (WIN - 1)))
    inside = (target >= 0) & (target < WIN)
    mine = jnp.where(same & inside, 1.0, 0.0).astype(BF)
    theirs = jnp.where(same & ~inside, 1.0, 0.0).astype(BF)
    return (dot(mine, own) + dot(theirs, other)).astype(BF)


def roll_kernel(sign, shifts, own, other, out):
    for block in range(own.shape[0]):
        out[block] = rolled_block(own[block], other[block], sign * shifts[block])


def roll_call(shifts, own, other, sign):
    body = functools.partial(roll_kernel, sign)
    return call(body, jax.ShapeDtypeStruct(own.shape, BF), "svv", 2)(shifts, own, other)


def embed_kernel(shifts, own, other, weight, out, gathered):
    for block in range(own.shape[0]):
        gathered[pl.ds(block * SPAN, SPAN), :] = rolled_block(
            own[block], other[block], shifts[block]
        )
    out[...] = dot(gathered[...], weight[...]) * TERM_SCALE


def embed_call(shifts, own, other, weight):
    rows = own.shape[0] * SPAN
    width = weight.shape[1]
    return call(
        embed_kernel,
        jax.ShapeDtypeStruct((rows, width), F32),
        "svvv",
        5,
        [pltpu.VMEM((rows, weight.shape[0]), BF)],
    )(shifts, own, other, weight)


def halves(value):
    left = lax.broadcasted_iota(jnp.int32, value.shape, 1) < HD
    zero = jnp.zeros_like(value)
    return jnp.concatenate([jnp.where(left, value, zero), jnp.where(left, zero, value)], 0)


def joined(value):
    top = value[:SPAN]
    left = lax.broadcasted_iota(jnp.int32, top.shape, 1) < HD
    return jnp.where(left, top, value[SPAN:])


def two_parts(value):
    high = value.astype(BF)
    return high, (value - high.astype(F32)).astype(BF)


def head_ones():
    row = lax.broadcasted_iota(jnp.int32, (PAIR, PAIR), 0)
    col = lax.broadcasted_iota(jnp.int32, (PAIR, PAIR), 1)
    return jnp.where((row < HD) == (col < HD), 1.0, 0.0).astype(BF)


def head_sums(value, ones):
    high, low = two_parts(value)
    return dot(high, ones) + dot(low, ones)


def square(value):
    wide = value.astype(F32)
    return wide * wide


def row_norms(query_halves):
    high, low = two_parts(square(query_halves))
    ones = jnp.ones((WIN, PAIR), BF)
    total = dot(ones, high, 1, 1) + dot(ones, low, 1, 1)
    return lax.rsqrt(total[:1] + eps)


def forward_kernel(rolled, w_qkv, scales, biases, qkv, probs, attended):
    width = w_qkv.shape[2]
    for part in range(3):
        qkv[:, part * width : (part + 1) * width] = dot(rolled[...], w_qkv[part]).astype(BF)
    ones = head_ones()
    pairs = width // PAIR
    for window in range(rolled.shape[0] // SPAN):
        rows = pl.ds(window * SPAN, SPAN)
        for pair in range(pairs):
            lanes = pl.ds(pair * PAIR, PAIR)
            query = qkv[rows, lanes]
            key = qkv[rows, pl.ds(width + pair * PAIR, PAIR)]
            value = qkv[rows, pl.ds(2 * width + pair * PAIR, PAIR)]
            query_halves = halves(query)
            key_norm = lax.rsqrt(head_sums(square(key), ones) + eps)
            query_norm = row_norms(query_halves) * scales[pair]
            scores = dot(key, query_halves, 1, 1) * key_norm * query_norm + biases[pair]
            weights = jnp.exp(scores - jnp.max(scores, 0, keepdims=True))
            share = weights * (1.0 / jnp.sum(weights, 0, keepdims=True))
            probs[window, pair] = share
            attended[rows, lanes] = joined(dot(share.astype(BF), value, 0, 0)).astype(BF)


def forward_call(mine, theirs, w_qkv, scales, biases):
    rolled = ((mine.astype(F32) + theirs.astype(F32)) * (1.0 / TERM_SCALE)).astype(BF)
    rows = rolled.shape[0]
    width = w_qkv.shape[2]
    pairs = width // PAIR
    out_shape = (
        shape((rows, 3 * width)),
        shape((rows // SPAN, pairs, SPAN, PAIR), F32),
        shape((rows, width)),
    )
    got = call(forward_kernel, out_shape, "vvvv", 9)(rolled, w_qkv, scales, biases)
    return (rolled,) + tuple(got)


def unit_grad(value, norm, grad, ones):
    wide = value.astype(F32)
    along = head_sums(wide * grad, ones)
    return norm * (grad - wide * (norm * norm) * along)


def backward_kernel(chunks, place, own_up, other_up, w_proj, scales, *refs):
    width, model = w_proj.shape
    d_qk, d_value, d_att = refs[2 * chunks :]
    half = model // 2
    mine = pl.ds(pl.multiple_of(place[0] * half, PAIR), half)
    theirs = pl.ds(pl.multiple_of((1 - place[0]) * half, PAIR), half)
    d_att[...] = (
        dot(own_up[...], w_proj[:, mine], 1, 1) + dot(other_up[...], w_proj[:, theirs], 1, 1)
    ).astype(BF)
    first = 0
    for qkv, probs in zip(refs[:chunks], refs[chunks : 2 * chunks]):
        backward_chunk(first, qkv, probs, scales, d_att, d_qk, d_value)
        first += probs.shape[0]


def backward_chunk(first, qkv, probs, scales, d_att, d_qk, d_value):
    width = d_att.shape[1]
    ones = head_ones()
    for window in range(probs.shape[0]):
        rows = pl.ds((first + window) * SPAN, SPAN)
        for pair in range(width // PAIR):
            spots = [pl.ds(part * width + pair * PAIR, PAIR) for part in range(3)]
            query, key, value = [qkv[pl.ds(window * SPAN, SPAN), spot] for spot in spots]
            query_halves = halves(query)
            key_norm = lax.rsqrt(head_sums(square(key), ones) + eps)
            query_norm = lax.rsqrt(head_sums(square(query), ones) + eps)
            query_lanes = row_norms(query_halves)
            share = probs[window, pair]
            grad_halves = halves(d_att[rows, pl.ds(pair * PAIR, PAIR)])
            d_value[rows, spots[0]] = dot(share.astype(BF), grad_halves).astype(BF)
            d_probs = dot(value, grad_halves, 1, 1).astype(BF).astype(F32)
            mean = jnp.sum(d_probs * share, 0, keepdims=True)
            d_cos = share * (d_probs - mean) * scales[pair]
            d_query = joined(dot((d_cos * key_norm).astype(BF), key, 0, 0))
            d_key = dot((d_cos * query_lanes).astype(BF), query_halves)
            d_qk[rows, spots[0]] = unit_grad(query, query_norm, d_query, ones).astype(BF)
            d_qk[rows, spots[1]] = unit_grad(key, key_norm, d_key, ones).astype(BF)


def backward_call(place, own_up, other_up, w_proj, scales, qkv, probs):
    rows = own_up.shape[0]
    width = w_proj.shape[0]
    return call(
        functools.partial(backward_kernel, len(qkv)),
        (shape((rows, 2 * width)), shape((rows, width))),
        "svvvv" + "vv" * len(qkv),
        9,
        [pltpu.VMEM((rows, width), BF)],
        SMALL_LIMIT,
    )(place, own_up, other_up, w_proj, scales, *qkv, *probs)


def half_up_kernel(place, own, other, w_head_t, out):
    rows = own.shape[0]
    out[pl.ds(pl.multiple_of(place[0] * rows, 32), rows), :] = dot(own[...], w_head_t[...]).astype(BF)
    out[pl.ds(pl.multiple_of((1 - place[0]) * rows, 32), rows), :] = dot(
        other[...], w_head_t[...]
    ).astype(BF)


def half_up_call(place, own, other, w_head_t):
    rows, depth = own.shape
    width = w_head_t.shape[1]
    return call(
        half_up_kernel, shape((2 * rows, width)), "svvv", 3
    )(place, own, other, w_head_t)


def mix_kernel(chunks, place, w_proj, *refs):
    att, keep, send = refs[:chunks], refs[chunks], refs[chunks + 1]
    half = w_proj.shape[1] // 2
    mine = pl.ds(pl.multiple_of(place[0] * half, PAIR), half)
    theirs = pl.ds(pl.multiple_of((1 - place[0]) * half, PAIR), half)
    start = 0
    for a in att:
        rows = pl.ds(start, a.shape[0])
        send[rows, :] = dot(a[...], w_proj[:, theirs]).astype(BF)
        keep[rows, :] = dot(a[...], w_proj[:, mine]).astype(BF)
        start += a.shape[0]


def mix_call(place, w_proj, attended):
    count = sum(a.shape[0] for a in attended)
    width, model = w_proj.shape
    out = shape((count, model // 2))
    return call(
        functools.partial(mix_kernel, len(attended)),
        (out, out),
        "sv" + "v" * len(attended),
        3,
    )(place, w_proj, *attended)


def head_kernel(chunks, place, mine, theirs, w_head_t, *refs):
    rolled, keep, send, merged = refs[:chunks], refs[chunks], refs[chunks + 1], refs[chunks + 2]
    half = w_head_t.shape[1]
    lanes = pl.ds(pl.multiple_of(place[0] * half, PAIR), half)
    start = 0
    for a in rolled:
        rows = pl.ds(start, a.shape[0])
        mixed = (mine[rows, :].astype(F32) + theirs[rows, :].astype(F32)).astype(BF)
        merged[rows, :] = (a[:, lanes].astype(F32) + mixed.astype(F32)).astype(BF)
        start += a.shape[0]
    count = keep.shape[0]
    own = pl.ds(pl.multiple_of(place[0] * count, 32), count)
    other = pl.ds(pl.multiple_of((1 - place[0]) * count, 32), count)
    send[...] = dot(merged[other, :], w_head_t[...], 1, 1).astype(BF)
    keep[...] = dot(merged[own, :], w_head_t[...], 1, 1).astype(BF)


def head_call(place, mine, theirs, w_head_t, rolled):
    count, half = mine.shape
    outputs = w_head_t.shape[0]
    out = shape((count // 2, outputs))
    return call(
        functools.partial(head_kernel, len(rolled)),
        (out, out),
        "svvv" + "v" * len(rolled),
        4,
        [pltpu.VMEM((count, half), BF)],
    )(place, mine, theirs, w_head_t, *rolled)


def offset_onehot(window):
    span = window * window
    places = jnp.arange(span, dtype=jnp.int32)
    across = places // window
    along = places % window
    code = (across[:, None] - across[None, :] + window - 1) * (2 * window - 1) + (
        along[:, None] - along[None, :] + window - 1
    )
    entries = jnp.arange((2 * window - 1) ** 2, dtype=jnp.int32)
    return (code[:, :, None] == entries[None, None, :]).astype(F32)


def bits_of(axis):
    bits = []
    bit = 1
    while bit < lax.axis_size(axis):
        bits.append((axis, bit))
        bit *= 2
    return bits


def my_bit(axis, bit):
    return (lax.axis_index(axis) // bit) % 2


class Sum:
    def __init__(self, keep, send, order):
        self.dims = [("lon", bit) for _, bit in reversed(bits_of("lon"))]
        self.dims += [("lat", bit) for _, bit in reversed(bits_of("lat"))][:-1]
        self.rows = keep.shape[1:]
        self.order = list(order)
        self.keep = keep
        self.got = swapped(send, "lat", 1)

    def step(self):
        axis, bit = self.order.pop(0)
        place = self.dims.index((axis, bit))
        cut = (2,) * len(self.dims) + self.rows
        keep, got = self.keep.reshape(cut), self.got.reshape(cut)
        mine = my_bit(axis, bit)

        def total(index):
            a = lax.dynamic_index_in_dim(keep, index, place, keepdims=False)
            b = lax.dynamic_index_in_dim(got, index, place, keepdims=False)
            return (a.astype(F32) + b.astype(F32)).astype(BF)

        send = total(1 - mine)
        self.keep = total(mine)
        self.got = swapped(send, axis, bit)
        self.dims.pop(place)
        return send

    def result(self):
        while self.order:
            self.step()
        return self.keep.reshape(self.rows).astype(F32) + self.got.reshape(self.rows).astype(F32)


def cut_pieces(value, pieces, axis):
    size = value.shape[axis] // pieces
    value = value.reshape(value.shape[:axis] + (pieces // 2, 2, size) + value.shape[axis + 1 :])
    low = my_bit("lat", 1)
    return [lax.dynamic_index_in_dim(value, bit, axis + 1, keepdims=False) for bit in (low, 1 - low)]


def local(fields, shift_offsets, w_embed, w_qkv, w_proj, w_head, log_scale, bias_table, cotangent):
    height, breadth, depth = fields.shape
    groups = height // WIN
    model = w_embed.shape[1]
    outputs = w_head.shape[1]
    width = w_qkv.shape[2]
    pairs = width // PAIR
    lat, mp = lax.axis_index("lat"), lax.axis_index("mp")
    rows_here = cotangent.shape[0]
    offsets = lax.dynamic_slice_in_dim(shift_offsets, lat * groups, groups)
    strip = 4
    strips = rows_here // strip
    firsts = mp * rows_here + strip * jnp.arange(strips, dtype=jnp.int32)
    strip_offsets = jnp.take(offsets, firsts // WIN)
    place = mp.reshape(1)
    pieces = lax.axis_size("lon") * lax.axis_size("lat")
    z_bits = bits_of("lon")
    x_bits = bits_of("lat")[1:]

    cuts = [0, 2, groups]
    tiles = fields.reshape(groups, SPAN, depth)
    tiles = [tiles[first:last] for first, last in zip(cuts[:-1], cuts[1:])]
    shifts = [offsets[first:last] for first, last in zip(cuts[:-1], cuts[1:])]
    cot = cotangent.reshape(-1, outputs)
    next_tiles = [moved(tile, "lon", -1) for tile in tiles]
    other_cot = swapped(cot, "mp", 1)

    scales = jnp.exp(jnp.minimum(log_scale, scale_cap))
    scales = jnp.repeat(scales.reshape(pairs, 1, 2), HD, axis=2)
    biases = jnp.einsum(
        "ije,he->hji", offset_onehot(WIN), bias_table, precision=lax.Precision.HIGHEST
    )
    biases = biases.reshape(pairs, 2, SPAN, SPAN).transpose(0, 2, 1, 3).reshape(pairs, SPAN, PAIR)

    half_up = half_up_call(place, cot, other_cot, w_head.T)
    next_tiles[0], half_up, biases = lax.optimization_barrier((next_tiles[0], half_up, biases))
    terms, other_terms = [], []
    for index, (shift, tile, next_tile) in enumerate(zip(shifts, tiles, next_tiles)):
        if terms:
            next_tile = after(next_tile, terms[-1])
            half_up = after(half_up, next_tile)
        terms.append(embed_call(shift, tile, next_tile, w_embed).astype(F16))
        other_terms.append(swapped(terms[-1], "mp", 1))
    half_up = half_up.reshape(groups, SPAN, -1)
    own_up = roll_call(offsets, half_up, moved(half_up, "lon", -1), 1)
    own_up = own_up.reshape(groups * SPAN, -1)
    other_up = swapped(after(own_up, other_terms[-1]), "mp", 1)

    w_parts = w_qkv.transpose(1, 0, 2)
    rolled, qkv, probs, attended = zip(
        *[forward_call(a, b, w_parts, scales, biases) for a, b in zip(terms, other_terms)]
    )
    mixed_here, mixed_there = mix_call(place, w_proj, attended)
    left_keep, left_send = [
        side.reshape(groups * SPAN, -1)
        for side in cut_pieces(jnp.concatenate(rolled, 0), pieces, 1)
    ]
    all_attended = jnp.concatenate(attended, 0)
    other_up, mixed_here, left_keep, left_send, all_attended = lax.optimization_barrier(
        (other_up, mixed_here, left_keep, left_send, all_attended)
    )
    mixed_got = swapped(after(mixed_there, other_up), "mp", 1)
    up = jnp.where(
        mp == 0, jnp.concatenate([own_up, other_up], 1), jnp.concatenate([other_up, own_up], 1)
    )
    keep, send = cut_pieces(dot(up, all_attended, 0, 0).astype(BF), pieces, 0)
    sum_p = Sum(keep, send, x_bits + z_bits)

    d_qk, d_value = backward_call(
        place, own_up, after(other_up, send), w_proj, scales, qkv, probs
    )

    def products(left, right):
        return dot(left, right, 0, 0).astype(BF).reshape(pieces // 2, model // pieces, -1)

    sum_p.got = after(sum_p.got, d_qk)
    sent = sum_p.step()
    pred_here, pred_there = head_call(place, after(mixed_here, sent), mixed_got, w_head.T, rolled)
    v_send = products(left_send, after(d_value, pred_there))
    sum_p.got = after(sum_p.got, v_send)
    sent = sum_p.step()
    qk_send = products(left_send, after(d_qk, sent))
    v_keep = products(left_keep, after(d_value, qk_send))
    sum_v = Sum(v_keep, v_send, x_bits + z_bits)
    sum_v.got = after(sum_v.got, qk_send)
    sent = sum_v.step()
    qk_keep = products(left_keep, after(d_qk, sent))
    sum_qk = Sum(qk_keep, qk_send, x_bits + z_bits)
    sum_qk.got = after(sum_qk.got, sent)
    sent = sum_qk.step()
    sum_p.got = after(sum_p.got, sent)
    sent = sum_p.step()
    pred_got = after(swapped(pred_there, "mp", 1), sent)
    pred = (pred_here.astype(F32) + pred_got.astype(F32)).astype(BF)
    pred = pred.reshape(strips, strip * WIN, outputs)
    before = moved(pred, "lon", 1)
    sum_v.got = after(sum_v.got, pred)
    sent = sum_v.step()
    sum_p.got = after(sum_p.got, sent)
    grad_proj = sum_p.result().T
    sum_v.got = after(sum_v.got, grad_proj)
    sent = sum_v.step()
    sum_qk.got = after(sum_qk.got, sent)
    sent = sum_qk.step()
    before = after(before, sent)
    prediction = roll_call(strip_offsets, pred, before, -1).reshape(rows_here, breadth, outputs)
    grad_v = sum_v.result()
    sum_qk.got = after(sum_qk.got, grad_v)
    grad_qk = sum_qk.result()
    grad_qkv = jnp.concatenate([grad_qk, grad_v], 1).reshape(-1, 3, width)
    return (prediction, grad_qkv, grad_proj)


def solution(mesh):
    in_specs = (
        P("lat", "lon", "mp"),
        P(),
        P("mp", None),
        P(None, None, "mp"),
        P("mp", None),
        P("mp", None),
        P("mp"),
        P("mp", None),
        P(("lat", "mp"), "lon", None),
    )
    out_specs = (
        P(("lat", "mp"), "lon", None),
        P(("lon", "lat"), None, "mp"),
        P("mp", ("lon", "lat")),
    )
    return jax.shard_map(local, mesh=mesh, in_specs=in_specs, out_specs=out_specs, check_vma=False)
```

time: 357 us -> 131 us (0.37)
  waiting for transfers between devices: 221 us -> 52.3 us
  blocking collectives: 39.4 us -> 0 us
  Pallas kernels: 0 us -> 24.2 us
  matrix products: 32.2 us -> 8.84 us
  local copies, waits for them, and re-layouts: 36 us -> 13.6 us
  starting transfers between devices: 5.17 us -> 25.1 us
  between operations: 14.2 us -> 1.05 us
    reduce_scatter x5 -> x0, waiting for transfers between devices: 199 us -> none  [the longest x1 93.9 us: local(): lax.psum_scatter(term.reshape(model_width // (cycle_size * band_size) * l...]
    all_gather x3 -> x0, blocking collectives: 39.4 us -> none  [the longest x1 16.3 us: local(): lax.all_gather(cotangent.reshape(-1, cotangent.shape[2]), 'mp', axis=0, t...]
    ppermute x3 -> x22, waiting for transfers between devices: 21.9 us -> 52.3 us  [the longest x18 49.4 us: swapped(): lax.ppermute(value, axis, [(source, source ^ bit) for source in range(cou...]
    pallas_call x0 -> x10, Pallas kernels: none -> 24.2 us  [the longest x1 7.55 us: backward_call(): call(functools.partial(backward_kernel, len(qkv)), (shape((rows, 2 * widt...]
    dot_general x15 -> x6, matrix products: 32.2 us -> 8.84 us  [the longest x5 5.35 us: dot(): lax.dot_general(a, b, (((ca,), (cb,)), ((), ())), preferred_element_type=...]
    ppermute x3 -> x22, starting transfers between devices: 4.96 us -> 25.1 us  [the longest x18 15.4 us: swapped(): lax.ppermute(value, axis, [(source, source ^ bit) for source in range(cou...]
    unnamed x36 -> x20, local copies, waits for them, and re-layouts: 14.2 us -> 0.16 us
    gather x5 -> x1, local copies, waits for them, and re-layouts: 5.75 us -> 0.64 us  [local(): strip_offsets = jnp.take(offsets, firsts // WIN)]
  transfers between devices with their start and end apart: 8 -> 22, of which waited for: 6 -> 13; matrix products, arithmetic and copies ran while one was open for 11% -> 16% of each run, Pallas kernels for 0% -> 16%
where the time goes in v1:
time: 131 us
  waiting for transfers between devices  52.3 us (40%)
  starting transfers between devices  25.1 us (19%)
  Pallas kernels  24.2 us (18%)
  local copies, waits for them, and re-layouts  13.6 us (10%)
  matrix products  8.84 us (7%)
  other arithmetic  5.65 us (4%)
    ppermute x18, waiting for transfers between devices, swapped(): lax.ppermute(value, axis, [(source, source ^ bit) for source in range(cou...  49.4 us
    ppermute x18, starting transfers between devices, swapped(): lax.ppermute(value, axis, [(source, source ^ bit) for source in range(cou...  15.4 us
    ppermute x4, starting transfers between devices, moved(): return lax.ppermute(value, axis, pairs)  9.73 us
    pallas_call x1, Pallas kernels, backward_call(): call(functools.partial(backward_kernel, len(qkv)), (shape((rows, 2 * widt...  7.55 us
    pallas_call x2, Pallas kernels, forward_call(): call(forward_kernel, out_shape, 'vvvv', 9)(rolled, w_qkv, scales, biases)  6.17 us
    dot_general x5, matrix products, dot(): lax.dot_general(a, b, (((ca,), (cb,)), ((), ())), preferred_element_type=...  5.35 us
    pallas_call x2, Pallas kernels, embed_call(): call(embed_kernel, jax.ShapeDtypeStruct((rows, width), F32), 'svvv', 5, [...  3.67 us
    dot_general x1, matrix products, local(): jnp.einsum('ije,he->hji', offset_onehot(WIN), bias_table, precision=lax.P...  3.49 us
  transfers between devices with their start and end apart: 22, of which 13 were waited for; matrix products, arithmetic and copies ran while one was open for 16% of the time, Pallas kernels for 16%

profile of v1, /device:TPU:0, one launch (start us, length us, event | category | flops | bytes accessed | tf_op | source)
XLA Modules:
  0.0 130.8 jit_solution(15664729788121737190)
XLA Ops:
  0.6 3.0 %collective-permute-start.1 = (bf16[160,1120]{1,0:T(8,128)(2,1)}, bf16[160,1120]{1,0:T(8,128)(2,1)}, u32[]{:S(2)}, u32[]{:S(2)}) collective-permute-start(bf16[160,1120]{1,0:T(8,128)(2,1)} %bitcast.158), channel_id=1, source_target_pairs={{0,1},{1,0},{2,3},{3,2},{4,5},{5,4},{6,7},{7,6},{8,9},{9,8},{10,11... | collective-permute-start | bytes 1075208 | tf_op jit(solution)/shard_map/ppermute | solution.py:34
  4.7 3.7 %collective-permute-start = (bf16[2,64,1120]{2,1,0:T(8,128)(2,1)S(1)}, bf16[2,64,1120]{2,1,0:T(8,128)(2,1)}, u32[]{:S(2)}, u32[]{:S(2)}) collective-permute-start(bf16[2,64,1120]{2,1,0:T(8,128)(2,1)S(1)} %bitcast.147), channel_id=1, source_target_pairs={{0,24},{8,0},{16,8},{24,16},{1,25},{9,1},{17,9},{25,17},{2,26},{10... | collective-permute-start | bytes 860168 | tf_op jit(solution)/shard_map/ppermute | solution.py:29
  10.0 3.5 %fusion.2 = f32[6,64,64]{1,0,2:T(8,128)} fusion(s32[64,64]{1,0:T(8,128)S(1)} %add_add_fusion, f32[6,225]{1,0:T(8,128)S(1)} %copy-done), kind=kOutput, calls=%fused_computation.12 | convolution fusion | flops 67276800 | bytes 120088 | tf_op jit(solution)/shard_map/ije,he->hji/dot_general | solution.py:407
  13.5 1.7 %copy.40 = f32[6,64,64]{2,1,0:T(8,128)} copy(f32[6,64,64]{1,0,2:T(8,128)} %fusion.2) | data formatting | bytes 196608 | tf_op jit(solution)/shard_map/ije,he->hji/transpose | solution.py:407
  15.3 1.8 %copy.41 = f32[3,64,2,64]{3,2,1,0:T(2,128)} copy(f32[3,64,2,64]{3,1,2,0:T(8,128)} %bitcast.174) | data formatting | bytes 196608 | tf_op jit(solution)/shard_map/transpose | solution.py:410
  18.5 2.0 %shard_map.112 = bf16[320,768]{1,0:T(8,128)(2,1)S(1)} custom-call(s32[1]{0:T(128)} %bitcast.1.place, bf16[160,1120]{1,0:T(8,128)(2,1)S(1)} %bitcast.159, bf16[160,1120]{1,0:T(8,128)(2,1)} %collective-permute-done.1.other, bf16[1120,768]{1,0:T(8,128)(2,1)S(1)} %bitcast.151), custom_call_target="tpu_custom_call" | custom-call | flops 3000000000 | bytes 1 | tf_op jit(solution)/shard_map/pallas_call | solution.py:253
  20.6 1.9 %shard_map.113 = f32[128,1536]{1,0:T(8,128)S(1)} custom-call(s32[2]{0:T(128)S(1)} %bitcast.142, bf16[2,64,1120]{2,1,0:T(8,128)(2,1)S(1)} %bitcast.148, bf16[2,64,1120]{2,1,0:T(8,128)(2,1)} %collective-permute-done.other, bf16[1120,1536]{1,0:T(8,128)(2,1)S(1)} %copy-done.2), custom_call_target="tpu_custom_call" | custom-call | flops 5000000000 | bytes 1 | tf_op jit(solution)/shard_map/pallas_call | solution.py:98
  23.8 1.8 %shard_map.115 = f32[192,1536]{1,0:T(8,128)S(1)} custom-call(s32[3]{0:T(128)S(1)} %slice.23.shifts, bf16[3,64,1120]{2,1,0:T(8,128)(2,1)S(1)} %bitcast.144, bf16[3,64,1120]{2,1,0:T(8,128)(2,1)S(1)} %collective-permute-done.2.other, bf16[1120,1536]{1,0:T(8,128)(2,1)S(1)} %copy-done.2), custom_call_target="tpu_custom_call" | custom-call | flops 5000000000 | bytes 1 | tf_op jit(solution)/shard_map/pallas_call | solution.py:98
  26.6 3.9 %collective-permute-start.3 = (bf16[5,64,768]{2,1,0:T(8,128)(2,1)S(1)}, bf16[5,64,768]{2,1,0:T(8,128)(2,1)S(1)}, u32[]{:S(2)}, u32[]{:S(2)}) collective-permute-start(bf16[5,64,768]{2,1,0:T(8,128)(2,1)S(1)} %bitcast.156), channel_id=1, source_target_pairs={{0,24},{8,0},{16,8},{24,16},{1,25},{9,1},{17,9},{25,17},{2,26},{10... | collective-permute-start | bytes 1474568 | tf_op jit(solution)/shard_map/ppermute | solution.py:29
  30.5 4.2 %collective-permute-done.6 = f16[128,1536]{1,0:T(8,128)(2,1)S(1)} collective-permute-done((f16[128,1536]{1,0:T(8,128)(2,1)S(1)}, f16[128,1536]{1,0:T(8,128)(2,1)S(1)}, u32[]{:S(2)}, u32[]{:S(2)}) %collective-permute-start.6) | collective-permute-done | bytes 393248 | tf_op jit(solution)/shard_map/ppermute | solution.py:34
  34.8 2.5 %shard_map.116 = (bf16[128,1152]{1,0:T(8,128)(2,1)S(1)}, f32[2,3,64,128]{3,2,1,0:T(8,128)S(1)}, bf16[128,384]{1,0:T(8,128)(2,1)S(1)}) custom-call(bf16[128,1536]{1,0:T(8,128)(2,1)S(1)} %multiply_convert_fusion.1.rolled.refs_0_, bf16[3,1536,384]{2,1,0:T(8,128)(2,1)S(1)} %bitcast.149, f32[3,1,128]{2,1,0:T(1,128)S(1)} %broadcast_in_dim.7.scales, ...), custom_call_target="tpu_custom_call" | custom-call | flops 8999999488 | bytes 1 | tf_op jit(solution)/shard_map/pallas_call | solution.py:180
  37.3 2.2 %collective-permute-done.3.other = bf16[5,64,768]{2,1,0:T(8,128)(2,1)S(1)} collective-permute-done((bf16[5,64,768]{2,1,0:T(8,128)(2,1)S(1)}, bf16[5,64,768]{2,1,0:T(8,128)(2,1)S(1)}, u32[]{:S(2)}, u32[]{:S(2)}) %collective-permute-start.3) | collective-permute-done | bytes 491552 | tf_op jit(solution)/shard_map/ppermute | solution.py:29
  40.5 4.8 %collective-permute-done.4 = f16[192,1536]{1,0:T(8,128)(2,1)S(1)} collective-permute-done((f16[192,1536]{1,0:T(8,128)(2,1)S(1)}, f16[192,1536]{1,0:T(8,128)(2,1)S(1)}, u32[]{:S(2)}, u32[]{:S(2)}) %collective-permute-start.4) | collective-permute-done | bytes 589856 | tf_op jit(solution)/shard_map/ppermute | solution.py:34
  46.5 3.7 %shard_map.117 = (bf16[192,1152]{1,0:T(8,128)(2,1)S(1)}, f32[3,3,64,128]{3,2,1,0:T(8,128)S(1)}, bf16[192,384]{1,0:T(8,128)(2,1)S(1)}) custom-call(bf16[192,1536]{1,0:T(8,128)(2,1)S(1)} %multiply_convert_fusion.rolled.refs_1_, bf16[3,1536,384]{2,1,0:T(8,128)(2,1)S(1)} %bitcast.150, f32[3,1,128]{2,1,0:T(1,128)S(1)} %broadcast_in_dim.7.scales, ...), custom_call_target="tpu_custom_call" | custom-call | flops 8999999488 | bytes 1 | tf_op jit(solution)/shard_map/pallas_call | solution.py:180
  50.2 2.6 %copy.42 = bf16[320,1536]{0,1:T(8,128)(2,1)} copy(bf16[320,1536]{1,0:T(8,128)(2,1)} %pad_maximum_fusion) | data formatting | bytes 1966080 | tf_op jit(solution)/shard_map/concatenate | solution.py:433
  53.3 2.3 %constant_dynamic-slice_fusion.3 = (bf16[320,8,1,96]{0,3,2,1:T(8,128)(2,1)S(1)}, bf16[320,8,1,96]{0,3,2,1:T(8,128)(2,1)}) fusion(bf16[320,8,2,96]{0,3,2,1:T(8,128)(2,1)} %bitcast.166, s32[]{:T(128)S(6)} %select_n.196, s32[]{:T(128)S(6)} %select_n.195), kind=kLoop, calls=%fused_computation.75 | loop fusion | bytes 1966088 | tf_op jit(solution)/shard_map/jit(dynamic_index_in_dim)/dynamic_slice | solution.py:375
  56.3 7.7 %collective-permute-done.5.other_up = bf16[320,768]{1,0:T(8,128)(2,1)S(1)} collective-permute-done((bf16[320,768]{1,0:T(8,128)(2,1)S(1)}, bf16[320,768]{1,0:T(8,128)(2,1)S(1)}, u32[]{:S(2)}, u32[]{:S(2)}) %collective-permute-start.5) | collective-permute-done | bytes 491552 | tf_op jit(solution)/shard_map/ppermute | solution.py:34
  65.7 7.6 %shard_map.119 = (bf16[320,768]{1,0:T(8,128)(2,1)S(1)}, bf16[320,384]{1,0:T(8,128)(2,1)S(1)}) custom-call(s32[1]{0:T(128)} %bitcast.1.place, bf16[320,768]{1,0:T(8,128)(2,1)S(1)} %bitcast.155, bf16[320,768]{1,0:T(8,128)(2,1)S(1)} %collective-permute-done.5.other_up, bf16[384,1536]{1,0:T(8,128)(2,1)S(1)} %copy-done.5, ...), custom_call_target="tpu_custom_call" | custom-call | flops 8999999488 | bytes 1 | tf_op jit(solution)/shard_map/pallas_call | solution.py:232
  73.4 1.5 %collective-permute-start.10 = (bf16[2,2,96,384]{3,2,1,0:T(8,128)(2,1)S(1)}, bf16[2,2,96,384]{3,2,1,0:T(8,128)(2,1)S(1)}, u32[]{:S(2)}, u32[]{:S(2)}) collective-permute-start(bf16[2,2,96,384]{3,2,1,0:T(8,128)(2,1)S(1)} %fusion.12), channel_id=1, source_target_pairs={{0,4},{2,6},{4,0},{6,2},{1,5},{3,7},{5,1},{7,3},{8,12},{10,14},{12... | collective-permute-start | bytes 884744 | tf_op jit(solution)/shard_map/ppermute | solution.py:34
  74.9 3.9 %collective-permute-done.8.theirs = bf16[320,768]{1,0:T(8,128)(2,1)S(1)} collective-permute-done((bf16[320,768]{1,0:T(8,128)(2,1)S(1)}, bf16[320,768]{1,0:T(8,128)(2,1)S(1)}, u32[]{:S(2)}, u32[]{:S(2)}) %collective-permute-start.8) | collective-permute-done | bytes 491552 | tf_op jit(solution)/shard_map/ppermute | solution.py:34
  78.8 1.6 %shard_map.120 = (bf16[160,1120]{1,0:T(8,128)(2,1)S(1)}, bf16[160,1120]{1,0:T(8,128)(2,1)S(1)}) custom-call(s32[1]{0:T(128)} %bitcast.1.place, bf16[320,768]{1,0:T(8,128)(2,1)S(1)} %get-tuple-element.64.mine, bf16[320,768]{1,0:T(8,128)(2,1)S(1)} %collective-permute-done.8.theirs, bf16[1120,768]{1,0:T(8,128)(2,1)S(1)} %bitcast.152, ...), custom_call_target="tpu_custom_call" | custom-call | flops 4000000000 | bytes 1 | tf_op jit(solution)/shard_map/pallas_call | solution.py:304
  82.6 1.8 %convolution_convert_fusion.2 = bf16[768,768]{1,0:T(8,128)(2,1)} fusion(bf16[320,768]{0,1:T(8,128)(2,1)S(1)} %bitcast.163, bf16[320,768]{1,0:T(8,128)(2,1)S(1)} %get-tuple-element.77), kind=kOutput, calls=%fused_computation.6 | convolution fusion | flops 378077184 | bytes 2162688 | tf_op jit(solution)/shard_map/dot_general | solution.py:62
  85.6 1.6 %collective-permute-start.9 = (bf16[160,1120]{1,0:T(8,128)(2,1)S(1)}, bf16[160,1120]{1,0:T(8,128)(2,1)S(1)}, u32[]{:S(2)}, u32[]{:S(2)}) collective-permute-start(bf16[160,1120]{1,0:T(8,128)(2,1)S(1)} %get-tuple-element.68), channel_id=1, source_target_pairs={{0,1},{1,0},{2,3},{3,2},{4,5},{5,4},{6,7},{7,6},{8,9},{9,8},{10,11... | collective-permute-start | bytes 1075208 | tf_op jit(solution)/shard_map/ppermute | solution.py:34
  87.2 1.6 %collective-permute-start.11 = (bf16[2,96,384]{2,1,0:T(8,128)(2,1)S(1)}, bf16[2,96,384]{2,1,0:T(8,128)(2,1)S(1)}, u32[]{:S(2)}, u32[]{:S(2)}) collective-permute-start(bf16[2,96,384]{2,1,0:T(8,128)(2,1)S(1)} %fusion.21), channel_id=1, source_target_pairs={{0,8},{8,0},{16,24},{24,16},{1,9},{9,1},{17,25},{25,17},{2,10},{10... | collective-permute-start | bytes 442376 | tf_op jit(solution)/shard_map/ppermute | solution.py:34
  93.8 2.4 %collective-permute-done.9 = bf16[160,1120]{1,0:T(8,128)(2,1)S(1)} collective-permute-done((bf16[160,1120]{1,0:T(8,128)(2,1)S(1)}, bf16[160,1120]{1,0:T(8,128)(2,1)S(1)}, u32[]{:S(2)}, u32[]{:S(2)}) %collective-permute-start.9) | collective-permute-done | bytes 358432 | tf_op jit(solution)/shard_map/ppermute | solution.py:34
  96.3 1.6 %collective-permute-start.14 = (bf16[5,32,1120]{2,1,0:T(8,128)(2,1)S(1)}, bf16[5,32,1120]{2,1,0:T(8,128)(2,1)S(1)}, u32[]{:S(2)}, u32[]{:S(2)}) collective-permute-start(bf16[5,32,1120]{2,1,0:T(8,128)(2,1)S(1)} %bitcast.145), channel_id=1, source_target_pairs={{0,8},{8,16},{16,24},{24,0},{1,9},{9,17},{17,25},{25,1},{2,10},{10... | collective-permute-start | bytes 1075208 | tf_op jit(solution)/shard_map/ppermute | solution.py:29
  97.9 1.6 %collective-permute-done.16 = bf16[2,2,96,384]{3,2,1,0:T(8,128)(2,1)S(1)} collective-permute-done((bf16[2,2,96,384]{3,2,1,0:T(8,128)(2,1)S(1)}, bf16[2,2,96,384]{3,2,1,0:T(8,128)(2,1)S(1)}, u32[]{:S(2)}, u32[]{:S(2)}) %collective-permute-start.16) | collective-permute-done | bytes 294944 | tf_op jit(solution)/shard_map/ppermute | solution.py:34
  101.9 9.0 %collective-permute-done.17 = bf16[2,96,384]{2,1,0:T(8,128)(2,1)S(1)} collective-permute-done((bf16[2,96,384]{2,1,0:T(8,128)(2,1)S(1)}, bf16[2,96,384]{2,1,0:T(8,128)(2,1)S(1)}, u32[]{:S(2)}, u32[]{:S(2)}) %collective-permute-start.17) | collective-permute-done | bytes 147488 | tf_op jit(solution)/shard_map/ppermute | solution.py:34
  111.8 5.1 %collective-permute-done.20 = bf16[96,384]{1,0:T(8,128)(2,1)S(1)} collective-permute-done((bf16[96,384]{1,0:T(8,128)(2,1)S(1)}, bf16[96,384]{1,0:T(8,128)(2,1)S(1)}, u32[]{:S(2)}, u32[]{:S(2)}) %collective-permute-start.20) | collective-permute-done | bytes 73760 | tf_op jit(solution)/shard_map/ppermute | solution.py:34
  117.0 4.7 %collective-permute-done.19 = bf16[2,96,768]{2,1,0:T(8,128)(2,1)S(1)} collective-permute-done((bf16[2,96,768]{2,1,0:T(8,128)(2,1)S(1)}, bf16[2,96,768]{2,1,0:T(8,128)(2,1)S(1)}, u32[]{:S(2)}, u32[]{:S(2)}) %collective-permute-start.19) | collective-permute-done | bytes 294944 | tf_op jit(solution)/shard_map/ppermute | solution.py:34
  122.8 1.6 %shard_map.121 = bf16[5,32,1120]{2,1,0:T(8,128)(2,1)} custom-call(s32[5]{0:T(128)S(1)} %and_select_fusion.3.shifts, bf16[5,32,1120]{2,1,0:T(8,128)(2,1)S(1)} %bitcast.146, bf16[5,32,1120]{2,1,0:T(8,128)(2,1)S(1)} %collective-permute-done.14.other), custom_call_target="tpu_custom_call" | custom-call | flops 2000000000 | bytes 1 | tf_op jit(solution)/shard_map/pallas_call | solution.py:84
  124.5 5.4 %collective-permute-done.21 = bf16[96,768]{1,0:T(8,128)(2,1)S(1)} collective-permute-done((bf16[96,768]{1,0:T(8,128)(2,1)S(1)}, bf16[96,768]{1,0:T(8,128)(2,1)S(1)}, u32[]{:S(2)}, u32[]{:S(2)}) %collective-permute-start.21) | collective-permute-done | bytes 147488 | tf_op jit(solution)/shard_map/ppermute | solution.py:34
  (94 shorter events, 25.6 us)
Async XLA Ops:
  0.6 9.3 %copy-start = (f32[6,225]{1,0:T(8,128)S(1)}, f32[6,225]{1,0:T(8,128)}, u32[]{:S(2)}) copy-start(f32[6,225]{1,0:T(8,128)} %param.16) | copy-start | bytes 16204
  0.6 17.9 %collective-permute-start.1 = (bf16[160,1120]{1,0:T(8,128)(2,1)}, bf16[160,1120]{1,0:T(8,128)(2,1)}, u32[]{:S(2)}, u32[]{:S(2)}) collective-permute-start(bf16[160,1120]{1,0:T(8,128)(2,1)} %bitcast.158), channel_id=1, source_target_pairs={{0,1},{1,0},{2,3},{3,2},{4,5},{5,4},{6,7},{7,6},{8,9},{9,8},{10,11... | collective-permute-start | bytes 1075208 | tf_op jit(solution)/shard_map/ppermute | solution.py:34
  4.7 8.9 %copy-start.8 = (f32[6]{0:T(128)S(1)}, f32[6]{0:T(128)}, u32[]{:S(2)}) copy-start(f32[6]{0:T(128)} %param.15) | copy-start | bytes 76
  4.7 15.8 %collective-permute-start = (bf16[2,64,1120]{2,1,0:T(8,128)(2,1)S(1)}, bf16[2,64,1120]{2,1,0:T(8,128)(2,1)}, u32[]{:S(2)}, u32[]{:S(2)}) collective-permute-start(bf16[2,64,1120]{2,1,0:T(8,128)(2,1)S(1)} %bitcast.147), channel_id=1, source_target_pairs={{0,24},{8,0},{16,8},{24,16},{1,25},{9,1},{17,9},{25,17},{2,26},{10... | collective-permute-start | bytes 860168 | tf_op jit(solution)/shard_map/ppermute | solution.py:29
  9.4 14.4 %collective-permute-start.2 = (bf16[3,64,1120]{2,1,0:T(8,128)(2,1)S(1)}, bf16[3,64,1120]{2,1,0:T(8,128)(2,1)S(1)}, u32[]{:S(2)}, u32[]{:S(2)}) collective-permute-start(bf16[3,64,1120]{2,1,0:T(8,128)(2,1)S(1)} %bitcast.143), channel_id=1, source_target_pairs={{0,24},{8,0},{16,8},{24,16},{1,25},{9,1},{17,9},{25,17},{2,26},{10... | collective-permute-start | bytes 1290248 | tf_op jit(solution)/shard_map/ppermute | solution.py:29
  10.0 8.1 %copy-start.9 = (s32[20]{0:T(128)S(1)}, s32[20]{0:T(128)}, u32[]{:S(2)}) copy-start(s32[20]{0:T(128)} %param.10) | copy-start | bytes 244
  10.0 8.5 %copy-start.3 = (bf16[768,1120]{0,1:T(8,128)(2,1)S(1)}, bf16[768,1120]{0,1:T(8,128)(2,1)}, u32[]{:S(2)}) copy-start(bf16[768,1120]{0,1:T(8,128)(2,1)} %param.14) | copy-start | bytes 5160964
  10.0 8.5 %copy-start.6 = (bf16[20,8,1120]{2,1,0:T(8,128)(2,1)S(1)}, bf16[20,8,1120]{2,1,0:T(8,128)(2,1)}, u32[]{:S(2)}) copy-start(bf16[20,8,1120]{2,1,0:T(8,128)(2,1)} %param.17) | copy-start | bytes 1075204
  18.5 2.1 %copy-start.2 = (bf16[1120,1536]{1,0:T(8,128)(2,1)S(1)}, bf16[1120,1536]{1,0:T(8,128)(2,1)}, u32[]{:S(2)}) copy-start(bf16[1120,1536]{1,0:T(8,128)(2,1)} %weight.3) | copy-start | bytes 10321924
  22.6 12.1 %collective-permute-start.6 = (f16[128,1536]{1,0:T(8,128)(2,1)S(1)}, f16[128,1536]{1,0:T(8,128)(2,1)S(1)}, u32[]{:S(2)}, u32[]{:S(2)}) collective-permute-start(f16[128,1536]{1,0:T(8,128)(2,1)S(1)} %convert_element_type.346), channel_id=1, source_target_pairs={{0,1},{1,0},{2,3},{3,2},{4,5},{5,4},{6,7},{7,6},{8,9},{9,8},{10,11... | collective-permute-start | bytes 1179656 | tf_op jit(solution)/shard_map/ppermute | solution.py:34
  23.8 11.0 %copy-start.1 = (bf16[1536,3,384]{2,0,1:T(8,128)(2,1)S(1)}, bf16[1536,3,384]{2,0,1:T(8,128)(2,1)}, u32[]{:S(2)}) copy-start(bf16[1536,3,384]{2,0,1:T(8,128)(2,1)} %param.12) | copy-start | bytes 10616836
  25.7 19.6 %collective-permute-start.4 = (f16[192,1536]{1,0:T(8,128)(2,1)S(1)}, f16[192,1536]{1,0:T(8,128)(2,1)S(1)}, u32[]{:S(2)}, u32[]{:S(2)}) collective-permute-start(f16[192,1536]{1,0:T(8,128)(2,1)S(1)} %convert_element_type.347), channel_id=1, source_target_pairs={{0,1},{1,0},{2,3},{3,2},{4,5},{5,4},{6,7},{7,6},{8,9},{9,8},{10,11... | collective-permute-start | bytes 1769480 | tf_op jit(solution)/shard_map/ppermute | solution.py:34
  26.6 12.9 %collective-permute-start.3 = (bf16[5,64,768]{2,1,0:T(8,128)(2,1)S(1)}, bf16[5,64,768]{2,1,0:T(8,128)(2,1)S(1)}, u32[]{:S(2)}, u32[]{:S(2)}) collective-permute-start(bf16[5,64,768]{2,1,0:T(8,128)(2,1)S(1)} %bitcast.156), channel_id=1, source_target_pairs={{0,24},{8,0},{16,8},{24,16},{1,25},{9,1},{17,9},{25,17},{2,26},{10... | collective-permute-start | bytes 1474568 | tf_op jit(solution)/shard_map/ppermute | solution.py:29
  52.8 11.2 %collective-permute-start.5 = (bf16[320,768]{1,0:T(8,128)(2,1)S(1)}, bf16[320,768]{1,0:T(8,128)(2,1)S(1)}, u32[]{:S(2)}, u32[]{:S(2)}) collective-permute-start(bf16[320,768]{1,0:T(8,128)(2,1)S(1)} %bitcast.153), channel_id=1, source_target_pairs={{0,1},{1,0},{2,3},{3,2},{4,5},{5,4},{6,7},{7,6},{8,9},{9,8},{10,11... | collective-permute-start | bytes 1474568 | tf_op jit(solution)/shard_map/ppermute | solution.py:34
  53.3 2.3 %copy-start.5 = (bf16[384,1536]{1,0:T(8,128)(2,1)S(1)}, bf16[384,1536]{1,0:T(8,128)(2,1)}, u32[]{:S(2)}) copy-start(bf16[384,1536]{1,0:T(8,128)(2,1)} %w_proj.3) | copy-start | bytes 3538948
  65.1 8.2 %collective-permute-start.7 = (bf16[8,96,384]{2,1,0:T(8,128)(2,1)S(1)}, bf16[8,96,384]{2,1,0:T(8,128)(2,1)S(1)}, u32[]{:S(2)}, u32[]{:S(2)}) collective-permute-start(bf16[8,96,384]{2,1,0:T(8,128)(2,1)S(1)} %get-tuple-element.96), channel_id=1, source_target_pairs={{0,2},{2,0},{4,6},{6,4},{1,3},{3,1},{5,7},{7,5},{8,10},{10,8},{12,... | collective-permute-start | bytes 1769480 | tf_op jit(solution)/shard_map/ppermute | solution.py:34
  65.2 13.6 %collective-permute-start.8 = (bf16[320,768]{1,0:T(8,128)(2,1)S(1)}, bf16[320,768]{1,0:T(8,128)(2,1)S(1)}, u32[]{:S(2)}, u32[]{:S(2)}) collective-permute-start(bf16[320,768]{1,0:T(8,128)(2,1)S(1)} %get-tuple-element.66), channel_id=1, source_target_pairs={{0,1},{1,0},{2,3},{3,2},{4,5},{5,4},{6,7},{7,6},{8,9},{9,8},{10,11... | collective-permute-start | bytes 1474568 | tf_op jit(solution)/shard_map/ppermute | solution.py:34
  65.7 13.1 %copy-start.4 = (bf16[768,1120]{0,1:T(8,128)(2,1)S(1)}, bf16[768,1120]{0,1:T(8,128)(2,1)}, u32[]{:S(2)}) copy-start(bf16[768,1120]{0,1:T(8,128)(2,1)} %param.14) | copy-start | bytes 5160964
  73.4 9.1 %collective-permute-start.10 = (bf16[2,2,96,384]{3,2,1,0:T(8,128)(2,1)S(1)}, bf16[2,2,96,384]{3,2,1,0:T(8,128)(2,1)S(1)}, u32[]{:S(2)}, u32[]{:S(2)}) collective-permute-start(bf16[2,2,96,384]{3,2,1,0:T(8,128)(2,1)S(1)} %fusion.12), channel_id=1, source_target_pairs={{0,4},{2,6},{4,0},{6,2},{1,5},{3,7},{5,1},{7,3},{8,12},{10,14},{12... | collective-permute-start | bytes 884744 | tf_op jit(solution)/shard_map/ppermute | solution.py:34
  82.6 6.2 %copy-start.7 = (bf16[320,8,1,96]{0,3,2,1:T(8,128)(2,1)S(1)}, bf16[320,8,1,96]{0,3,2,1:T(8,128)(2,1)}, u32[]{:S(2)}) copy-start(bf16[320,8,1,96]{0,3,2,1:T(8,128)(2,1)} %get-tuple-element.98) | copy-start | bytes 1474564
  84.4 7.4 %collective-permute-start.13 = (bf16[8,96,768]{2,1,0:T(8,128)(2,1)}, bf16[8,96,768]{2,1,0:T(8,128)(2,1)}, u32[]{:S(2)}, u32[]{:S(2)}) collective-permute-start(bf16[8,96,768]{2,1,0:T(8,128)(2,1)} %bitcast.27), channel_id=1, source_target_pairs={{0,2},{2,0},{4,6},{6,4},{1,3},{3,1},{5,7},{7,5},{8,10},{10,8},{12,... | collective-permute-start | bytes 3538952 | tf_op jit(solution)/shard_map/ppermute | solution.py:34
  84.4 4.9 %collective-permute-start.12 = (bf16[8,96,384]{2,1,0:T(8,128)(2,1)}, bf16[8,96,384]{2,1,0:T(8,128)(2,1)S(1)}, u32[]{:S(2)}, u32[]{:S(2)}) collective-permute-start(bf16[8,96,384]{2,1,0:T(8,128)(2,1)} %bitcast.179), channel_id=1, source_target_pairs={{0,2},{2,0},{4,6},{6,4},{1,3},{3,1},{5,7},{7,5},{8,10},{10,8},{12,... | collective-permute-start | bytes 1769480 | tf_op jit(solution)/shard_map/ppermute | solution.py:34
  85.6 10.6 %collective-permute-start.9 = (bf16[160,1120]{1,0:T(8,128)(2,1)S(1)}, bf16[160,1120]{1,0:T(8,128)(2,1)S(1)}, u32[]{:S(2)}, u32[]{:S(2)}) collective-permute-start(bf16[160,1120]{1,0:T(8,128)(2,1)S(1)} %get-tuple-element.68), channel_id=1, source_target_pairs={{0,1},{1,0},{2,3},{3,2},{4,5},{5,4},{6,7},{7,6},{8,9},{9,8},{10,11... | collective-permute-start | bytes 1075208 | tf_op jit(solution)/shard_map/ppermute | solution.py:34
  87.2 6.5 %collective-permute-start.11 = (bf16[2,96,384]{2,1,0:T(8,128)(2,1)S(1)}, bf16[2,96,384]{2,1,0:T(8,128)(2,1)S(1)}, u32[]{:S(2)}, u32[]{:S(2)}) collective-permute-start(bf16[2,96,384]{2,1,0:T(8,128)(2,1)S(1)} %fusion.21), channel_id=1, source_target_pairs={{0,8},{8,0},{16,24},{24,16},{1,9},{9,1},{17,25},{25,17},{2,10},{10... | collective-permute-start | bytes 442376 | tf_op jit(solution)/shard_map/ppermute | solution.py:34
  89.4 10.0 %collective-permute-start.16 = (bf16[2,2,96,384]{3,2,1,0:T(8,128)(2,1)S(1)}, bf16[2,2,96,384]{3,2,1,0:T(8,128)(2,1)S(1)}, u32[]{:S(2)}, u32[]{:S(2)}) collective-permute-start(bf16[2,2,96,384]{3,2,1,0:T(8,128)(2,1)S(1)} %fusion.13), channel_id=1, source_target_pairs={{0,4},{2,6},{4,0},{6,2},{1,5},{3,7},{5,1},{7,3},{8,12},{10,14},{12... | collective-permute-start | bytes 884744 | tf_op jit(solution)/shard_map/ppermute | solution.py:34
  93.0 18.5 %collective-permute-start.15 = (bf16[2,2,96,768]{3,2,0,1:T(8,128)(2,1)S(1)}, bf16[2,2,96,768]{3,2,0,1:T(8,128)(2,1)S(1)}, u32[]{:S(2)}, u32[]{:S(2)}) collective-permute-start(bf16[2,2,96,768]{3,2,0,1:T(8,128)(2,1)S(1)} %fusion.9), channel_id=1, source_target_pairs={{0,4},{2,6},{4,0},{6,2},{1,5},{3,7},{5,1},{7,3},{8,12},{10,14},{12... | collective-permute-start | bytes 1769480 | tf_op jit(solution)/shard_map/ppermute | solution.py:34
  93.7 7.5 %collective-permute-start.18 = (bf16[96,384]{1,0:T(8,128)(2,1)S(1)}, bf16[96,384]{1,0:T(8,128)(2,1)S(1)}, u32[]{:S(2)}, u32[]{:S(2)}) collective-permute-start(bf16[96,384]{1,0:T(8,128)(2,1)S(1)} %fusion.30), channel_id=1, source_target_pairs={{0,16},{8,24},{16,0},{24,8},{1,17},{9,25},{17,1},{25,9},{2,18},{10... | collective-permute-start | bytes 221192 | tf_op jit(solution)/shard_map/ppermute | solution.py:34
  96.3 20.7 %collective-permute-start.14 = (bf16[5,32,1120]{2,1,0:T(8,128)(2,1)S(1)}, bf16[5,32,1120]{2,1,0:T(8,128)(2,1)S(1)}, u32[]{:S(2)}, u32[]{:S(2)}) collective-permute-start(bf16[5,32,1120]{2,1,0:T(8,128)(2,1)S(1)} %bitcast.145), channel_id=1, source_target_pairs={{0,8},{8,16},{16,24},{24,0},{1,9},{9,17},{17,25},{25,1},{2,10},{10... | collective-permute-start | bytes 1075208 | tf_op jit(solution)/shard_map/ppermute | solution.py:29
  99.5 11.4 %collective-permute-start.17 = (bf16[2,96,384]{2,1,0:T(8,128)(2,1)S(1)}, bf16[2,96,384]{2,1,0:T(8,128)(2,1)S(1)}, u32[]{:S(2)}, u32[]{:S(2)}) collective-permute-start(bf16[2,96,384]{2,1,0:T(8,128)(2,1)S(1)} %fusion.22), channel_id=1, source_target_pairs={{0,8},{8,0},{16,24},{24,16},{1,9},{9,1},{17,25},{25,17},{2,10},{10... | collective-permute-start | bytes 442376 | tf_op jit(solution)/shard_map/ppermute | solution.py:34
  110.9 6.1 %collective-permute-start.20 = (bf16[96,384]{1,0:T(8,128)(2,1)S(1)}, bf16[96,384]{1,0:T(8,128)(2,1)S(1)}, u32[]{:S(2)}, u32[]{:S(2)}) collective-permute-start(bf16[96,384]{1,0:T(8,128)(2,1)S(1)} %fusion.31), channel_id=1, source_target_pairs={{0,16},{8,24},{16,0},{24,8},{1,17},{9,25},{17,1},{25,9},{2,18},{10... | collective-permute-start | bytes 221192 | tf_op jit(solution)/shard_map/ppermute | solution.py:34
  111.7 10.0 %collective-permute-start.19 = (bf16[2,96,768]{2,1,0:T(8,128)(2,1)S(1)}, bf16[2,96,768]{2,1,0:T(8,128)(2,1)S(1)}, u32[]{:S(2)}, u32[]{:S(2)}) collective-permute-start(bf16[2,96,768]{2,1,0:T(8,128)(2,1)S(1)} %get-tuple-element.94), channel_id=1, source_target_pairs={{0,8},{8,0},{16,24},{24,16},{1,9},{9,1},{17,25},{25,17},{2,10},{10... | collective-permute-start | bytes 884744 | tf_op jit(solution)/shard_map/ppermute | solution.py:34
  121.7 8.2 %collective-permute-start.21 = (bf16[96,768]{1,0:T(8,128)(2,1)S(1)}, bf16[96,768]{1,0:T(8,128)(2,1)S(1)}, u32[]{:S(2)}, u32[]{:S(2)}) collective-permute-start(bf16[96,768]{1,0:T(8,128)(2,1)S(1)} %fusion.24), channel_id=1, source_target_pairs={{0,16},{8,24},{16,0},{24,8},{1,17},{9,25},{17,1},{25,9},{2,18},{10... | collective-permute-start | bytes 442376 | tf_op jit(solution)/shard_map/ppermute | solution.py:34

commit v2 on v1

--- a/solution.py
+++ b/solution.py
@@ -127,6 +127,10 @@
     return jnp.where((row < HD) == (col < HD), 1.0, 0.0).astype(BF)
 
 
+def short_sums(value, ones):
+    return dot(value.astype(BF), ones)
+
+
 def head_sums(value, ones):
     high, low = two_parts(value)
     return dot(high, ones) + dot(low, ones)
@@ -141,6 +145,12 @@
     high, low = two_parts(square(query_halves))
     ones = jnp.ones((WIN, PAIR), BF)
     total = dot(ones, high, 1, 1) + dot(ones, low, 1, 1)
+    return lax.rsqrt(total[:1] + eps)
+
+
+def short_row_norms(query_halves):
+    ones = jnp.ones((WIN, PAIR), BF)
+    total = dot(ones, square(query_halves).astype(BF), 1, 1)
     return lax.rsqrt(total[:1] + eps)
 
 
@@ -177,13 +187,13 @@
         shape((rows // SPAN, pairs, SPAN, PAIR), F32),
         shape((rows, width)),
     )
-    got = call(forward_kernel, out_shape, "vvvv", 9)(rolled, w_qkv, scales, biases)
+    got = call(forward_kernel, out_shape, "vvvv", 0.05)(rolled, w_qkv, scales, biases)
     return (rolled,) + tuple(got)
 
 
 def unit_grad(value, norm, grad, ones):
     wide = value.astype(F32)
-    along = head_sums(wide * grad, ones)
+    along = short_sums(wide * grad, ones)
     return norm * (grad - wide * (norm * norm) * along)
 
 
@@ -211,9 +221,9 @@
             spots = [pl.ds(part * width + pair * PAIR, PAIR) for part in range(3)]
             query, key, value = [qkv[pl.ds(window * SPAN, SPAN), spot] for spot in spots]
             query_halves = halves(query)
-            key_norm = lax.rsqrt(head_sums(square(key), ones) + eps)
-            query_norm = lax.rsqrt(head_sums(square(query), ones) + eps)
-            query_lanes = row_norms(query_halves)
+            key_norm = lax.rsqrt(short_sums(square(key), ones) + eps)
+            query_norm = lax.rsqrt(short_sums(square(query), ones) + eps)
+            query_lanes = short_row_norms(query_halves)
             share = probs[window, pair]
             grad_halves = halves(d_att[rows, pl.ds(pair * PAIR, PAIR)])
             d_value[rows, spots[0]] = dot(share.astype(BF), grad_halves).astype(BF)
@@ -276,7 +286,7 @@
         functools.partial(mix_kernel, len(attended)),
         (out, out),
         "sv" + "v" * len(attended),
-        3,
+        0.05,
     )(place, w_proj, *attended)
 
 
@@ -338,11 +348,12 @@
 class Sum:
     def __init__(self, keep, send, order):
         self.dims = [("lon", bit) for _, bit in reversed(bits_of("lon"))]
-        self.dims += [("lat", bit) for _, bit in reversed(bits_of("lat"))][:-1]
+        self.dims += [("lat", bit) for _, bit in reversed(bits_of("lat"))]
+        self.dims.remove(order[0])
         self.rows = keep.shape[1:]
-        self.order = list(order)
+        self.order = list(order[1:])
         self.keep = keep
-        self.got = swapped(send, "lat", 1)
+        self.got = swapped(send, *order[0])
 
     def step(self):
         axis, bit = self.order.pop(0)
@@ -368,11 +379,13 @@
         return self.keep.reshape(self.rows).astype(F32) + self.got.reshape(self.rows).astype(F32)
 
 
-def cut_pieces(value, pieces, axis):
-    size = value.shape[axis] // pieces
-    value = value.reshape(value.shape[:axis] + (pieces // 2, 2, size) + value.shape[axis + 1 :])
-    low = my_bit("lat", 1)
-    return [lax.dynamic_index_in_dim(value, bit, axis + 1, keepdims=False) for bit in (low, 1 - low)]
+def cut_pieces(value, pieces, axis, mesh_axis, bit):
+    stride = bit * (lax.axis_size("lat") if mesh_axis == "lon" else 1)
+    size = stride * (value.shape[axis] // pieces)
+    dims = (pieces // (2 * stride), 2, size)
+    value = value.reshape(value.shape[:axis] + dims + value.shape[axis + 1 :])
+    mine = my_bit(mesh_axis, bit)
+    return [lax.dynamic_index_in_dim(value, one, axis + 1, keepdims=False) for one in (mine, 1 - mine)]
 
 
 def local(fields, shift_offsets, w_embed, w_qkv, w_proj, w_head, log_scale, bias_table, cotangent):
@@ -391,8 +404,6 @@
     strip_offsets = jnp.take(offsets, firsts // WIN)
     place = mp.reshape(1)
     pieces = lax.axis_size("lon") * lax.axis_size("lat")
-    z_bits = bits_of("lon")
-    x_bits = bits_of("lat")[1:]
 
     cuts = [0, 2, groups]
     tiles = fields.reshape(groups, SPAN, depth)
@@ -410,7 +421,9 @@
     biases = biases.reshape(pairs, 2, SPAN, SPAN).transpose(0, 2, 1, 3).reshape(pairs, SPAN, PAIR)
 
     half_up = half_up_call(place, cot, other_cot, w_head.T)
-    next_tiles[0], half_up, biases = lax.optimization_barrier((next_tiles[0], half_up, biases))
+    next_tiles[0], half_up, biases, strip_offsets = lax.optimization_barrier(
+        (next_tiles[0], half_up, biases, strip_offsets)
+    )
     terms, other_terms = [], []
     for index, (shift, tile, next_tile) in enumerate(zip(shifts, tiles, next_tiles)):
         if terms:
@@ -430,7 +443,7 @@
     mixed_here, mixed_there = mix_call(place, w_proj, attended)
     left_keep, left_send = [
         side.reshape(groups * SPAN, -1)
-        for side in cut_pieces(jnp.concatenate(rolled, 0), pieces, 1)
+        for side in cut_pieces(jnp.concatenate(rolled, 0), pieces, 1, "lat", 1)
     ]
     all_attended = jnp.concatenate(attended, 0)
     other_up, mixed_here, left_keep, left_send, all_attended = lax.optimization_barrier(
@@ -440,8 +453,14 @@
     up = jnp.where(
         mp == 0, jnp.concatenate([own_up, other_up], 1), jnp.concatenate([other_up, own_up], 1)
     )
-    keep, send = cut_pieces(dot(up, all_attended, 0, 0).astype(BF), pieces, 0)
-    sum_p = Sum(keep, send, x_bits + z_bits)
+    all_bits = bits_of("lat") + bits_of("lon")
+    z_first = bits_of("lon")[:1] + bits_of("lat") + bits_of("lon")[1:]
+    grad_p = dot(up, all_attended, 0, 0).astype(BF)
+    keep, send = [
+        side.reshape(pieces // 2, -1, width) for side in cut_pieces(grad_p, pieces, 0, *z_first[0])
+    ]
+    v_order = bits_of("lat")[:1] + bits_of("lon")[:1] + bits_of("lat")[1:] + bits_of("lon")[1:]
+    sum_p = Sum(keep, send, z_first)
 
     d_qk, d_value = backward_call(
         place, own_up, after(other_up, send), w_proj, scales, qkv, probs
@@ -450,37 +469,41 @@
     def products(left, right):
         return dot(left, right, 0, 0).astype(BF).reshape(pieces // 2, model // pieces, -1)
 
-    sum_p.got = after(sum_p.got, d_qk)
+    pred_here, pred_there = head_call(place, after(mixed_here, d_qk), mixed_got, w_head.T, rolled)
+    qk_send = products(left_send, after(d_qk, pred_there))
+    sum_p.got = after(sum_p.got, qk_send)
     sent = sum_p.step()
-    pred_here, pred_there = head_call(place, after(mixed_here, sent), mixed_got, w_head.T, rolled)
-    v_send = products(left_send, after(d_value, pred_there))
-    sum_p.got = after(sum_p.got, v_send)
-    sent = sum_p.step()
-    qk_send = products(left_send, after(d_qk, sent))
-    v_keep = products(left_keep, after(d_value, qk_send))
-    sum_v = Sum(v_keep, v_send, x_bits + z_bits)
-    sum_v.got = after(sum_v.got, qk_send)
-    sent = sum_v.step()
-    qk_keep = products(left_keep, after(d_qk, sent))
-    sum_qk = Sum(qk_keep, qk_send, x_bits + z_bits)
-    sum_qk.got = after(sum_qk.got, sent)
+    qk_send = after(qk_send, sent)
+    v_send = products(left_send, after(d_value, qk_send))
+    qk_keep = products(left_keep, after(d_qk, v_send))
+    sum_qk = Sum(qk_keep, qk_send, all_bits)
+    sum_qk.got = after(sum_qk.got, qk_keep)
     sent = sum_qk.step()
     sum_p.got = after(sum_p.got, sent)
     sent = sum_p.step()
+    v_keep = products(left_keep, after(d_value, sent))
+    sum_v = Sum(v_keep, v_send, v_order)
+    sum_v.got = after(sum_v.got, v_keep)
+    sent = sum_v.step()
     pred_got = after(swapped(pred_there, "mp", 1), sent)
     pred = (pred_here.astype(F32) + pred_got.astype(F32)).astype(BF)
     pred = pred.reshape(strips, strip * WIN, outputs)
     before = moved(pred, "lon", 1)
-    sum_v.got = after(sum_v.got, pred)
+    sum_p.got = after(sum_p.got, pred)
+    sent = sum_p.step()
+    sum_qk.got = after(sum_qk.got, sent)
+    sent = sum_qk.step()
+    sum_v.got = after(sum_v.got, sent)
     sent = sum_v.step()
-    sum_p.got = after(sum_p.got, sent)
+    before = after(before, sent)
+    prediction = roll_call(strip_offsets, pred, before, -1).reshape(rows_here, breadth, outputs)
+    sum_p.got = after(sum_p.got, prediction)
     grad_proj = sum_p.result().T
     sum_v.got = after(sum_v.got, grad_proj)
     sent = sum_v.step()
     sum_qk.got = after(sum_qk.got, sent)
     sent = sum_qk.step()
-    before = after(before, sent)
-    prediction = roll_call(strip_offsets, pred, before, -1).reshape(rows_here, breadth, outputs)
+    sum_v.got = after(sum_v.got, sent)
     grad_v = sum_v.result()
     sum_qk.got = after(sum_qk.got, grad_v)
     grad_qk = sum_qk.result()

time: 131 us -> 122 us (0.931)
  waiting for transfers between devices: 52.3 us -> 36 us
  other arithmetic: 5.65 us -> 8.02 us
  local copies, waits for them, and re-layouts: 13.6 us -> 15.9 us
  matrix products: 8.84 us -> 10.3 us
    ppermute x18, waiting for transfers between devices: 49.4 us -> 35.3 us  [swapped(): lax.ppermute(value, axis, [(source, source ^ bit) for source in range(cou...]
    unnamed x20 -> x58, local copies, waits for them, and re-layouts: 0.16 us -> 5.28 us
    ppermute x4, waiting for transfers between devices: 2.9 us -> 0.7 us  [moved(): return lax.ppermute(value, axis, pairs)]
    dynamic_slice x2, local copies, waits for them, and re-layouts: 2.46 us -> 0.29 us  [cut_pieces(): lax.dynamic_index_in_dim(value, one, axis + 1, keepdims=False)]
    convert_element_type x14 -> x13, other arithmetic: 3.12 us -> 5.07 us  [total(): return (a.astype(F32) + b.astype(F32)).astype(BF)]
    dot_general x5, matrix products: 5.35 us -> 6.79 us  [dot(): lax.dot_general(a, b, (((ca,), (cb,)), ((), ())), preferred_element_type=...]
  transfers between devices with their start and end apart: 22 -> 22, of which waited for: 13 -> 11; matrix products, arithmetic and copies ran while one was open for 16% -> 20% of each run, Pallas kernels for 16% -> 21%
where the time goes in v2:
time: 122 us
  waiting for transfers between devices  36 us (30%)
  Pallas kernels  25.5 us (21%)
  starting transfers between devices  24.7 us (20%)
  local copies, waits for them, and re-layouts  15.9 us (13%)
  matrix products  10.3 us (8%)
  other arithmetic  8.02 us (7%)
    ppermute x18, waiting for transfers between devices, swapped(): lax.ppermute(value, axis, [(source, source ^ bit) for source in range(cou...  35.3 us
    ppermute x18, starting transfers between devices, swapped(): lax.ppermute(value, axis, [(source, source ^ bit) for source in range(cou...  15.3 us
    ppermute x4, starting transfers between devices, moved(): return lax.ppermute(value, axis, pairs)  9.36 us
    pallas_call x1, Pallas kernels, backward_call(): call(functools.partial(backward_kernel, len(qkv)), (shape((rows, 2 * widt...  8.08 us
    dot_general x5, matrix products, dot(): lax.dot_general(a, b, (((ca,), (cb,)), ((), ())), preferred_element_type=...  6.79 us
    pallas_call x2, Pallas kernels, forward_call(): call(forward_kernel, out_shape, 'vvvv', 0.05)(rolled, w_qkv, scales, biases)  6.17 us
    unnamed x58, local copies, waits for them, and re-layouts  5.28 us
    convert_element_type x13, other arithmetic, total(): return (a.astype(F32) + b.astype(F32)).astype(BF)  5.07 us
  transfers between devices with their start and end apart: 22, of which 11 were waited for; matrix products, arithmetic and copies ran while one was open for 20% of the time, Pallas kernels for 21%

profile of v2, /device:TPU:0, one launch (start us, length us, event | category | flops | bytes accessed | tf_op | source)
XLA Modules:
  0.0 121.6 jit_solution(13167418302002919088)
XLA Ops:
  1.7 5.1 %collective-permute-start = (bf16[2,64,1120]{2,1,0:T(8,128)(2,1)S(1)}, bf16[2,64,1120]{2,1,0:T(8,128)(2,1)}, u32[]{:S(2)}, u32[]{:S(2)}) collective-permute-start(bf16[2,64,1120]{2,1,0:T(8,128)(2,1)S(1)} %bitcast.140), channel_id=1, source_target_pairs={{0,24},{8,0},{16,8},{24,16},{1,25},{9,1},{17,9},{25,17},{2,26},{10... | collective-permute-start | bytes 860168 | tf_op jit(solution)/shard_map/ppermute | solution.py:29
  6.8 1.5 %collective-permute-start.1 = (bf16[160,1120]{1,0:T(8,128)(2,1)}, bf16[160,1120]{1,0:T(8,128)(2,1)}, u32[]{:S(2)}, u32[]{:S(2)}) collective-permute-start(bf16[160,1120]{1,0:T(8,128)(2,1)} %bitcast.146), channel_id=1, source_target_pairs={{0,1},{1,0},{2,3},{3,2},{4,5},{5,4},{6,7},{7,6},{8,9},{9,8},{10,11... | collective-permute-start | bytes 1075208 | tf_op jit(solution)/shard_map/ppermute | solution.py:34
  10.7 3.5 %fusion.2 = f32[6,64,64]{1,0,2:T(8,128)} fusion(s32[64,64]{1,0:T(8,128)S(1)} %add_add_fusion, f32[6,225]{1,0:T(8,128)S(1)} %copy-done), kind=kOutput, calls=%fused_computation.12 | convolution fusion | flops 67276800 | bytes 120088 | tf_op jit(solution)/shard_map/ije,he->hji/dot_general | solution.py:418
  17.5 1.7 %reshape.369.biases = f32[3,64,128]{2,1,0:T(8,128)} reshape(f32[3,64,2,64]{3,2,1,0:T(2,128)} %copy.42) | data formatting | bytes 196608 | tf_op jit(solution)/shard_map/reshape | solution.py:421
  19.2 2.0 %shard_map.112 = bf16[320,768]{1,0:T(8,128)(2,1)S(1)} custom-call(s32[1]{0:T(128)} %bitcast.1.place, bf16[160,1120]{1,0:T(8,128)(2,1)S(1)} %bitcast.147, bf16[160,1120]{1,0:T(8,128)(2,1)} %collective-permute-done.1.other, bf16[1120,768]{1,0:T(8,128)(2,1)S(1)} %bitcast.142), custom_call_target="tpu_custom_call" | custom-call | flops 3000000000 | bytes 1 | tf_op jit(solution)/shard_map/pallas_call | solution.py:263
  21.3 1.9 %shard_map.113 = f32[128,1536]{1,0:T(8,128)S(1)} custom-call(s32[2]{0:T(128)S(1)} %bitcast.133, bf16[2,64,1120]{2,1,0:T(8,128)(2,1)S(1)} %bitcast.141, bf16[2,64,1120]{2,1,0:T(8,128)(2,1)} %collective-permute-done.other, bf16[1120,1536]{1,0:T(8,128)(2,1)S(1)} %copy-done.14), custom_call_target="tpu_custom_call" | custom-call | flops 5000000000 | bytes 1 | tf_op jit(solution)/shard_map/pallas_call | solution.py:98
  24.6 2.9 %collective-permute-start.3 = (bf16[5,64,768]{2,1,0:T(8,128)(2,1)S(1)}, bf16[5,64,768]{2,1,0:T(8,128)(2,1)S(1)}, u32[]{:S(2)}, u32[]{:S(2)}) collective-permute-start(bf16[5,64,768]{2,1,0:T(8,128)(2,1)S(1)} %bitcast.144), channel_id=1, source_target_pairs={{0,24},{8,0},{16,8},{24,16},{1,25},{9,1},{17,9},{25,17},{2,26},{10... | collective-permute-start | bytes 1474568 | tf_op jit(solution)/shard_map/ppermute | solution.py:29
  28.6 1.8 %shard_map.115 = f32[192,1536]{1,0:T(8,128)S(1)} custom-call(s32[3]{0:T(128)S(1)} %copy-done.25, bf16[3,64,1120]{2,1,0:T(8,128)(2,1)S(1)} %bitcast.137, bf16[3,64,1120]{2,1,0:T(8,128)(2,1)S(1)} %copy-done.18, bf16[1120,1536]{1,0:T(8,128)(2,1)S(1)} %copy-done.14), custom_call_target="tpu_custom_call" | custom-call | flops 5000000000 | bytes 1 | tf_op jit(solution)/shard_map/pallas_call | solution.py:98
  30.4 1.6 %collective-permute-start.4 = (f16[192,1536]{1,0:T(8,128)(2,1)S(1)}, f16[192,1536]{1,0:T(8,128)(2,1)S(1)}, u32[]{:S(2)}, u32[]{:S(2)}) collective-permute-start(f16[192,1536]{1,0:T(8,128)(2,1)S(1)} %convert_element_type.347), channel_id=1, source_target_pairs={{0,1},{1,0},{2,3},{3,2},{4,5},{5,4},{6,7},{7,6},{8,9},{9,8},{10,11... | collective-permute-start | bytes 1769480 | tf_op jit(solution)/shard_map/ppermute | solution.py:34
  32.0 2.8 %collective-permute-done.6 = f16[128,1536]{1,0:T(8,128)(2,1)S(1)} collective-permute-done((f16[128,1536]{1,0:T(8,128)(2,1)S(1)}, f16[128,1536]{1,0:T(8,128)(2,1)S(1)}, u32[]{:S(2)}, u32[]{:S(2)}) %collective-permute-start.6) | collective-permute-done | bytes 393248 | tf_op jit(solution)/shard_map/ppermute | solution.py:34
  35.0 2.5 %shard_map.116 = (bf16[128,1152]{1,0:T(8,128)(2,1)S(1)}, f32[2,3,64,128]{3,2,1,0:T(8,128)S(1)}, bf16[128,384]{1,0:T(8,128)(2,1)S(1)}) custom-call(bf16[128,1536]{1,0:T(8,128)(2,1)S(1)} %multiply_convert_fusion.1.rolled.refs_0_, bf16[3,1536,384]{2,1,0:T(8,128)(2,1)S(1)} %bitcast.134, f32[3,1,128]{2,1,0:T(1,128)S(1)} %broadcast_in_dim.7.scales, ...), custom_call_target="tpu_custom_call" | custom-call | flops 50000000 | bytes 1 | tf_op jit(solution)/shard_map/pallas_call | solution.py:190
  37.5 1.7 %shard_map.114 = bf16[5,64,768]{2,1,0:T(8,128)(2,1)} custom-call(s32[5]{0:T(128)S(1)} %dynamic_slice.132.shifts, bf16[5,64,768]{2,1,0:T(8,128)(2,1)S(1)} %bitcast.145, bf16[5,64,768]{2,1,0:T(8,128)(2,1)S(1)} %collective-permute-done.3.other), custom_call_target="tpu_custom_call" | custom-call | flops 2000000000 | bytes 1 | tf_op jit(solution)/shard_map/pallas_call | solution.py:84
  39.3 6.7 %collective-permute-done.4 = f16[192,1536]{1,0:T(8,128)(2,1)S(1)} collective-permute-done((f16[192,1536]{1,0:T(8,128)(2,1)S(1)}, f16[192,1536]{1,0:T(8,128)(2,1)S(1)}, u32[]{:S(2)}, u32[]{:S(2)}) %collective-permute-start.4) | collective-permute-done | bytes 589856 | tf_op jit(solution)/shard_map/ppermute | solution.py:34
  48.5 2.3 %copy.43 = bf16[320,1536]{0,1:T(8,128)(2,1)} copy(bf16[320,1536]{1,0:T(8,128)(2,1)} %pad_maximum_fusion) | data formatting | bytes 1966080 | tf_op jit(solution)/shard_map/concatenate | solution.py:446
  52.8 3.7 %shard_map.117 = (bf16[192,1152]{1,0:T(8,128)(2,1)S(1)}, f32[3,3,64,128]{3,2,1,0:T(8,128)S(1)}, bf16[192,384]{1,0:T(8,128)(2,1)S(1)}) custom-call(bf16[192,1536]{1,0:T(8,128)(2,1)S(1)} %copy-done.3, bf16[3,1536,384]{2,1,0:T(8,128)(2,1)S(1)} %bitcast.135, f32[3,1,128]{2,1,0:T(1,128)S(1)} %broadcast_in_dim.7.scales, f32[3,64,128]{2,1,0:T(8,128)S(1)} %copy-done.9), custom_call_target="tpu_custom_call" | custom-call | flops 50000000 | bytes 1 | tf_op jit(solution)/shard_map/pallas_call | solution.py:190
  58.0 2.4 %convolution_convert_fusion = bf16[1536,384]{1,0:T(8,128)(2,1)S(1)} fusion(bf16[320,384]{1,0:T(8,128)(2,1)S(1)} %pad_maximum_fusion.2, bf16[320,768]{1,0:T(8,128)(2,1)} %collective-permute-done.5.other_up, bf16[320,768]{1,0:T(8,128)(2,1)} %bitcast.11.own_up, pred[]{:T(512)S(6)} %eq.33), kind=kOutput, calls=%fused_computation.3 | convolution fusion | flops 382500864 | bytes 2408449 | tf_op jit(solution)/shard_map/dot_general | solution.py:62
  60.6 1.6 %collective-permute-start.9 = (bf16[8,96,384]{2,1,0:T(8,128)(2,1)S(1)}, bf16[8,96,384]{2,1,0:T(8,128)(2,1)S(1)}, u32[]{:S(2)}, u32[]{:S(2)}) collective-permute-start(bf16[8,96,384]{2,1,0:T(8,128)(2,1)S(1)} %bitcast.165), channel_id=1, source_target_pairs={{0,8},{8,0},{16,24},{24,16},{1,9},{9,1},{17,25},{25,17},{2,10},{10... | collective-permute-start | bytes 1769480 | tf_op jit(solution)/shard_map/ppermute | solution.py:34
  62.2 1.5 %collective-permute-start.7 = (bf16[320,768]{1,0:T(8,128)(2,1)S(1)}, bf16[320,768]{1,0:T(8,128)(2,1)S(1)}, u32[]{:S(2)}, u32[]{:S(2)}) collective-permute-start(bf16[320,768]{1,0:T(8,128)(2,1)S(1)} %get-tuple-element.68), channel_id=1, source_target_pairs={{0,1},{1,0},{2,3},{3,2},{4,5},{5,4},{6,7},{7,6},{8,9},{9,8},{10,11... | collective-permute-start | bytes 1474568 | tf_op jit(solution)/shard_map/ppermute | solution.py:34
  63.7 8.1 %shard_map.119 = (bf16[320,768]{1,0:T(8,128)(2,1)S(1)}, bf16[320,384]{1,0:T(8,128)(2,1)S(1)}) custom-call(s32[1]{0:T(128)} %bitcast.1.place, bf16[320,768]{1,0:T(8,128)(2,1)} %bitcast.11.own_up, bf16[320,768]{1,0:T(8,128)(2,1)} %collective-permute-done.5.other_up, bf16[384,1536]{1,0:T(8,128)(2,1)S(1)} %copy-done.7, f32[3,1,128]{2,1,0:T(1,128)S(1)} %broadcast_in_dim.7.scales, ...), custom_call_target="tpu_custom_call" | custom-call | flops 8999999488 | bytes 1 | tf_op jit(solution)/shard_map/pallas_call | solution.py:242
  72.8 1.6 %shard_map.120 = (bf16[160,1120]{1,0:T(8,128)(2,1)S(1)}, bf16[160,1120]{1,0:T(8,128)(2,1)S(1)}) custom-call(s32[1]{0:T(128)} %bitcast.1.place, bf16[320,768]{1,0:T(8,128)(2,1)S(1)} %get-tuple-element.66.mine, bf16[320,768]{1,0:T(8,128)(2,1)S(1)} %collective-permute-done.7.theirs, bf16[1120,768]{1,0:T(8,128)(2,1)S(1)} %bitcast.143, ...), custom_call_target="tpu_custom_call" | custom-call | flops 4000000000 | bytes 1 | tf_op jit(solution)/shard_map/pallas_call | solution.py:314
  74.4 1.8 %convolution_convert_fusion.2 = bf16[768,768]{1,0:T(8,128)(2,1)} fusion(bf16[320,768]{0,1:T(8,128)(2,1)S(1)} %bitcast.150, bf16[320,768]{1,0:T(8,128)(2,1)S(1)} %get-tuple-element.78), kind=kOutput, calls=%fused_computation.6 | convolution fusion | flops 378077184 | bytes 2162688 | tf_op jit(solution)/shard_map/dot_general | solution.py:62
  76.4 1.3 %convolution_convert_fusion.4 = bf16[768,384]{1,0:T(8,128)(2,1)} fusion(bf16[320,768]{0,1:T(8,128)(2,1)S(1)} %bitcast.151, bf16[320,384]{1,0:T(8,128)(2,1)S(1)} %get-tuple-element.80), kind=kOutput, calls=%fused_computation.8 | convolution fusion | flops 189038592 | bytes 1327104 | tf_op jit(solution)/shard_map/dot_general | solution.py:62
  78.2 1.5 %collective-permute-start.8 = (bf16[160,1120]{1,0:T(8,128)(2,1)S(1)}, bf16[160,1120]{1,0:T(8,128)(2,1)S(1)}, u32[]{:S(2)}, u32[]{:S(2)}) collective-permute-start(bf16[160,1120]{1,0:T(8,128)(2,1)S(1)} %get-tuple-element.70), channel_id=1, source_target_pairs={{0,1},{1,0},{2,3},{3,2},{4,5},{5,4},{6,7},{7,6},{8,9},{9,8},{10,11... | collective-permute-start | bytes 1075208 | tf_op jit(solution)/shard_map/ppermute | solution.py:34
  80.6 1.2 fusion.9
  81.9 1.6 %collective-permute-start.16 = (bf16[2,96,384]{2,1,0:T(8,128)(2,1)S(1)}, bf16[2,96,384]{2,1,0:T(8,128)(2,1)S(1)}, u32[]{:S(2)}, u32[]{:S(2)}) collective-permute-start(bf16[2,96,384]{2,1,0:T(8,128)(2,1)S(1)} %fusion.21), channel_id=1, source_target_pairs={{0,4},{2,6},{4,0},{6,2},{1,5},{3,7},{5,1},{7,3},{8,12},{10,14},{12... | collective-permute-start | bytes 442376 | tf_op jit(solution)/shard_map/ppermute | solution.py:34
  86.6 2.1 %collective-permute-done.8 = bf16[160,1120]{1,0:T(8,128)(2,1)S(1)} collective-permute-done((bf16[160,1120]{1,0:T(8,128)(2,1)S(1)}, bf16[160,1120]{1,0:T(8,128)(2,1)S(1)}, u32[]{:S(2)}, u32[]{:S(2)}) %collective-permute-start.8) | collective-permute-done | bytes 358432 | tf_op jit(solution)/shard_map/ppermute | solution.py:34
  92.1 8.8 %collective-permute-done.15 = bf16[2,2,96,768]{3,2,0,1:T(8,128)(2,1)S(1)} collective-permute-done((bf16[2,2,96,768]{3,2,0,1:T(8,128)(2,1)S(1)}, bf16[2,2,96,768]{3,2,0,1:T(8,128)(2,1)S(1)}, u32[]{:S(2)}, u32[]{:S(2)}) %collective-permute-start.15) | collective-permute-done | bytes 589856 | tf_op jit(solution)/shard_map/ppermute | solution.py:34
  102.1 1.6 %collective-permute-start.18 = (bf16[2,96,384]{2,1,0:T(8,128)(2,1)S(1)}, bf16[2,96,384]{2,1,0:T(8,128)(2,1)S(1)}, u32[]{:S(2)}, u32[]{:S(2)}) collective-permute-start(bf16[2,96,384]{2,1,0:T(8,128)(2,1)S(1)} %get-tuple-element.104), channel_id=1, source_target_pairs={{0,4},{2,6},{4,0},{6,2},{1,5},{3,7},{5,1},{7,3},{8,12},{10,14},{12... | collective-permute-start | bytes 442376 | tf_op jit(solution)/shard_map/ppermute | solution.py:34
  104.4 1.6 %shard_map.121 = bf16[5,32,1120]{2,1,0:T(8,128)(2,1)} custom-call(s32[5]{0:T(128)S(1)} %copy-done.24, bf16[5,32,1120]{2,1,0:T(8,128)(2,1)S(1)} %bitcast.139, bf16[5,32,1120]{2,1,0:T(8,128)(2,1)S(1)} %collective-permute-done.13.other), custom_call_target="tpu_custom_call" | custom-call | flops 2000000000 | bytes 1 | tf_op jit(solution)/shard_map/pallas_call | solution.py:84
  107.5 4.3 %collective-permute-done.17 = bf16[2,96,768]{2,1,0:T(8,128)(2,1)S(1)} collective-permute-done((bf16[2,96,768]{2,1,0:T(8,128)(2,1)S(1)}, bf16[2,96,768]{2,1,0:T(8,128)(2,1)S(1)}, u32[]{:S(2)}, u32[]{:S(2)}) %collective-permute-start.17) | collective-permute-done | bytes 294944 | tf_op jit(solution)/shard_map/ppermute | solution.py:34
  112.0 1.6 %collective-permute-done.21 = bf16[96,384]{1,0:T(8,128)(2,1)S(1)} collective-permute-done((bf16[96,384]{1,0:T(8,128)(2,1)S(1)}, bf16[96,384]{1,0:T(8,128)(2,1)S(1)}, u32[]{:S(2)}, u32[]{:S(2)}) %collective-permute-start.21) | collective-permute-done | bytes 73760 | tf_op jit(solution)/shard_map/ppermute | solution.py:34
  113.6 7.1 %collective-permute-done.20 = bf16[96,768]{1,0:T(8,128)(2,1)S(1)} collective-permute-done((bf16[96,768]{1,0:T(8,128)(2,1)S(1)}, bf16[96,768]{1,0:T(8,128)(2,1)S(1)}, u32[]{:S(2)}, u32[]{:S(2)}) %collective-permute-start.20) | collective-permute-done | bytes 147488 | tf_op jit(solution)/shard_map/ppermute | solution.py:34
  (131 shorter events, 29.0 us)
Async XLA Ops:
  0.6 10.1 %copy-start = (f32[6,225]{1,0:T(8,128)S(1)}, f32[6,225]{1,0:T(8,128)}, u32[]{:S(2)}) copy-start(f32[6,225]{1,0:T(8,128)} %param.16) | copy-start | bytes 16204
  0.6 9.2 %copy-start.27 = (s32[20]{0:T(128)S(1)}, s32[20]{0:T(128)}, u32[]{:S(2)}) copy-start(s32[20]{0:T(128)} %param.10) | copy-start | bytes 244
  1.7 19.6 %collective-permute-start = (bf16[2,64,1120]{2,1,0:T(8,128)(2,1)S(1)}, bf16[2,64,1120]{2,1,0:T(8,128)(2,1)}, u32[]{:S(2)}, u32[]{:S(2)}) collective-permute-start(bf16[2,64,1120]{2,1,0:T(8,128)(2,1)S(1)} %bitcast.140), channel_id=1, source_target_pairs={{0,24},{8,0},{16,8},{24,16},{1,25},{9,1},{17,9},{25,17},{2,26},{10... | collective-permute-start | bytes 860168 | tf_op jit(solution)/shard_map/ppermute | solution.py:29
  6.8 12.5 %collective-permute-start.1 = (bf16[160,1120]{1,0:T(8,128)(2,1)}, bf16[160,1120]{1,0:T(8,128)(2,1)}, u32[]{:S(2)}, u32[]{:S(2)}) collective-permute-start(bf16[160,1120]{1,0:T(8,128)(2,1)} %bitcast.146), channel_id=1, source_target_pairs={{0,1},{1,0},{2,3},{3,2},{4,5},{5,4},{6,7},{7,6},{8,9},{9,8},{10,11... | collective-permute-start | bytes 1075208 | tf_op jit(solution)/shard_map/ppermute | solution.py:34
  9.3 8.2 %copy-start.10 = (bf16[24,8,1120]{2,1,0:T(8,128)(2,1)}, bf16[24,8,1120]{2,1,0:T(8,128)(2,1)S(1)}, u32[]{:S(2)}) copy-start(bf16[24,8,1120]{2,1,0:T(8,128)(2,1)S(1)} %slice.20) | copy-start | bytes 1290244
  9.3 14.5 %collective-permute-start.2 = (bf16[3,64,1120]{2,1,0:T(8,128)(2,1)S(1)}, bf16[3,64,1120]{2,1,0:T(8,128)(2,1)S(1)}, u32[]{:S(2)}, u32[]{:S(2)}) collective-permute-start(bf16[3,64,1120]{2,1,0:T(8,128)(2,1)S(1)} %bitcast.136), channel_id=1, source_target_pairs={{0,24},{8,0},{16,8},{24,16},{1,25},{9,1},{17,9},{25,17},{2,26},{10... | collective-permute-start | bytes 1290248 | tf_op jit(solution)/shard_map/ppermute | solution.py:29
  10.7 8.5 %copy-start.15 = (bf16[768,1120]{0,1:T(8,128)(2,1)S(1)}, bf16[768,1120]{0,1:T(8,128)(2,1)}, u32[]{:S(2)}) copy-start(bf16[768,1120]{0,1:T(8,128)(2,1)} %param.14) | copy-start | bytes 5160964
  10.7 8.5 %copy-start.19 = (bf16[20,8,1120]{2,1,0:T(8,128)(2,1)S(1)}, bf16[20,8,1120]{2,1,0:T(8,128)(2,1)}, u32[]{:S(2)}) copy-start(bf16[20,8,1120]{2,1,0:T(8,128)(2,1)} %param.17) | copy-start | bytes 1075204
  23.3 11.6 %collective-permute-start.6 = (f16[128,1536]{1,0:T(8,128)(2,1)S(1)}, f16[128,1536]{1,0:T(8,128)(2,1)S(1)}, u32[]{:S(2)}, u32[]{:S(2)}) collective-permute-start(f16[128,1536]{1,0:T(8,128)(2,1)S(1)} %convert_element_type.346), channel_id=1, source_target_pairs={{0,1},{1,0},{2,3},{3,2},{4,5},{5,4},{6,7},{7,6},{8,9},{9,8},{10,11... | collective-permute-start | bytes 1179656 | tf_op jit(solution)/shard_map/ppermute | solution.py:34
  24.6 12.9 %collective-permute-start.3 = (bf16[5,64,768]{2,1,0:T(8,128)(2,1)S(1)}, bf16[5,64,768]{2,1,0:T(8,128)(2,1)S(1)}, u32[]{:S(2)}, u32[]{:S(2)}) collective-permute-start(bf16[5,64,768]{2,1,0:T(8,128)(2,1)S(1)} %bitcast.144), channel_id=1, source_target_pairs={{0,24},{8,0},{16,8},{24,16},{1,25},{9,1},{17,9},{25,17},{2,26},{10... | collective-permute-start | bytes 1474568 | tf_op jit(solution)/shard_map/ppermute | solution.py:29
  30.4 15.6 %collective-permute-start.4 = (f16[192,1536]{1,0:T(8,128)(2,1)S(1)}, f16[192,1536]{1,0:T(8,128)(2,1)S(1)}, u32[]{:S(2)}, u32[]{:S(2)}) collective-permute-start(f16[192,1536]{1,0:T(8,128)(2,1)S(1)} %convert_element_type.347), channel_id=1, source_target_pairs={{0,1},{1,0},{2,3},{3,2},{4,5},{5,4},{6,7},{7,6},{8,9},{9,8},{10,11... | collective-permute-start | bytes 1769480 | tf_op jit(solution)/shard_map/ppermute | solution.py:34
  35.0 11.7 %copy-start.5 = (bf16[128,1536]{1,0:T(8,128)(2,1)}, bf16[128,1536]{1,0:T(8,128)(2,1)S(1)}, u32[]{:S(2)}) copy-start(bf16[128,1536]{1,0:T(8,128)(2,1)S(1)} %multiply_convert_fusion.1.rolled.refs_0_) | copy-start | bytes 1179652
  46.0 12.0 %collective-permute-start.5 = (bf16[320,768]{1,0:T(8,128)(2,1)}, bf16[320,768]{1,0:T(8,128)(2,1)}, u32[]{:S(2)}, u32[]{:S(2)}) collective-permute-start(bf16[320,768]{1,0:T(8,128)(2,1)} %bitcast.11.own_up), channel_id=1, source_target_pairs={{0,1},{1,0},{2,3},{3,2},{4,5},{5,4},{6,7},{7,6},{8,9},{9,8},{10,11... | collective-permute-start | bytes 1474568 | tf_op jit(solution)/shard_map/ppermute | solution.py:34
  60.6 15.6 %collective-permute-start.9 = (bf16[8,96,384]{2,1,0:T(8,128)(2,1)S(1)}, bf16[8,96,384]{2,1,0:T(8,128)(2,1)S(1)}, u32[]{:S(2)}, u32[]{:S(2)}) collective-permute-start(bf16[8,96,384]{2,1,0:T(8,128)(2,1)S(1)} %bitcast.165), channel_id=1, source_target_pairs={{0,8},{8,0},{16,24},{24,16},{1,9},{9,1},{17,25},{25,17},{2,10},{10... | collective-permute-start | bytes 1769480 | tf_op jit(solution)/shard_map/ppermute | solution.py:34
  62.2 10.6 %collective-permute-start.7 = (bf16[320,768]{1,0:T(8,128)(2,1)S(1)}, bf16[320,768]{1,0:T(8,128)(2,1)S(1)}, u32[]{:S(2)}, u32[]{:S(2)}) collective-permute-start(bf16[320,768]{1,0:T(8,128)(2,1)S(1)} %get-tuple-element.68), channel_id=1, source_target_pairs={{0,1},{1,0},{2,3},{3,2},{4,5},{5,4},{6,7},{7,6},{8,9},{9,8},{10,11... | collective-permute-start | bytes 1474568 | tf_op jit(solution)/shard_map/ppermute | solution.py:34
  63.7 9.1 %copy-start.4 = (bf16[192,1536]{1,0:T(8,128)(2,1)S(1)}, bf16[192,1536]{1,0:T(8,128)(2,1)}, u32[]{:S(2)}) copy-start(bf16[192,1536]{1,0:T(8,128)(2,1)} %copy-done.2) | copy-start | bytes 1769476
  63.7 9.1 %copy-start.6 = (bf16[128,1536]{1,0:T(8,128)(2,1)S(1)}, bf16[128,1536]{1,0:T(8,128)(2,1)}, u32[]{:S(2)}) copy-start(bf16[128,1536]{1,0:T(8,128)(2,1)} %copy-done.5) | copy-start | bytes 1179652
  63.7 9.1 %copy-start.16 = (bf16[768,1120]{0,1:T(8,128)(2,1)S(1)}, bf16[768,1120]{0,1:T(8,128)(2,1)}, u32[]{:S(2)}) copy-start(bf16[768,1120]{0,1:T(8,128)(2,1)} %param.14) | copy-start | bytes 5160964
  76.3 4.3 %collective-permute-start.11 = (bf16[8,96,768]{2,1,0:T(8,128)(2,1)}, bf16[8,96,768]{2,1,0:T(8,128)(2,1)}, u32[]{:S(2)}, u32[]{:S(2)}) collective-permute-start(bf16[8,96,768]{2,1,0:T(8,128)(2,1)} %bitcast.19), channel_id=1, source_target_pairs={{0,2},{2,0},{4,6},{6,4},{1,3},{3,1},{5,7},{7,5},{8,10},{10,8},{12,... | collective-permute-start | bytes 3538952 | tf_op jit(solution)/shard_map/ppermute | solution.py:34
  77.7 2.9 %collective-permute-start.12 = (bf16[8,96,384]{2,1,0:T(8,128)(2,1)}, bf16[8,96,384]{2,1,0:T(8,128)(2,1)}, u32[]{:S(2)}, u32[]{:S(2)}) collective-permute-start(bf16[8,96,384]{2,1,0:T(8,128)(2,1)} %bitcast.23), channel_id=1, source_target_pairs={{0,2},{2,0},{4,6},{6,4},{1,3},{3,1},{5,7},{7,5},{8,10},{10,8},{12,... | collective-permute-start | bytes 1769480 | tf_op jit(solution)/shard_map/ppermute | solution.py:34
  78.2 10.5 %collective-permute-start.8 = (bf16[160,1120]{1,0:T(8,128)(2,1)S(1)}, bf16[160,1120]{1,0:T(8,128)(2,1)S(1)}, u32[]{:S(2)}, u32[]{:S(2)}) collective-permute-start(bf16[160,1120]{1,0:T(8,128)(2,1)S(1)} %get-tuple-element.70), channel_id=1, source_target_pairs={{0,1},{1,0},{2,3},{3,2},{4,5},{5,4},{6,7},{7,6},{8,9},{9,8},{10,11... | collective-permute-start | bytes 1075208 | tf_op jit(solution)/shard_map/ppermute | solution.py:34
  79.7 2.1 %collective-permute-start.10 = (bf16[2,2,96,384]{3,2,1,0:T(8,128)(2,1)S(1)}, bf16[2,2,96,384]{3,2,1,0:T(8,128)(2,1)S(1)}, u32[]{:S(2)}, u32[]{:S(2)}) collective-permute-start(bf16[2,2,96,384]{3,2,1,0:T(8,128)(2,1)S(1)} %fusion.12), channel_id=1, source_target_pairs={{0,2},{2,0},{4,6},{6,4},{1,3},{3,1},{5,7},{7,5},{8,10},{10,8},{12,... | collective-permute-start | bytes 884744 | tf_op jit(solution)/shard_map/ppermute | solution.py:34
  81.9 10.1 %collective-permute-start.16 = (bf16[2,96,384]{2,1,0:T(8,128)(2,1)S(1)}, bf16[2,96,384]{2,1,0:T(8,128)(2,1)S(1)}, u32[]{:S(2)}, u32[]{:S(2)}) collective-permute-start(bf16[2,96,384]{2,1,0:T(8,128)(2,1)S(1)} %fusion.21), channel_id=1, source_target_pairs={{0,4},{2,6},{4,0},{6,2},{1,5},{3,7},{5,1},{7,3},{8,12},{10,14},{12... | collective-permute-start | bytes 442376 | tf_op jit(solution)/shard_map/ppermute | solution.py:34
  83.5 17.4 %collective-permute-start.15 = (bf16[2,2,96,768]{3,2,0,1:T(8,128)(2,1)S(1)}, bf16[2,2,96,768]{3,2,0,1:T(8,128)(2,1)S(1)}, u32[]{:S(2)}, u32[]{:S(2)}) collective-permute-start(bf16[2,2,96,768]{3,2,0,1:T(8,128)(2,1)S(1)} %fusion.9), channel_id=1, source_target_pairs={{0,4},{2,6},{4,0},{6,2},{1,5},{3,7},{5,1},{7,3},{8,12},{10,14},{12... | collective-permute-start | bytes 1769480 | tf_op jit(solution)/shard_map/ppermute | solution.py:34
  85.5 16.5 %collective-permute-start.14 = (bf16[2,2,96,384]{3,2,1,0:T(8,128)(2,1)S(1)}, bf16[2,2,96,384]{3,2,1,0:T(8,128)(2,1)S(1)}, u32[]{:S(2)}, u32[]{:S(2)}) collective-permute-start(bf16[2,2,96,384]{3,2,1,0:T(8,128)(2,1)S(1)} %fusion.13), channel_id=1, source_target_pairs={{0,8},{8,0},{16,24},{24,16},{1,9},{9,1},{17,25},{25,17},{2,10},{10... | collective-permute-start | bytes 884744 | tf_op jit(solution)/shard_map/ppermute | solution.py:34
  91.1 13.3 %collective-permute-start.13 = (bf16[5,32,1120]{2,1,0:T(8,128)(2,1)S(1)}, bf16[5,32,1120]{2,1,0:T(8,128)(2,1)S(1)}, u32[]{:S(2)}, u32[]{:S(2)}) collective-permute-start(bf16[5,32,1120]{2,1,0:T(8,128)(2,1)S(1)} %bitcast.138), channel_id=1, source_target_pairs={{0,8},{8,16},{16,24},{24,0},{1,9},{9,17},{17,25},{25,1},{2,10},{10... | collective-permute-start | bytes 1075208 | tf_op jit(solution)/shard_map/ppermute | solution.py:29
  92.0 12.4 %copy-start.24 = (s32[5]{0:T(128)S(1)}, s32[5]{0:T(128)}, u32[]{:S(2)}) copy-start(s32[5]{0:T(128)} %and_select_fusion.1.shifts) | copy-start | bytes 64
  92.0 14.0 %collective-permute-start.19 = (bf16[96,384]{1,0:T(8,128)(2,1)S(1)}, bf16[96,384]{1,0:T(8,128)(2,1)S(1)}, u32[]{:S(2)}, u32[]{:S(2)}) collective-permute-start(bf16[96,384]{1,0:T(8,128)(2,1)S(1)} %fusion.30), channel_id=1, source_target_pairs={{0,16},{8,24},{16,0},{24,8},{1,17},{9,25},{17,1},{25,9},{2,18},{10... | collective-permute-start | bytes 221192 | tf_op jit(solution)/shard_map/ppermute | solution.py:34
  101.0 10.8 %collective-permute-start.17 = (bf16[2,96,768]{2,1,0:T(8,128)(2,1)S(1)}, bf16[2,96,768]{2,1,0:T(8,128)(2,1)S(1)}, u32[]{:S(2)}, u32[]{:S(2)}) collective-permute-start(bf16[2,96,768]{2,1,0:T(8,128)(2,1)S(1)} %get-tuple-element.98), channel_id=1, source_target_pairs={{0,8},{8,0},{16,24},{24,16},{1,9},{9,1},{17,25},{25,17},{2,10},{10... | collective-permute-start | bytes 884744 | tf_op jit(solution)/shard_map/ppermute | solution.py:34
  102.1 5.3 %collective-permute-start.18 = (bf16[2,96,384]{2,1,0:T(8,128)(2,1)S(1)}, bf16[2,96,384]{2,1,0:T(8,128)(2,1)S(1)}, u32[]{:S(2)}, u32[]{:S(2)}) collective-permute-start(bf16[2,96,384]{2,1,0:T(8,128)(2,1)S(1)} %get-tuple-element.104), channel_id=1, source_target_pairs={{0,4},{2,6},{4,0},{6,2},{1,5},{3,7},{5,1},{7,3},{8,12},{10,14},{12... | collective-permute-start | bytes 442376 | tf_op jit(solution)/shard_map/ppermute | solution.py:34
  107.4 6.1 %collective-permute-start.21 = (bf16[96,384]{1,0:T(8,128)(2,1)S(1)}, bf16[96,384]{1,0:T(8,128)(2,1)S(1)}, u32[]{:S(2)}, u32[]{:S(2)}) collective-permute-start(bf16[96,384]{1,0:T(8,128)(2,1)S(1)} %fusion.31), channel_id=1, source_target_pairs={{0,16},{8,24},{16,0},{24,8},{1,17},{9,25},{17,1},{25,9},{2,18},{10... | collective-permute-start | bytes 221192 | tf_op jit(solution)/shard_map/ppermute | solution.py:34
  111.9 8.8 %collective-permute-start.20 = (bf16[96,768]{1,0:T(8,128)(2,1)S(1)}, bf16[96,768]{1,0:T(8,128)(2,1)S(1)}, u32[]{:S(2)}, u32[]{:S(2)}) collective-permute-start(bf16[96,768]{1,0:T(8,128)(2,1)S(1)} %fusion.24), channel_id=1, source_target_pairs={{0,16},{8,24},{16,0},{24,8},{1,17},{9,25},{17,1},{25,9},{2,18},{10... | collective-permute-start | bytes 442376 | tf_op jit(solution)/shard_map/ppermute | solution.py:34
  (19 other events, 54.2 us)

commit v3 on v2

--- a/solution.py
+++ b/solution.py
@@ -420,18 +420,15 @@
     )
     biases = biases.reshape(pairs, 2, SPAN, SPAN).transpose(0, 2, 1, 3).reshape(pairs, SPAN, PAIR)
 
-    half_up = half_up_call(place, cot, other_cot, w_head.T)
-    next_tiles[0], half_up, biases, strip_offsets = lax.optimization_barrier(
-        (next_tiles[0], half_up, biases, strip_offsets)
+    next_tiles[0], biases, strip_offsets = lax.optimization_barrier(
+        (next_tiles[0], biases, strip_offsets)
     )
     terms, other_terms = [], []
     for index, (shift, tile, next_tile) in enumerate(zip(shifts, tiles, next_tiles)):
-        if terms:
-            next_tile = after(next_tile, terms[-1])
-            half_up = after(half_up, next_tile)
         terms.append(embed_call(shift, tile, next_tile, w_embed).astype(F16))
         other_terms.append(swapped(terms[-1], "mp", 1))
-    half_up = half_up.reshape(groups, SPAN, -1)
+    half_up = half_up_call(place, cot, after(other_cot, terms[0]), w_head.T)
+    half_up = after(half_up, terms[1]).reshape(groups, SPAN, -1)
     own_up = roll_call(offsets, half_up, moved(half_up, "lon", -1), 1)
     own_up = own_up.reshape(groups * SPAN, -1)
     other_up = swapped(after(own_up, other_terms[-1]), "mp", 1)
@@ -469,22 +466,21 @@
     def products(left, right):
         return dot(left, right, 0, 0).astype(BF).reshape(pieces // 2, model // pieces, -1)
 
-    pred_here, pred_there = head_call(place, after(mixed_here, d_qk), mixed_got, w_head.T, rolled)
+    v_send = products(left_send, d_value)
+    pred_here, pred_there = head_call(
+        place, after(mixed_here, v_send, d_qk), mixed_got, w_head.T, rolled
+    )
     qk_send = products(left_send, after(d_qk, pred_there))
     sum_p.got = after(sum_p.got, qk_send)
     sent = sum_p.step()
     qk_send = after(qk_send, sent)
-    v_send = products(left_send, after(d_value, qk_send))
-    qk_keep = products(left_keep, after(d_qk, v_send))
+    v_keep = products(left_keep, after(d_value, qk_send))
+    sum_v = Sum(v_keep, v_send, v_order)
+    sent = sum_v.step()
+    qk_keep = products(left_keep, after(d_qk, sent))
     sum_qk = Sum(qk_keep, qk_send, all_bits)
     sum_qk.got = after(sum_qk.got, qk_keep)
     sent = sum_qk.step()
-    sum_p.got = after(sum_p.got, sent)
-    sent = sum_p.step()
-    v_keep = products(left_keep, after(d_value, sent))
-    sum_v = Sum(v_keep, v_send, v_order)
-    sum_v.got = after(sum_v.got, v_keep)
-    sent = sum_v.step()
     pred_got = after(swapped(pred_there, "mp", 1), sent)
     pred = (pred_here.astype(F32) + pred_got.astype(F32)).astype(BF)
     pred = pred.reshape(strips, strip * WIN, outputs)
@@ -495,15 +491,17 @@
     sent = sum_qk.step()
     sum_v.got = after(sum_v.got, sent)
     sent = sum_v.step()
+    sum_p.got = after(sum_p.got, sent)
+    sent = sum_p.step()
     before = after(before, sent)
     prediction = roll_call(strip_offsets, pred, before, -1).reshape(rows_here, breadth, outputs)
-    sum_p.got = after(sum_p.got, prediction)
-    grad_proj = sum_p.result().T
-    sum_v.got = after(sum_v.got, grad_proj)
+    sum_v.got = after(sum_v.got, prediction)
     sent = sum_v.step()
     sum_qk.got = after(sum_qk.got, sent)
     sent = sum_qk.step()
-    sum_v.got = after(sum_v.got, sent)
+    sum_p.got = after(sum_p.got, sent)
+    grad_proj = sum_p.result().T
+    sum_v.got = after(sum_v.got, grad_proj)
     grad_v = sum_v.result()
     sum_qk.got = after(sum_qk.got, grad_v)
     grad_qk = sum_qk.result()

time: 122 us -> 120 us (0.984)
  waiting for transfers between devices: 36 us -> 26.2 us
  starting transfers between devices: 24.7 us -> 32.9 us
  Pallas kernels: 25.5 us -> 24 us
    ppermute x18, waiting for transfers between devices: 35.3 us -> 18.7 us  [swapped(): lax.ppermute(value, axis, [(source, source ^ bit) for source in range(cou...]
    ppermute x4, waiting for transfers between devices: 0.7 us -> 7.48 us  [moved(): return lax.ppermute(value, axis, pairs)]
    ppermute x18, starting transfers between devices: 15.3 us -> 21.9 us  [swapped(): lax.ppermute(value, axis, [(source, source ^ bit) for source in range(cou...]
    unnamed x58 -> x66, local copies, waits for them, and re-layouts: 5.28 us -> 8.21 us
    ppermute x4, starting transfers between devices: 9.36 us -> 11 us  [moved(): return lax.ppermute(value, axis, pairs)]
  transfers between devices with their start and end apart: 22 -> 22, of which waited for: 11 -> 6; matrix products, arithmetic and copies ran while one was open for 20% -> 19% of each run, Pallas kernels for 21% -> 20%
where the time goes in v3:
time: 120 us
  starting transfers between devices  32.9 us (27%)
  waiting for transfers between devices  26.2 us (22%)
  Pallas kernels  24 us (20%)
  local copies, waits for them, and re-layouts  16.3 us (14%)
  matrix products  10.1 us (8%)
  other arithmetic  8.99 us (7%)
    ppermute x18, starting transfers between devices, swapped(): lax.ppermute(value, axis, [(source, source ^ bit) for source in range(cou...  21.9 us
    ppermute x18, waiting for transfers between devices, swapped(): lax.ppermute(value, axis, [(source, source ^ bit) for source in range(cou...  18.7 us
    ppermute x4, starting transfers between devices, moved(): return lax.ppermute(value, axis, pairs)  11 us
    unnamed x66, local copies, waits for them, and re-layouts  8.21 us
    pallas_call x1, Pallas kernels, backward_call(): call(functools.partial(backward_kernel, len(qkv)), (shape((rows, 2 * widt...  8.06 us
    ppermute x4, waiting for transfers between devices, moved(): return lax.ppermute(value, axis, pairs)  7.48 us
    dot_general x5, matrix products, dot(): lax.dot_general(a, b, (((ca,), (cb,)), ((), ())), preferred_element_type=...  6.86 us
    pallas_call x2, Pallas kernels, forward_call(): call(forward_kernel, out_shape, 'vvvv', 0.05)(rolled, w_qkv, scales, biases)  6.17 us
  transfers between devices with their start and end apart: 22, of which 6 were waited for; matrix products, arithmetic and copies ran while one was open for 19% of the time, Pallas kernels for 20%

profile of v3, /device:TPU:0, one launch (start us, length us, event | category | flops | bytes accessed | tf_op | source)
XLA Modules:
  0.0 119.6 jit_solution(8456459640262379684)
XLA Ops:
  1.7 5.1 %collective-permute-start = (bf16[2,64,1120]{2,1,0:T(8,128)(2,1)S(1)}, bf16[2,64,1120]{2,1,0:T(8,128)(2,1)S(1)}, u32[]{:S(2)}, u32[]{:S(2)}) collective-permute-start(bf16[2,64,1120]{2,1,0:T(8,128)(2,1)S(1)} %bitcast.142), channel_id=1, source_target_pairs={{0,24},{8,0},{16,8},{24,16},{1,25},{9,1},{17,9},{25,17},{2,26},{10... | collective-permute-start | bytes 860168 | tf_op jit(solution)/shard_map/ppermute | solution.py:29
  6.8 1.5 %collective-permute-start.1 = (bf16[160,1120]{1,0:T(8,128)(2,1)}, bf16[160,1120]{1,0:T(8,128)(2,1)S(1)}, u32[]{:S(2)}, u32[]{:S(2)}) collective-permute-start(bf16[160,1120]{1,0:T(8,128)(2,1)} %bitcast.148), channel_id=1, source_target_pairs={{0,1},{1,0},{2,3},{3,2},{4,5},{5,4},{6,7},{7,6},{8,9},{9,8},{10,11... | collective-permute-start | bytes 1075208 | tf_op jit(solution)/shard_map/ppermute | solution.py:34
  10.9 3.2 %fusion.2 = f32[6,64,64]{1,0,2:T(8,128)S(1)} fusion(s32[64,64]{1,0:T(8,128)S(1)} %add_add_fusion, f32[6,225]{1,0:T(8,128)S(1)} %copy-done), kind=kOutput, calls=%fused_computation.12 | convolution fusion | flops 67276800 | bytes 120088 | tf_op jit(solution)/shard_map/ije,he->hji/dot_general | solution.py:418
  16.4 2.0 %copy-done.14 = bf16[1120,1536]{1,0:T(8,128)(2,1)S(1)} copy-done((bf16[1120,1536]{1,0:T(8,128)(2,1)S(1)}, bf16[1120,1536]{1,0:T(8,128)(2,1)}, u32[]{:S(2)}) %copy-start.14) | copy-done | bytes 3440664
  18.4 1.5 %shard_map.112 = f32[128,1536]{1,0:T(8,128)S(1)} custom-call(s32[2]{0:T(128)S(1)} %bitcast.135, bf16[2,64,1120]{2,1,0:T(8,128)(2,1)S(1)} %bitcast.143, bf16[2,64,1120]{2,1,0:T(8,128)(2,1)S(1)} %collective-permute-done.other, bf16[1120,1536]{1,0:T(8,128)(2,1)S(1)} %copy-done.14), custom_call_target="tpu_custom_call" | custom-call | flops 5000000000 | bytes 1 | tf_op jit(solution)/shard_map/pallas_call | solution.py:98
  24.3 1.8 %shard_map.114 = f32[192,1536]{1,0:T(8,128)S(1)} custom-call(s32[3]{0:T(128)S(1)} %copy-done.26, bf16[3,64,1120]{2,1,0:T(8,128)(2,1)S(1)} %bitcast.139, bf16[3,64,1120]{2,1,0:T(8,128)(2,1)S(1)} %copy-done.19, bf16[1120,1536]{1,0:T(8,128)(2,1)S(1)} %copy-done.15), custom_call_target="tpu_custom_call" | custom-call | flops 5000000000 | bytes 1 | tf_op jit(solution)/shard_map/pallas_call | solution.py:98
  26.2 1.6 %collective-permute-start.4 = (f16[192,1536]{1,0:T(8,128)(2,1)S(1)}, f16[192,1536]{1,0:T(8,128)(2,1)S(1)}, u32[]{:S(2)}, u32[]{:S(2)}) collective-permute-start(f16[192,1536]{1,0:T(8,128)(2,1)S(1)} %convert_element_type.347), channel_id=1, source_target_pairs={{0,1},{1,0},{2,3},{3,2},{4,5},{5,4},{6,7},{7,6},{8,9},{9,8},{10,11... | collective-permute-start | bytes 1769480 | tf_op jit(solution)/shard_map/ppermute | solution.py:34
  27.8 4.3 %collective-permute-start.3 = (bf16[5,64,768]{2,1,0:T(8,128)(2,1)S(1)}, bf16[5,64,768]{2,1,0:T(8,128)(2,1)S(1)}, u32[]{:S(2)}, u32[]{:S(2)}) collective-permute-start(bf16[5,64,768]{2,1,0:T(8,128)(2,1)S(1)} %bitcast.146), channel_id=1, source_target_pairs={{0,24},{8,0},{16,8},{24,16},{1,25},{9,1},{17,9},{25,17},{2,26},{10... | collective-permute-start | bytes 1474568 | tf_op jit(solution)/shard_map/ppermute | solution.py:29
  32.2 2.5 %shard_map.116 = (bf16[128,1152]{1,0:T(8,128)(2,1)S(1)}, f32[2,3,64,128]{3,2,1,0:T(8,128)S(1)}, bf16[128,384]{1,0:T(8,128)(2,1)S(1)}) custom-call(bf16[128,1536]{1,0:T(8,128)(2,1)S(1)} %multiply_convert_fusion.1.rolled.refs_0_, bf16[3,1536,384]{2,1,0:T(8,128)(2,1)S(1)} %bitcast.136, f32[3,1,128]{2,1,0:T(1,128)S(1)} %broadcast_in_dim.7.scales, ...), custom_call_target="tpu_custom_call" | custom-call | flops 50000000 | bytes 1 | tf_op jit(solution)/shard_map/pallas_call | solution.py:190
  34.8 6.6 %collective-permute-done.3.other = bf16[5,64,768]{2,1,0:T(8,128)(2,1)S(1)} collective-permute-done((bf16[5,64,768]{2,1,0:T(8,128)(2,1)S(1)}, bf16[5,64,768]{2,1,0:T(8,128)(2,1)S(1)}, u32[]{:S(2)}, u32[]{:S(2)}) %collective-permute-start.3) | collective-permute-done | bytes 491552 | tf_op jit(solution)/shard_map/ppermute | solution.py:29
  41.4 1.7 %shard_map.115 = bf16[5,64,768]{2,1,0:T(8,128)(2,1)} custom-call(s32[5]{0:T(128)S(1)} %dynamic_slice.132.shifts, bf16[5,64,768]{2,1,0:T(8,128)(2,1)S(1)} %bitcast.147, bf16[5,64,768]{2,1,0:T(8,128)(2,1)S(1)} %collective-permute-done.3.other), custom_call_target="tpu_custom_call" | custom-call | flops 2000000000 | bytes 1 | tf_op jit(solution)/shard_map/pallas_call | solution.py:84
  45.8 2.3 %copy.42 = bf16[320,1536]{0,1:T(8,128)(2,1)} copy(bf16[320,1536]{1,0:T(8,128)(2,1)} %pad_maximum_fusion) | data formatting | bytes 1966080 | tf_op jit(solution)/shard_map/concatenate | solution.py:443
  50.1 3.7 %shard_map.117 = (bf16[192,1152]{1,0:T(8,128)(2,1)S(1)}, f32[3,3,64,128]{3,2,1,0:T(8,128)S(1)}, bf16[192,384]{1,0:T(8,128)(2,1)S(1)}) custom-call(bf16[192,1536]{1,0:T(8,128)(2,1)S(1)} %copy-done.3, bf16[3,1536,384]{2,1,0:T(8,128)(2,1)S(1)} %bitcast.137, f32[3,1,128]{2,1,0:T(1,128)S(1)} %broadcast_in_dim.7.scales, f32[3,64,128]{2,1,0:T(8,128)S(1)} %copy-done.9), custom_call_target="tpu_custom_call" | custom-call | flops 50000000 | bytes 1 | tf_op jit(solution)/shard_map/pallas_call | solution.py:190
  55.2 2.4 %convolution_convert_fusion = bf16[1536,384]{1,0:T(8,128)(2,1)S(1)} fusion(bf16[320,384]{1,0:T(8,128)(2,1)S(1)} %pad_maximum_fusion.2, bf16[320,768]{1,0:T(8,128)(2,1)} %collective-permute-done.5.other_up, bf16[320,768]{1,0:T(8,128)(2,1)} %bitcast.11.own_up, pred[]{:T(512)S(6)} %eq.33), kind=kOutput, calls=%fused_computation.3 | convolution fusion | flops 382500864 | bytes 2408449 | tf_op jit(solution)/shard_map/dot_general | solution.py:62
  58.8 1.5 %collective-permute-start.7 = (bf16[320,768]{1,0:T(8,128)(2,1)S(1)}, bf16[320,768]{1,0:T(8,128)(2,1)S(1)}, u32[]{:S(2)}, u32[]{:S(2)}) collective-permute-start(bf16[320,768]{1,0:T(8,128)(2,1)S(1)} %get-tuple-element.67), channel_id=1, source_target_pairs={{0,1},{1,0},{2,3},{3,2},{4,5},{5,4},{6,7},{7,6},{8,9},{9,8},{10,11... | collective-permute-start | bytes 1474568 | tf_op jit(solution)/shard_map/ppermute | solution.py:34
  60.3 8.1 %shard_map.119 = (bf16[320,768]{1,0:T(8,128)(2,1)S(1)}, bf16[320,384]{1,0:T(8,128)(2,1)S(1)}) custom-call(s32[1]{0:T(128)} %bitcast.6.place, bf16[320,768]{1,0:T(8,128)(2,1)} %bitcast.11.own_up, bf16[320,768]{1,0:T(8,128)(2,1)} %collective-permute-done.5.other_up, bf16[384,1536]{1,0:T(8,128)(2,1)S(1)} %copy-done.7, f32[3,1,128]{2,1,0:T(1,128)S(1)} %broadcast_in_dim.7.scales, ...), custom_call_target="tpu_custom_call" | custom-call | flops 8999999488 | bytes 1 | tf_op jit(solution)/shard_map/pallas_call | solution.py:242
  68.4 1.3 %convolution_convert_fusion.4 = bf16[768,384]{1,0:T(8,128)(2,1)} fusion(bf16[320,768]{0,1:T(8,128)(2,1)S(1)} %bitcast.152, bf16[320,384]{1,0:T(8,128)(2,1)S(1)} %get-tuple-element.74), kind=kOutput, calls=%fused_computation.8 | convolution fusion | flops 189038592 | bytes 1327104 | tf_op jit(solution)/shard_map/dot_general | solution.py:62
  69.8 1.6 %shard_map.120 = (bf16[160,1120]{1,0:T(8,128)(2,1)S(1)}, bf16[160,1120]{1,0:T(8,128)(2,1)S(1)}) custom-call(s32[1]{0:T(128)} %bitcast.6.place, bf16[320,768]{1,0:T(8,128)(2,1)S(1)} %get-tuple-element.65.mine, bf16[320,768]{1,0:T(8,128)(2,1)S(1)} %collective-permute-done.7.theirs, bf16[1120,768]{1,0:T(8,128)(2,1)S(1)} %bitcast.145, ...), custom_call_target="tpu_custom_call" | custom-call | flops 4000000000 | bytes 1 | tf_op jit(solution)/shard_map/pallas_call | solution.py:314
  71.4 1.8 %convolution_convert_fusion.2 = bf16[768,768]{1,0:T(8,128)(2,1)} fusion(bf16[320,768]{0,1:T(8,128)(2,1)S(1)} %bitcast.153, bf16[320,768]{1,0:T(8,128)(2,1)S(1)} %get-tuple-element.75), kind=kOutput, calls=%fused_computation.6 | convolution fusion | flops 378077184 | bytes 2162688 | tf_op jit(solution)/shard_map/dot_general | solution.py:62
  80.7 1.2 %fusion.9 = bf16[2,2,96,768]{3,2,0,1:T(8,128)(2,1)S(1)} fusion(bf16[2,2,2,96,768]{4,3,2,1,0:T(8,128)(2,1)S(1)} %bitcast.154, s32[]{:T(128)S(6)} %select_n.205, bf16[2,2,2,96,768]{4,3,2,1,0:T(8,128)(2,1)} %bitcast.27), kind=kLoop, calls=%fused_computation.23 | loop fusion | flops 1179648 | bytes 1770496 | tf_op jit(solution)/shard_map/convert_element_type | solution.py:368
  82.0 1.5 %collective-permute-start.16 = (bf16[2,2,96,768]{3,2,0,1:T(8,128)(2,1)S(1)}, bf16[2,2,96,768]{3,2,0,1:T(8,128)(2,1)S(1)}, u32[]{:S(2)}, u32[]{:S(2)}) collective-permute-start(bf16[2,2,96,768]{3,2,0,1:T(8,128)(2,1)S(1)} %fusion.9), channel_id=1, source_target_pairs={{0,4},{2,6},{4,0},{6,2},{1,5},{3,7},{5,1},{7,3},{8,12},{10,14},{12... | collective-permute-start | bytes 1769480 | tf_op jit(solution)/shard_map/ppermute | solution.py:34
  83.5 1.6 %collective-permute-done.8 = bf16[160,1120]{1,0:T(8,128)(2,1)S(1)} collective-permute-done((bf16[160,1120]{1,0:T(8,128)(2,1)S(1)}, bf16[160,1120]{1,0:T(8,128)(2,1)S(1)}, u32[]{:S(2)}, u32[]{:S(2)}) %collective-permute-start.8) | collective-permute-done | bytes 358432 | tf_op jit(solution)/shard_map/ppermute | solution.py:34
  87.6 1.6 %collective-permute-start.14 = (bf16[2,96,384]{2,1,0:T(8,128)(2,1)S(1)}, bf16[2,96,384]{2,1,0:T(8,128)(2,1)S(1)}, u32[]{:S(2)}, u32[]{:S(2)}) collective-permute-start(bf16[2,96,384]{2,1,0:T(8,128)(2,1)S(1)} %fusion.21), channel_id=1, source_target_pairs={{0,4},{2,6},{4,0},{6,2},{1,5},{3,7},{5,1},{7,3},{8,12},{10,14},{12... | collective-permute-start | bytes 442376 | tf_op jit(solution)/shard_map/ppermute | solution.py:34
  89.2 9.0 %collective-permute-done.16 = bf16[2,2,96,768]{3,2,0,1:T(8,128)(2,1)S(1)} collective-permute-done((bf16[2,2,96,768]{3,2,0,1:T(8,128)(2,1)S(1)}, bf16[2,2,96,768]{3,2,0,1:T(8,128)(2,1)S(1)}, u32[]{:S(2)}, u32[]{:S(2)}) %collective-permute-start.16) | collective-permute-done | bytes 589856 | tf_op jit(solution)/shard_map/ppermute | solution.py:34
  98.3 1.4 %collective-permute-start.17 = (bf16[2,96,768]{2,1,0:T(8,128)(2,1)S(1)}, bf16[2,96,768]{2,1,0:T(8,128)(2,1)S(1)}, u32[]{:S(2)}, u32[]{:S(2)}) collective-permute-start(bf16[2,96,768]{2,1,0:T(8,128)(2,1)S(1)} %get-tuple-element.94), channel_id=1, source_target_pairs={{0,8},{8,0},{16,24},{24,16},{1,9},{9,1},{17,25},{25,17},{2,10},{10... | collective-permute-start | bytes 884744 | tf_op jit(solution)/shard_map/ppermute | solution.py:34
  99.8 1.6 %collective-permute-start.18 = (bf16[2,96,384]{2,1,0:T(8,128)(2,1)S(1)}, bf16[2,96,384]{2,1,0:T(8,128)(2,1)S(1)}, u32[]{:S(2)}, u32[]{:S(2)}) collective-permute-start(bf16[2,96,384]{2,1,0:T(8,128)(2,1)S(1)} %get-tuple-element.100), channel_id=1, source_target_pairs={{0,4},{2,6},{4,0},{6,2},{1,5},{3,7},{5,1},{7,3},{8,12},{10,14},{12... | collective-permute-start | bytes 442376 | tf_op jit(solution)/shard_map/ppermute | solution.py:34
  101.4 3.6 %collective-permute-start.21 = (bf16[96,384]{1,0:T(8,128)(2,1)S(1)}, bf16[96,384]{1,0:T(8,128)(2,1)S(1)}, u32[]{:S(2)}, u32[]{:S(2)}) collective-permute-start(bf16[96,384]{1,0:T(8,128)(2,1)S(1)} %fusion.30), channel_id=1, source_target_pairs={{0,16},{8,24},{16,0},{24,8},{1,17},{9,25},{17,1},{25,9},{2,18},{10... | collective-permute-start | bytes 221192 | tf_op jit(solution)/shard_map/ppermute | solution.py:34
  105.0 1.6 %shard_map.121 = bf16[5,32,1120]{2,1,0:T(8,128)(2,1)} custom-call(s32[5]{0:T(128)S(1)} %copy-done.25, bf16[5,32,1120]{2,1,0:T(8,128)(2,1)S(1)} %bitcast.141, bf16[5,32,1120]{2,1,0:T(8,128)(2,1)S(1)} %collective-permute-done.12.other), custom_call_target="tpu_custom_call" | custom-call | flops 2000000000 | bytes 1 | tf_op jit(solution)/shard_map/pallas_call | solution.py:84
  106.6 2.0 %collective-permute-start.20 = (bf16[96,384]{1,0:T(8,128)(2,1)S(1)}, bf16[96,384]{1,0:T(8,128)(2,1)S(1)}, u32[]{:S(2)}, u32[]{:S(2)}) collective-permute-start(bf16[96,384]{1,0:T(8,128)(2,1)S(1)} %fusion.31), channel_id=1, source_target_pairs={{0,16},{8,24},{16,0},{24,8},{1,17},{9,25},{17,1},{25,9},{2,18},{10... | collective-permute-start | bytes 221192 | tf_op jit(solution)/shard_map/ppermute | solution.py:34
  108.7 1.2 %collective-permute-start.19 = (bf16[96,768]{1,0:T(8,128)(2,1)S(1)}, bf16[96,768]{1,0:T(8,128)(2,1)S(1)}, u32[]{:S(2)}, u32[]{:S(2)}) collective-permute-start(bf16[96,768]{1,0:T(8,128)(2,1)S(1)} %fusion.24), channel_id=1, source_target_pairs={{0,16},{8,24},{16,0},{24,8},{1,17},{9,25},{17,1},{25,9},{2,18},{10... | collective-permute-start | bytes 442376 | tf_op jit(solution)/shard_map/ppermute | solution.py:34
  110.6 5.8 %collective-permute-done.20 = bf16[96,384]{1,0:T(8,128)(2,1)S(1)} collective-permute-done((bf16[96,384]{1,0:T(8,128)(2,1)S(1)}, bf16[96,384]{1,0:T(8,128)(2,1)S(1)}, u32[]{:S(2)}, u32[]{:S(2)}) %collective-permute-start.20) | collective-permute-done | bytes 73760 | tf_op jit(solution)/shard_map/ppermute | solution.py:34
  116.4 2.2 %collective-permute-done.19 = bf16[96,768]{1,0:T(8,128)(2,1)S(1)} collective-permute-done((bf16[96,768]{1,0:T(8,128)(2,1)S(1)}, bf16[96,768]{1,0:T(8,128)(2,1)S(1)}, u32[]{:S(2)}, u32[]{:S(2)}) %collective-permute-start.19) | collective-permute-done | bytes 147488 | tf_op jit(solution)/shard_map/ppermute | solution.py:34
  (139 shorter events, 29.5 us)
Async XLA Ops:
  0.6 10.3 %copy-start = (f32[6,225]{1,0:T(8,128)S(1)}, f32[6,225]{1,0:T(8,128)}, u32[]{:S(2)}) copy-start(f32[6,225]{1,0:T(8,128)} %param.16) | copy-start | bytes 16204
  0.6 9.2 %copy-start.31 = (s32[20]{0:T(128)S(1)}, s32[20]{0:T(128)}, u32[]{:S(2)}) copy-start(s32[20]{0:T(128)} %param.10) | copy-start | bytes 244
  0.7 9.9 %copy-start.32 = (f32[6]{0:T(128)S(1)}, f32[6]{0:T(128)}, u32[]{:S(2)}) copy-start(f32[6]{0:T(128)} %param.15) | copy-start | bytes 76
  1.7 14.7 %collective-permute-start = (bf16[2,64,1120]{2,1,0:T(8,128)(2,1)S(1)}, bf16[2,64,1120]{2,1,0:T(8,128)(2,1)S(1)}, u32[]{:S(2)}, u32[]{:S(2)}) collective-permute-start(bf16[2,64,1120]{2,1,0:T(8,128)(2,1)S(1)} %bitcast.142), channel_id=1, source_target_pairs={{0,24},{8,0},{16,8},{24,16},{1,25},{9,1},{17,9},{25,17},{2,26},{10... | collective-permute-start | bytes 860168 | tf_op jit(solution)/shard_map/ppermute | solution.py:29
  6.8 13.7 %collective-permute-start.1 = (bf16[160,1120]{1,0:T(8,128)(2,1)}, bf16[160,1120]{1,0:T(8,128)(2,1)S(1)}, u32[]{:S(2)}, u32[]{:S(2)}) collective-permute-start(bf16[160,1120]{1,0:T(8,128)(2,1)} %bitcast.148), channel_id=1, source_target_pairs={{0,1},{1,0},{2,3},{3,2},{4,5},{5,4},{6,7},{7,6},{8,9},{9,8},{10,11... | collective-permute-start | bytes 1075208 | tf_op jit(solution)/shard_map/ppermute | solution.py:34
  9.4 13.2 %collective-permute-start.2 = (bf16[3,64,1120]{2,1,0:T(8,128)(2,1)S(1)}, bf16[3,64,1120]{2,1,0:T(8,128)(2,1)S(1)}, u32[]{:S(2)}, u32[]{:S(2)}) collective-permute-start(bf16[3,64,1120]{2,1,0:T(8,128)(2,1)S(1)} %bitcast.138), channel_id=1, source_target_pairs={{0,24},{8,0},{16,8},{24,16},{1,25},{9,1},{17,9},{25,17},{2,26},{10... | collective-permute-start | bytes 1290248 | tf_op jit(solution)/shard_map/ppermute | solution.py:29
  19.9 12.2 %collective-permute-start.6 = (f16[128,1536]{1,0:T(8,128)(2,1)S(1)}, f16[128,1536]{1,0:T(8,128)(2,1)S(1)}, u32[]{:S(2)}, u32[]{:S(2)}) collective-permute-start(f16[128,1536]{1,0:T(8,128)(2,1)S(1)} %convert_element_type.346), channel_id=1, source_target_pairs={{0,1},{1,0},{2,3},{3,2},{4,5},{5,4},{6,7},{7,6},{8,9},{9,8},{10,11... | collective-permute-start | bytes 1179656 | tf_op jit(solution)/shard_map/ppermute | solution.py:34
  26.2 17.0 %collective-permute-start.4 = (f16[192,1536]{1,0:T(8,128)(2,1)S(1)}, f16[192,1536]{1,0:T(8,128)(2,1)S(1)}, u32[]{:S(2)}, u32[]{:S(2)}) collective-permute-start(f16[192,1536]{1,0:T(8,128)(2,1)S(1)} %convert_element_type.347), channel_id=1, source_target_pairs={{0,1},{1,0},{2,3},{3,2},{4,5},{5,4},{6,7},{7,6},{8,9},{9,8},{10,11... | collective-permute-start | bytes 1769480 | tf_op jit(solution)/shard_map/ppermute | solution.py:34
  27.8 13.6 %collective-permute-start.3 = (bf16[5,64,768]{2,1,0:T(8,128)(2,1)S(1)}, bf16[5,64,768]{2,1,0:T(8,128)(2,1)S(1)}, u32[]{:S(2)}, u32[]{:S(2)}) collective-permute-start(bf16[5,64,768]{2,1,0:T(8,128)(2,1)S(1)} %bitcast.146), channel_id=1, source_target_pairs={{0,24},{8,0},{16,8},{24,16},{1,25},{9,1},{17,9},{25,17},{2,26},{10... | collective-permute-start | bytes 1474568 | tf_op jit(solution)/shard_map/ppermute | solution.py:29
  32.2 11.7 %copy-start.5 = (bf16[128,1536]{1,0:T(8,128)(2,1)}, bf16[128,1536]{1,0:T(8,128)(2,1)S(1)}, u32[]{:S(2)}) copy-start(bf16[128,1536]{1,0:T(8,128)(2,1)S(1)} %multiply_convert_fusion.1.rolled.refs_0_) | copy-start | bytes 1179652
  34.7 8.4 %copy-start.12 = (bf16[128,384]{1,0:T(8,128)(2,1)}, bf16[128,384]{1,0:T(8,128)(2,1)S(1)}, u32[]{:S(2)}) copy-start(bf16[128,384]{1,0:T(8,128)(2,1)S(1)} %get-tuple-element.51.refs_0_) | copy-start | bytes 294916
  34.7 8.4 %copy-start.21 = (bf16[128,1152]{1,0:T(8,128)(2,1)}, bf16[128,1152]{1,0:T(8,128)(2,1)S(1)}, u32[]{:S(2)}) copy-start(bf16[128,1152]{1,0:T(8,128)(2,1)S(1)} %get-tuple-element.59.refs_0_) | copy-start | bytes 884740
  34.7 8.4 %copy-start.23 = (f32[2,3,64,128]{3,2,1,0:T(8,128)}, f32[2,3,64,128]{3,2,1,0:T(8,128)S(1)}, u32[]{:S(2)}) copy-start(f32[2,3,64,128]{3,2,1,0:T(8,128)S(1)} %get-tuple-element.61.refs_2_) | copy-start | bytes 589828
  43.2 12.0 %collective-permute-start.5 = (bf16[320,768]{1,0:T(8,128)(2,1)}, bf16[320,768]{1,0:T(8,128)(2,1)}, u32[]{:S(2)}, u32[]{:S(2)}) collective-permute-start(bf16[320,768]{1,0:T(8,128)(2,1)} %bitcast.11.own_up), channel_id=1, source_target_pairs={{0,1},{1,0},{2,3},{3,2},{4,5},{5,4},{6,7},{7,6},{8,9},{9,8},{10,11... | collective-permute-start | bytes 1474568 | tf_op jit(solution)/shard_map/ppermute | solution.py:34
  57.8 15.5 %copy-start.28 = (bf16[2,1,384,384]{3,2,1,0:T(8,128)(2,1)}, bf16[2,1,384,384]{3,2,1,0:T(8,128)(2,1)S(1)}, u32[]{:S(2)}) copy-start(bf16[2,1,384,384]{3,2,1,0:T(8,128)(2,1)S(1)} %get-tuple-element.95) | copy-start | bytes 1769476
  57.8 15.5 %collective-permute-start.9 = (bf16[8,96,384]{2,1,0:T(8,128)(2,1)S(1)}, bf16[8,96,384]{2,1,0:T(8,128)(2,1)S(1)}, u32[]{:S(2)}, u32[]{:S(2)}) collective-permute-start(bf16[8,96,384]{2,1,0:T(8,128)(2,1)S(1)} %bitcast.168), channel_id=1, source_target_pairs={{0,8},{8,0},{16,24},{24,16},{1,9},{9,1},{17,25},{25,17},{2,10},{10... | collective-permute-start | bytes 1769480 | tf_op jit(solution)/shard_map/ppermute | solution.py:34
  58.8 11.0 %collective-permute-start.7 = (bf16[320,768]{1,0:T(8,128)(2,1)S(1)}, bf16[320,768]{1,0:T(8,128)(2,1)S(1)}, u32[]{:S(2)}, u32[]{:S(2)}) collective-permute-start(bf16[320,768]{1,0:T(8,128)(2,1)S(1)} %get-tuple-element.67), channel_id=1, source_target_pairs={{0,1},{1,0},{2,3},{3,2},{4,5},{5,4},{6,7},{7,6},{8,9},{9,8},{10,11... | collective-permute-start | bytes 1474568 | tf_op jit(solution)/shard_map/ppermute | solution.py:34
  60.3 9.4 %copy-start.17 = (bf16[768,1120]{0,1:T(8,128)(2,1)S(1)}, bf16[768,1120]{0,1:T(8,128)(2,1)}, u32[]{:S(2)}) copy-start(bf16[768,1120]{0,1:T(8,128)(2,1)} %param.14) | copy-start | bytes 5160964
  69.8 6.2 %collective-permute-start.10 = (bf16[8,96,384]{2,1,0:T(8,128)(2,1)}, bf16[8,96,384]{2,1,0:T(8,128)(2,1)}, u32[]{:S(2)}, u32[]{:S(2)}) collective-permute-start(bf16[8,96,384]{2,1,0:T(8,128)(2,1)} %bitcast.18), channel_id=1, source_target_pairs={{0,2},{2,0},{4,6},{6,4},{1,3},{3,1},{5,7},{7,5},{8,10},{10,8},{12,... | collective-permute-start | bytes 1769480 | tf_op jit(solution)/shard_map/ppermute | solution.py:34
  74.1 6.7 %collective-permute-start.11 = (bf16[8,96,768]{2,1,0:T(8,128)(2,1)}, bf16[8,96,768]{2,1,0:T(8,128)(2,1)}, u32[]{:S(2)}, u32[]{:S(2)}) collective-permute-start(bf16[8,96,768]{2,1,0:T(8,128)(2,1)} %bitcast.19), channel_id=1, source_target_pairs={{0,2},{2,0},{4,6},{6,4},{1,3},{3,1},{5,7},{7,5},{8,10},{10,8},{12,... | collective-permute-start | bytes 3538952 | tf_op jit(solution)/shard_map/ppermute | solution.py:34
  74.6 10.5 %collective-permute-start.8 = (bf16[160,1120]{1,0:T(8,128)(2,1)S(1)}, bf16[160,1120]{1,0:T(8,128)(2,1)S(1)}, u32[]{:S(2)}, u32[]{:S(2)}) collective-permute-start(bf16[160,1120]{1,0:T(8,128)(2,1)S(1)} %get-tuple-element.69), channel_id=1, source_target_pairs={{0,1},{1,0},{2,3},{3,2},{4,5},{5,4},{6,7},{7,6},{8,9},{9,8},{10,11... | collective-permute-start | bytes 1075208 | tf_op jit(solution)/shard_map/ppermute | solution.py:34
  75.3 11.0 %collective-permute-start.13 = (bf16[2,2,96,384]{3,2,1,0:T(8,128)(2,1)S(1)}, bf16[2,2,96,384]{3,2,1,0:T(8,128)(2,1)S(1)}, u32[]{:S(2)}, u32[]{:S(2)}) collective-permute-start(bf16[2,2,96,384]{3,2,1,0:T(8,128)(2,1)S(1)} %fusion.12), channel_id=1, source_target_pairs={{0,2},{2,0},{4,6},{6,4},{1,3},{3,1},{5,7},{7,5},{8,10},{10,8},{12,... | collective-permute-start | bytes 884744 | tf_op jit(solution)/shard_map/ppermute | solution.py:34
  77.1 22.6 %collective-permute-start.15 = (bf16[2,2,96,384]{3,2,0,1:T(8,128)(2,1)S(1)}, bf16[2,2,96,384]{3,2,0,1:T(8,128)(2,1)S(1)}, u32[]{:S(2)}, u32[]{:S(2)}) collective-permute-start(bf16[2,2,96,384]{3,2,0,1:T(8,128)(2,1)S(1)} %fusion.13), channel_id=1, source_target_pairs={{0,8},{8,0},{16,24},{24,16},{1,9},{9,1},{17,25},{25,17},{2,10},{10... | collective-permute-start | bytes 884744 | tf_op jit(solution)/shard_map/ppermute | solution.py:34
  82.0 16.2 %collective-permute-start.16 = (bf16[2,2,96,768]{3,2,0,1:T(8,128)(2,1)S(1)}, bf16[2,2,96,768]{3,2,0,1:T(8,128)(2,1)S(1)}, u32[]{:S(2)}, u32[]{:S(2)}) collective-permute-start(bf16[2,2,96,768]{3,2,0,1:T(8,128)(2,1)S(1)} %fusion.9), channel_id=1, source_target_pairs={{0,4},{2,6},{4,0},{6,2},{1,5},{3,7},{5,1},{7,3},{8,12},{10,14},{12... | collective-permute-start | bytes 1769480 | tf_op jit(solution)/shard_map/ppermute | solution.py:34
  85.2 19.8 %collective-permute-start.12 = (bf16[5,32,1120]{2,1,0:T(8,128)(2,1)S(1)}, bf16[5,32,1120]{2,1,0:T(8,128)(2,1)S(1)}, u32[]{:S(2)}, u32[]{:S(2)}) collective-permute-start(bf16[5,32,1120]{2,1,0:T(8,128)(2,1)S(1)} %bitcast.140), channel_id=1, source_target_pairs={{0,8},{8,16},{16,24},{24,0},{1,9},{9,17},{17,25},{25,1},{2,10},{10... | collective-permute-start | bytes 1075208 | tf_op jit(solution)/shard_map/ppermute | solution.py:29
  87.6 17.4 %copy-start.25 = (s32[5]{0:T(128)S(1)}, s32[5]{0:T(128)}, u32[]{:S(2)}) copy-start(s32[5]{0:T(128)} %and_select_fusion.1.shifts) | copy-start | bytes 64
  87.6 13.7 %collective-permute-start.14 = (bf16[2,96,384]{2,1,0:T(8,128)(2,1)S(1)}, bf16[2,96,384]{2,1,0:T(8,128)(2,1)S(1)}, u32[]{:S(2)}, u32[]{:S(2)}) collective-permute-start(bf16[2,96,384]{2,1,0:T(8,128)(2,1)S(1)} %fusion.21), channel_id=1, source_target_pairs={{0,4},{2,6},{4,0},{6,2},{1,5},{3,7},{5,1},{7,3},{8,12},{10,14},{12... | collective-permute-start | bytes 442376 | tf_op jit(solution)/shard_map/ppermute | solution.py:34
  98.3 10.3 %collective-permute-start.17 = (bf16[2,96,768]{2,1,0:T(8,128)(2,1)S(1)}, bf16[2,96,768]{2,1,0:T(8,128)(2,1)S(1)}, u32[]{:S(2)}, u32[]{:S(2)}) collective-permute-start(bf16[2,96,768]{2,1,0:T(8,128)(2,1)S(1)} %get-tuple-element.94), channel_id=1, source_target_pairs={{0,8},{8,0},{16,24},{24,16},{1,9},{9,1},{17,25},{25,17},{2,10},{10... | collective-permute-start | bytes 884744 | tf_op jit(solution)/shard_map/ppermute | solution.py:34
  99.8 6.8 %collective-permute-start.18 = (bf16[2,96,384]{2,1,0:T(8,128)(2,1)S(1)}, bf16[2,96,384]{2,1,0:T(8,128)(2,1)S(1)}, u32[]{:S(2)}, u32[]{:S(2)}) collective-permute-start(bf16[2,96,384]{2,1,0:T(8,128)(2,1)S(1)} %get-tuple-element.100), channel_id=1, source_target_pairs={{0,4},{2,6},{4,0},{6,2},{1,5},{3,7},{5,1},{7,3},{8,12},{10,14},{12... | collective-permute-start | bytes 442376 | tf_op jit(solution)/shard_map/ppermute | solution.py:34
  101.4 8.5 %collective-permute-start.21 = (bf16[96,384]{1,0:T(8,128)(2,1)S(1)}, bf16[96,384]{1,0:T(8,128)(2,1)S(1)}, u32[]{:S(2)}, u32[]{:S(2)}) collective-permute-start(bf16[96,384]{1,0:T(8,128)(2,1)S(1)} %fusion.30), channel_id=1, source_target_pairs={{0,16},{8,24},{16,0},{24,8},{1,17},{9,25},{17,1},{25,9},{2,18},{10... | collective-permute-start | bytes 221192 | tf_op jit(solution)/shard_map/ppermute | solution.py:34
  106.6 9.8 %collective-permute-start.20 = (bf16[96,384]{1,0:T(8,128)(2,1)S(1)}, bf16[96,384]{1,0:T(8,128)(2,1)S(1)}, u32[]{:S(2)}, u32[]{:S(2)}) collective-permute-start(bf16[96,384]{1,0:T(8,128)(2,1)S(1)} %fusion.31), channel_id=1, source_target_pairs={{0,16},{8,24},{16,0},{24,8},{1,17},{9,25},{17,1},{25,9},{2,18},{10... | collective-permute-start | bytes 221192 | tf_op jit(solution)/shard_map/ppermute | solution.py:34
  108.7 10.0 %collective-permute-start.19 = (bf16[96,768]{1,0:T(8,128)(2,1)S(1)}, bf16[96,768]{1,0:T(8,128)(2,1)S(1)}, u32[]{:S(2)}, u32[]{:S(2)}) collective-permute-start(bf16[96,768]{1,0:T(8,128)(2,1)S(1)} %fusion.24), channel_id=1, source_target_pairs={{0,16},{8,24},{16,0},{24,8},{1,17},{9,25},{17,1},{25,9},{2,18},{10... | collective-permute-start | bytes 442376 | tf_op jit(solution)/shard_map/ppermute | solution.py:34
  (23 other events, 57.7 us)

commit v4 on v3

--- a/solution.py
+++ b/solution.py
@@ -19,7 +19,7 @@
 F32 = jnp.float32
 F16 = jnp.float16
 TERM_SCALE = 64.0
-VMEM_LIMIT = 30 * 1024 * 1024
+VMEM_LIMIT = 38 * 1024 * 1024
 SMALL_LIMIT = 24 * 1024 * 1024
 
 

time: 120 us -> 120 us (level)
  no operation moved by 1% of the time
where the time goes in v4:
time: 120 us
  starting transfers between devices  32.9 us (27%)
  waiting for transfers between devices  26.2 us (22%)
  Pallas kernels  24 us (20%)
  local copies, waits for them, and re-layouts  16.3 us (14%)
  matrix products  10.1 us (8%)
  other arithmetic  9.04 us (8%)
    ppermute x18, starting transfers between devices, swapped(): lax.ppermute(value, axis, [(source, source ^ bit) for source in range(cou...  21.9 us
    ppermute x18, waiting for transfers between devices, swapped(): lax.ppermute(value, axis, [(source, source ^ bit) for source in range(cou...  18.7 us
    ppermute x4, starting transfers between devices, moved(): return lax.ppermute(value, axis, pairs)  11 us
    unnamed x66, local copies, waits for them, and re-layouts  8.21 us
    pallas_call x1, Pallas kernels, backward_call(): call(functools.partial(backward_kernel, len(qkv)), (shape((rows, 2 * widt...  8.06 us
    ppermute x4, waiting for transfers between devices, moved(): return lax.ppermute(value, axis, pairs)  7.48 us
    dot_general x5, matrix products, dot(): lax.dot_general(a, b, (((ca,), (cb,)), ((), ())), preferred_element_type=...  6.86 us
    pallas_call x2, Pallas kernels, forward_call(): call(forward_kernel, out_shape, 'vvvv', 0.05)(rolled, w_qkv, scales, biases)  6.17 us
  transfers between devices with their start and end apart: 22, of which 6 were waited for; matrix products, arithmetic and copies ran while one was open for 19% of the time, Pallas kernels for 20%

profile of v4, /device:TPU:0, one launch (start us, length us, event | category | flops | bytes accessed | tf_op | source)
XLA Modules:
  0.0 119.6 jit_solution(14962446603358524603)
XLA Ops:
  1.7 5.1 %collective-permute-start = (bf16[2,64,1120]{2,1,0:T(8,128)(2,1)S(1)}, bf16[2,64,1120]{2,1,0:T(8,128)(2,1)S(1)}, u32[]{:S(2)}, u32[]{:S(2)}) collective-permute-start(bf16[2,64,1120]{2,1,0:T(8,128)(2,1)S(1)} %bitcast.142), channel_id=1, source_target_pairs={{0,24},{8,0},{16,8},{24,16},{1,25},{9,1},{17,9},{25,17},{2,26},{10... | collective-permute-start | bytes 860168 | tf_op jit(solution)/shard_map/ppermute | solution.py:29
  6.8 1.5 %collective-permute-start.1 = (bf16[160,1120]{1,0:T(8,128)(2,1)}, bf16[160,1120]{1,0:T(8,128)(2,1)S(1)}, u32[]{:S(2)}, u32[]{:S(2)}) collective-permute-start(bf16[160,1120]{1,0:T(8,128)(2,1)} %bitcast.148), channel_id=1, source_target_pairs={{0,1},{1,0},{2,3},{3,2},{4,5},{5,4},{6,7},{7,6},{8,9},{9,8},{10,11... | collective-permute-start | bytes 1075208 | tf_op jit(solution)/shard_map/ppermute | solution.py:34
  10.9 3.2 %fusion.2 = f32[6,64,64]{1,0,2:T(8,128)S(1)} fusion(s32[64,64]{1,0:T(8,128)S(1)} %add_add_fusion, f32[6,225]{1,0:T(8,128)S(1)} %copy-done), kind=kOutput, calls=%fused_computation.12 | convolution fusion | flops 67276800 | bytes 120088 | tf_op jit(solution)/shard_map/ije,he->hji/dot_general | solution.py:418
  16.4 2.0 %copy-done.14 = bf16[1120,1536]{1,0:T(8,128)(2,1)S(1)} copy-done((bf16[1120,1536]{1,0:T(8,128)(2,1)S(1)}, bf16[1120,1536]{1,0:T(8,128)(2,1)}, u32[]{:S(2)}) %copy-start.14) | copy-done | bytes 3440664
  18.4 1.5 %shard_map.112 = f32[128,1536]{1,0:T(8,128)S(1)} custom-call(s32[2]{0:T(128)S(1)} %bitcast.135, bf16[2,64,1120]{2,1,0:T(8,128)(2,1)S(1)} %bitcast.143, bf16[2,64,1120]{2,1,0:T(8,128)(2,1)S(1)} %collective-permute-done.other, bf16[1120,1536]{1,0:T(8,128)(2,1)S(1)} %copy-done.14), custom_call_target="tpu_custom_call" | custom-call | flops 5000000000 | bytes 1 | tf_op jit(solution)/shard_map/pallas_call | solution.py:98
  24.3 1.8 %shard_map.114 = f32[192,1536]{1,0:T(8,128)S(1)} custom-call(s32[3]{0:T(128)S(1)} %copy-done.26, bf16[3,64,1120]{2,1,0:T(8,128)(2,1)S(1)} %bitcast.139, bf16[3,64,1120]{2,1,0:T(8,128)(2,1)S(1)} %copy-done.19, bf16[1120,1536]{1,0:T(8,128)(2,1)S(1)} %copy-done.15), custom_call_target="tpu_custom_call" | custom-call | flops 5000000000 | bytes 1 | tf_op jit(solution)/shard_map/pallas_call | solution.py:98
  26.2 1.6 %collective-permute-start.4 = (f16[192,1536]{1,0:T(8,128)(2,1)S(1)}, f16[192,1536]{1,0:T(8,128)(2,1)S(1)}, u32[]{:S(2)}, u32[]{:S(2)}) collective-permute-start(f16[192,1536]{1,0:T(8,128)(2,1)S(1)} %convert_element_type.347), channel_id=1, source_target_pairs={{0,1},{1,0},{2,3},{3,2},{4,5},{5,4},{6,7},{7,6},{8,9},{9,8},{10,11... | collective-permute-start | bytes 1769480 | tf_op jit(solution)/shard_map/ppermute | solution.py:34
  27.8 4.3 %collective-permute-start.3 = (bf16[5,64,768]{2,1,0:T(8,128)(2,1)S(1)}, bf16[5,64,768]{2,1,0:T(8,128)(2,1)S(1)}, u32[]{:S(2)}, u32[]{:S(2)}) collective-permute-start(bf16[5,64,768]{2,1,0:T(8,128)(2,1)S(1)} %bitcast.146), channel_id=1, source_target_pairs={{0,24},{8,0},{16,8},{24,16},{1,25},{9,1},{17,9},{25,17},{2,26},{10... | collective-permute-start | bytes 1474568 | tf_op jit(solution)/shard_map/ppermute | solution.py:29
  32.2 2.5 %shard_map.116 = (bf16[128,1152]{1,0:T(8,128)(2,1)S(1)}, f32[2,3,64,128]{3,2,1,0:T(8,128)S(1)}, bf16[128,384]{1,0:T(8,128)(2,1)S(1)}) custom-call(bf16[128,1536]{1,0:T(8,128)(2,1)S(1)} %multiply_convert_fusion.1.rolled.refs_0_, bf16[3,1536,384]{2,1,0:T(8,128)(2,1)S(1)} %bitcast.136, f32[3,1,128]{2,1,0:T(1,128)S(1)} %broadcast_in_dim.7.scales, ...), custom_call_target="tpu_custom_call" | custom-call | flops 50000000 | bytes 1 | tf_op jit(solution)/shard_map/pallas_call | solution.py:190
  34.8 6.6 %collective-permute-done.3.other = bf16[5,64,768]{2,1,0:T(8,128)(2,1)S(1)} collective-permute-done((bf16[5,64,768]{2,1,0:T(8,128)(2,1)S(1)}, bf16[5,64,768]{2,1,0:T(8,128)(2,1)S(1)}, u32[]{:S(2)}, u32[]{:S(2)}) %collective-permute-start.3) | collective-permute-done | bytes 491552 | tf_op jit(solution)/shard_map/ppermute | solution.py:29
  41.4 1.7 %shard_map.115 = bf16[5,64,768]{2,1,0:T(8,128)(2,1)} custom-call(s32[5]{0:T(128)S(1)} %dynamic_slice.132.shifts, bf16[5,64,768]{2,1,0:T(8,128)(2,1)S(1)} %bitcast.147, bf16[5,64,768]{2,1,0:T(8,128)(2,1)S(1)} %collective-permute-done.3.other), custom_call_target="tpu_custom_call" | custom-call | flops 2000000000 | bytes 1 | tf_op jit(solution)/shard_map/pallas_call | solution.py:84
  45.8 2.3 %copy.42 = bf16[320,1536]{0,1:T(8,128)(2,1)} copy(bf16[320,1536]{1,0:T(8,128)(2,1)} %pad_maximum_fusion) | data formatting | bytes 1966080 | tf_op jit(solution)/shard_map/concatenate | solution.py:443
  50.1 3.7 %shard_map.117 = (bf16[192,1152]{1,0:T(8,128)(2,1)S(1)}, f32[3,3,64,128]{3,2,1,0:T(8,128)S(1)}, bf16[192,384]{1,0:T(8,128)(2,1)S(1)}) custom-call(bf16[192,1536]{1,0:T(8,128)(2,1)S(1)} %copy-done.3, bf16[3,1536,384]{2,1,0:T(8,128)(2,1)S(1)} %bitcast.137, f32[3,1,128]{2,1,0:T(1,128)S(1)} %broadcast_in_dim.7.scales, f32[3,64,128]{2,1,0:T(8,128)S(1)} %copy-done.9), custom_call_target="tpu_custom_call" | custom-call | flops 50000000 | bytes 1 | tf_op jit(solution)/shard_map/pallas_call | solution.py:190
  55.2 2.4 %convolution_convert_fusion = bf16[1536,384]{1,0:T(8,128)(2,1)S(1)} fusion(bf16[320,384]{1,0:T(8,128)(2,1)S(1)} %pad_maximum_fusion.2, bf16[320,768]{1,0:T(8,128)(2,1)} %collective-permute-done.5.other_up, bf16[320,768]{1,0:T(8,128)(2,1)} %bitcast.11.own_up, pred[]{:T(512)S(6)} %eq.33), kind=kOutput, calls=%fused_computation.3 | convolution fusion | flops 382500864 | bytes 2408449 | tf_op jit(solution)/shard_map/dot_general | solution.py:62
  58.8 1.5 %collective-permute-start.7 = (bf16[320,768]{1,0:T(8,128)(2,1)S(1)}, bf16[320,768]{1,0:T(8,128)(2,1)S(1)}, u32[]{:S(2)}, u32[]{:S(2)}) collective-permute-start(bf16[320,768]{1,0:T(8,128)(2,1)S(1)} %get-tuple-element.67), channel_id=1, source_target_pairs={{0,1},{1,0},{2,3},{3,2},{4,5},{5,4},{6,7},{7,6},{8,9},{9,8},{10,11... | collective-permute-start | bytes 1474568 | tf_op jit(solution)/shard_map/ppermute | solution.py:34
  60.3 8.1 %shard_map.119 = (bf16[320,768]{1,0:T(8,128)(2,1)S(1)}, bf16[320,384]{1,0:T(8,128)(2,1)S(1)}) custom-call(s32[1]{0:T(128)} %bitcast.6.place, bf16[320,768]{1,0:T(8,128)(2,1)} %bitcast.11.own_up, bf16[320,768]{1,0:T(8,128)(2,1)} %collective-permute-done.5.other_up, bf16[384,1536]{1,0:T(8,128)(2,1)S(1)} %copy-done.7, f32[3,1,128]{2,1,0:T(1,128)S(1)} %broadcast_in_dim.7.scales, ...), custom_call_target="tpu_custom_call" | custom-call | flops 8999999488 | bytes 1 | tf_op jit(solution)/shard_map/pallas_call | solution.py:242
  68.4 1.3 %convolution_convert_fusion.4 = bf16[768,384]{1,0:T(8,128)(2,1)} fusion(bf16[320,768]{0,1:T(8,128)(2,1)S(1)} %bitcast.152, bf16[320,384]{1,0:T(8,128)(2,1)S(1)} %get-tuple-element.74), kind=kOutput, calls=%fused_computation.8 | convolution fusion | flops 189038592 | bytes 1327104 | tf_op jit(solution)/shard_map/dot_general | solution.py:62
  69.8 1.6 %shard_map.120 = (bf16[160,1120]{1,0:T(8,128)(2,1)S(1)}, bf16[160,1120]{1,0:T(8,128)(2,1)S(1)}) custom-call(s32[1]{0:T(128)} %bitcast.6.place, bf16[320,768]{1,0:T(8,128)(2,1)S(1)} %get-tuple-element.65.mine, bf16[320,768]{1,0:T(8,128)(2,1)S(1)} %collective-permute-done.7.theirs, bf16[1120,768]{1,0:T(8,128)(2,1)S(1)} %bitcast.145, ...), custom_call_target="tpu_custom_call" | custom-call | flops 4000000000 | bytes 1 | tf_op jit(solution)/shard_map/pallas_call | solution.py:314
  71.4 1.8 %convolution_convert_fusion.2 = bf16[768,768]{1,0:T(8,128)(2,1)} fusion(bf16[320,768]{0,1:T(8,128)(2,1)S(1)} %bitcast.153, bf16[320,768]{1,0:T(8,128)(2,1)S(1)} %get-tuple-element.75), kind=kOutput, calls=%fused_computation.6 | convolution fusion | flops 378077184 | bytes 2162688 | tf_op jit(solution)/shard_map/dot_general | solution.py:62
  80.7 1.2 %fusion.9 = bf16[2,2,96,768]{3,2,0,1:T(8,128)(2,1)S(1)} fusion(bf16[2,2,2,96,768]{4,3,2,1,0:T(8,128)(2,1)S(1)} %bitcast.154, s32[]{:T(128)S(6)} %select_n.205, bf16[2,2,2,96,768]{4,3,2,1,0:T(8,128)(2,1)} %bitcast.27), kind=kLoop, calls=%fused_computation.23 | loop fusion | flops 1179648 | bytes 1770496 | tf_op jit(solution)/shard_map/convert_element_type | solution.py:368
  82.0 1.5 %collective-permute-start.16 = (bf16[2,2,96,768]{3,2,0,1:T(8,128)(2,1)S(1)}, bf16[2,2,96,768]{3,2,0,1:T(8,128)(2,1)S(1)}, u32[]{:S(2)}, u32[]{:S(2)}) collective-permute-start(bf16[2,2,96,768]{3,2,0,1:T(8,128)(2,1)S(1)} %fusion.9), channel_id=1, source_target_pairs={{0,4},{2,6},{4,0},{6,2},{1,5},{3,7},{5,1},{7,3},{8,12},{10,14},{12... | collective-permute-start | bytes 1769480 | tf_op jit(solution)/shard_map/ppermute | solution.py:34
  83.5 1.6 %collective-permute-done.8 = bf16[160,1120]{1,0:T(8,128)(2,1)S(1)} collective-permute-done((bf16[160,1120]{1,0:T(8,128)(2,1)S(1)}, bf16[160,1120]{1,0:T(8,128)(2,1)S(1)}, u32[]{:S(2)}, u32[]{:S(2)}) %collective-permute-start.8) | collective-permute-done | bytes 358432 | tf_op jit(solution)/shard_map/ppermute | solution.py:34
  86.3 1.2 %add_convert_fusion = bf16[2,2,1,96,768]{4,3,2,1,0:T(8,128)(2,1)S(1)} fusion(bf16[2,2,2,96,768]{4,3,2,1,0:T(8,128)(2,1)} %bitcast.27, s32[]{:T(128)S(6)} %select_n.206, bf16[2,2,2,96,768]{4,3,2,1,0:T(8,128)(2,1)S(1)} %bitcast.155), kind=kLoop, calls=%fused_computation.9 | loop fusion | flops 1179648 | bytes 1769476 | tf_op jit(solution)/shard_map/convert_element_type | solution.py:368
  87.7 1.6 %collective-permute-start.14 = (bf16[2,96,384]{2,1,0:T(8,128)(2,1)S(1)}, bf16[2,96,384]{2,1,0:T(8,128)(2,1)S(1)}, u32[]{:S(2)}, u32[]{:S(2)}) collective-permute-start(bf16[2,96,384]{2,1,0:T(8,128)(2,1)S(1)} %fusion.21), channel_id=1, source_target_pairs={{0,4},{2,6},{4,0},{6,2},{1,5},{3,7},{5,1},{7,3},{8,12},{10,14},{12... | collective-permute-start | bytes 442376 | tf_op jit(solution)/shard_map/ppermute | solution.py:34
  89.2 9.0 %collective-permute-done.16 = bf16[2,2,96,768]{3,2,0,1:T(8,128)(2,1)S(1)} collective-permute-done((bf16[2,2,96,768]{3,2,0,1:T(8,128)(2,1)S(1)}, bf16[2,2,96,768]{3,2,0,1:T(8,128)(2,1)S(1)}, u32[]{:S(2)}, u32[]{:S(2)}) %collective-permute-start.16) | collective-permute-done | bytes 589856 | tf_op jit(solution)/shard_map/ppermute | solution.py:34
  98.3 1.4 %collective-permute-start.17 = (bf16[2,96,768]{2,1,0:T(8,128)(2,1)S(1)}, bf16[2,96,768]{2,1,0:T(8,128)(2,1)S(1)}, u32[]{:S(2)}, u32[]{:S(2)}) collective-permute-start(bf16[2,96,768]{2,1,0:T(8,128)(2,1)S(1)} %get-tuple-element.94), channel_id=1, source_target_pairs={{0,8},{8,0},{16,24},{24,16},{1,9},{9,1},{17,25},{25,17},{2,10},{10... | collective-permute-start | bytes 884744 | tf_op jit(solution)/shard_map/ppermute | solution.py:34
  99.8 1.6 %collective-permute-start.18 = (bf16[2,96,384]{2,1,0:T(8,128)(2,1)S(1)}, bf16[2,96,384]{2,1,0:T(8,128)(2,1)S(1)}, u32[]{:S(2)}, u32[]{:S(2)}) collective-permute-start(bf16[2,96,384]{2,1,0:T(8,128)(2,1)S(1)} %get-tuple-element.100), channel_id=1, source_target_pairs={{0,4},{2,6},{4,0},{6,2},{1,5},{3,7},{5,1},{7,3},{8,12},{10,14},{12... | collective-permute-start | bytes 442376 | tf_op jit(solution)/shard_map/ppermute | solution.py:34
  101.4 3.6 %collective-permute-start.21 = (bf16[96,384]{1,0:T(8,128)(2,1)S(1)}, bf16[96,384]{1,0:T(8,128)(2,1)S(1)}, u32[]{:S(2)}, u32[]{:S(2)}) collective-permute-start(bf16[96,384]{1,0:T(8,128)(2,1)S(1)} %fusion.30), channel_id=1, source_target_pairs={{0,16},{8,24},{16,0},{24,8},{1,17},{9,25},{17,1},{25,9},{2,18},{10... | collective-permute-start | bytes 221192 | tf_op jit(solution)/shard_map/ppermute | solution.py:34
  105.0 1.6 %shard_map.121 = bf16[5,32,1120]{2,1,0:T(8,128)(2,1)} custom-call(s32[5]{0:T(128)S(1)} %copy-done.25, bf16[5,32,1120]{2,1,0:T(8,128)(2,1)S(1)} %bitcast.141, bf16[5,32,1120]{2,1,0:T(8,128)(2,1)S(1)} %collective-permute-done.12.other), custom_call_target="tpu_custom_call" | custom-call | flops 2000000000 | bytes 1 | tf_op jit(solution)/shard_map/pallas_call | solution.py:84
  106.7 2.0 %collective-permute-start.20 = (bf16[96,384]{1,0:T(8,128)(2,1)S(1)}, bf16[96,384]{1,0:T(8,128)(2,1)S(1)}, u32[]{:S(2)}, u32[]{:S(2)}) collective-permute-start(bf16[96,384]{1,0:T(8,128)(2,1)S(1)} %fusion.31), channel_id=1, source_target_pairs={{0,16},{8,24},{16,0},{24,8},{1,17},{9,25},{17,1},{25,9},{2,18},{10... | collective-permute-start | bytes 221192 | tf_op jit(solution)/shard_map/ppermute | solution.py:34
  110.6 5.8 %collective-permute-done.20 = bf16[96,384]{1,0:T(8,128)(2,1)S(1)} collective-permute-done((bf16[96,384]{1,0:T(8,128)(2,1)S(1)}, bf16[96,384]{1,0:T(8,128)(2,1)S(1)}, u32[]{:S(2)}, u32[]{:S(2)}) %collective-permute-start.20) | collective-permute-done | bytes 73760 | tf_op jit(solution)/shard_map/ppermute | solution.py:34
  116.5 2.2 %collective-permute-done.19 = bf16[96,768]{1,0:T(8,128)(2,1)S(1)} collective-permute-done((bf16[96,768]{1,0:T(8,128)(2,1)S(1)}, bf16[96,768]{1,0:T(8,128)(2,1)S(1)}, u32[]{:S(2)}, u32[]{:S(2)}) %collective-permute-start.19) | collective-permute-done | bytes 147488 | tf_op jit(solution)/shard_map/ppermute | solution.py:34
  (139 shorter events, 29.5 us)
Async XLA Ops:
  0.6 10.3 %copy-start = (f32[6,225]{1,0:T(8,128)S(1)}, f32[6,225]{1,0:T(8,128)}, u32[]{:S(2)}) copy-start(f32[6,225]{1,0:T(8,128)} %param.16) | copy-start | bytes 16204
  0.6 9.2 %copy-start.31 = (s32[20]{0:T(128)S(1)}, s32[20]{0:T(128)}, u32[]{:S(2)}) copy-start(s32[20]{0:T(128)} %param.10) | copy-start | bytes 244
  0.7 9.9 %copy-start.32 = (f32[6]{0:T(128)S(1)}, f32[6]{0:T(128)}, u32[]{:S(2)}) copy-start(f32[6]{0:T(128)} %param.15) | copy-start | bytes 76
  1.7 14.7 %collective-permute-start = (bf16[2,64,1120]{2,1,0:T(8,128)(2,1)S(1)}, bf16[2,64,1120]{2,1,0:T(8,128)(2,1)S(1)}, u32[]{:S(2)}, u32[]{:S(2)}) collective-permute-start(bf16[2,64,1120]{2,1,0:T(8,128)(2,1)S(1)} %bitcast.142), channel_id=1, source_target_pairs={{0,24},{8,0},{16,8},{24,16},{1,25},{9,1},{17,9},{25,17},{2,26},{10... | collective-permute-start | bytes 860168 | tf_op jit(solution)/shard_map/ppermute | solution.py:29
  6.8 13.7 %collective-permute-start.1 = (bf16[160,1120]{1,0:T(8,128)(2,1)}, bf16[160,1120]{1,0:T(8,128)(2,1)S(1)}, u32[]{:S(2)}, u32[]{:S(2)}) collective-permute-start(bf16[160,1120]{1,0:T(8,128)(2,1)} %bitcast.148), channel_id=1, source_target_pairs={{0,1},{1,0},{2,3},{3,2},{4,5},{5,4},{6,7},{7,6},{8,9},{9,8},{10,11... | collective-permute-start | bytes 1075208 | tf_op jit(solution)/shard_map/ppermute | solution.py:34
  9.4 13.2 %collective-permute-start.2 = (bf16[3,64,1120]{2,1,0:T(8,128)(2,1)S(1)}, bf16[3,64,1120]{2,1,0:T(8,128)(2,1)S(1)}, u32[]{:S(2)}, u32[]{:S(2)}) collective-permute-start(bf16[3,64,1120]{2,1,0:T(8,128)(2,1)S(1)} %bitcast.138), channel_id=1, source_target_pairs={{0,24},{8,0},{16,8},{24,16},{1,25},{9,1},{17,9},{25,17},{2,26},{10... | collective-permute-start | bytes 1290248 | tf_op jit(solution)/shard_map/ppermute | solution.py:29
  19.9 12.2 %collective-permute-start.6 = (f16[128,1536]{1,0:T(8,128)(2,1)S(1)}, f16[128,1536]{1,0:T(8,128)(2,1)S(1)}, u32[]{:S(2)}, u32[]{:S(2)}) collective-permute-start(f16[128,1536]{1,0:T(8,128)(2,1)S(1)} %convert_element_type.346), channel_id=1, source_target_pairs={{0,1},{1,0},{2,3},{3,2},{4,5},{5,4},{6,7},{7,6},{8,9},{9,8},{10,11... | collective-permute-start | bytes 1179656 | tf_op jit(solution)/shard_map/ppermute | solution.py:34
  26.2 17.0 %collective-permute-start.4 = (f16[192,1536]{1,0:T(8,128)(2,1)S(1)}, f16[192,1536]{1,0:T(8,128)(2,1)S(1)}, u32[]{:S(2)}, u32[]{:S(2)}) collective-permute-start(f16[192,1536]{1,0:T(8,128)(2,1)S(1)} %convert_element_type.347), channel_id=1, source_target_pairs={{0,1},{1,0},{2,3},{3,2},{4,5},{5,4},{6,7},{7,6},{8,9},{9,8},{10,11... | collective-permute-start | bytes 1769480 | tf_op jit(solution)/shard_map/ppermute | solution.py:34
  27.8 13.6 %collective-permute-start.3 = (bf16[5,64,768]{2,1,0:T(8,128)(2,1)S(1)}, bf16[5,64,768]{2,1,0:T(8,128)(2,1)S(1)}, u32[]{:S(2)}, u32[]{:S(2)}) collective-permute-start(bf16[5,64,768]{2,1,0:T(8,128)(2,1)S(1)} %bitcast.146), channel_id=1, source_target_pairs={{0,24},{8,0},{16,8},{24,16},{1,25},{9,1},{17,9},{25,17},{2,26},{10... | collective-permute-start | bytes 1474568 | tf_op jit(solution)/shard_map/ppermute | solution.py:29
  32.2 11.7 %copy-start.5 = (bf16[128,1536]{1,0:T(8,128)(2,1)}, bf16[128,1536]{1,0:T(8,128)(2,1)S(1)}, u32[]{:S(2)}) copy-start(bf16[128,1536]{1,0:T(8,128)(2,1)S(1)} %multiply_convert_fusion.1.rolled.refs_0_) | copy-start | bytes 1179652
  34.7 8.4 %copy-start.12 = (bf16[128,384]{1,0:T(8,128)(2,1)}, bf16[128,384]{1,0:T(8,128)(2,1)S(1)}, u32[]{:S(2)}) copy-start(bf16[128,384]{1,0:T(8,128)(2,1)S(1)} %get-tuple-element.51.refs_0_) | copy-start | bytes 294916
  34.7 8.4 %copy-start.21 = (bf16[128,1152]{1,0:T(8,128)(2,1)}, bf16[128,1152]{1,0:T(8,128)(2,1)S(1)}, u32[]{:S(2)}) copy-start(bf16[128,1152]{1,0:T(8,128)(2,1)S(1)} %get-tuple-element.59.refs_0_) | copy-start | bytes 884740
  34.7 8.4 %copy-start.23 = (f32[2,3,64,128]{3,2,1,0:T(8,128)}, f32[2,3,64,128]{3,2,1,0:T(8,128)S(1)}, u32[]{:S(2)}) copy-start(f32[2,3,64,128]{3,2,1,0:T(8,128)S(1)} %get-tuple-element.61.refs_2_) | copy-start | bytes 589828
  43.2 12.0 %collective-permute-start.5 = (bf16[320,768]{1,0:T(8,128)(2,1)}, bf16[320,768]{1,0:T(8,128)(2,1)}, u32[]{:S(2)}, u32[]{:S(2)}) collective-permute-start(bf16[320,768]{1,0:T(8,128)(2,1)} %bitcast.11.own_up), channel_id=1, source_target_pairs={{0,1},{1,0},{2,3},{3,2},{4,5},{5,4},{6,7},{7,6},{8,9},{9,8},{10,11... | collective-permute-start | bytes 1474568 | tf_op jit(solution)/shard_map/ppermute | solution.py:34
  57.8 15.5 %copy-start.28 = (bf16[2,1,384,384]{3,2,1,0:T(8,128)(2,1)}, bf16[2,1,384,384]{3,2,1,0:T(8,128)(2,1)S(1)}, u32[]{:S(2)}) copy-start(bf16[2,1,384,384]{3,2,1,0:T(8,128)(2,1)S(1)} %get-tuple-element.95) | copy-start | bytes 1769476
  57.8 15.5 %collective-permute-start.9 = (bf16[8,96,384]{2,1,0:T(8,128)(2,1)S(1)}, bf16[8,96,384]{2,1,0:T(8,128)(2,1)S(1)}, u32[]{:S(2)}, u32[]{:S(2)}) collective-permute-start(bf16[8,96,384]{2,1,0:T(8,128)(2,1)S(1)} %bitcast.168), channel_id=1, source_target_pairs={{0,8},{8,0},{16,24},{24,16},{1,9},{9,1},{17,25},{25,17},{2,10},{10... | collective-permute-start | bytes 1769480 | tf_op jit(solution)/shard_map/ppermute | solution.py:34
  58.8 11.0 %collective-permute-start.7 = (bf16[320,768]{1,0:T(8,128)(2,1)S(1)}, bf16[320,768]{1,0:T(8,128)(2,1)S(1)}, u32[]{:S(2)}, u32[]{:S(2)}) collective-permute-start(bf16[320,768]{1,0:T(8,128)(2,1)S(1)} %get-tuple-element.67), channel_id=1, source_target_pairs={{0,1},{1,0},{2,3},{3,2},{4,5},{5,4},{6,7},{7,6},{8,9},{9,8},{10,11... | collective-permute-start | bytes 1474568 | tf_op jit(solution)/shard_map/ppermute | solution.py:34
  60.3 9.4 %copy-start.17 = (bf16[768,1120]{0,1:T(8,128)(2,1)S(1)}, bf16[768,1120]{0,1:T(8,128)(2,1)}, u32[]{:S(2)}) copy-start(bf16[768,1120]{0,1:T(8,128)(2,1)} %param.14) | copy-start | bytes 5160964
  69.8 6.2 %collective-permute-start.10 = (bf16[8,96,384]{2,1,0:T(8,128)(2,1)}, bf16[8,96,384]{2,1,0:T(8,128)(2,1)}, u32[]{:S(2)}, u32[]{:S(2)}) collective-permute-start(bf16[8,96,384]{2,1,0:T(8,128)(2,1)} %bitcast.18), channel_id=1, source_target_pairs={{0,2},{2,0},{4,6},{6,4},{1,3},{3,1},{5,7},{7,5},{8,10},{10,8},{12,... | collective-permute-start | bytes 1769480 | tf_op jit(solution)/shard_map/ppermute | solution.py:34
  74.1 6.7 %collective-permute-start.11 = (bf16[8,96,768]{2,1,0:T(8,128)(2,1)}, bf16[8,96,768]{2,1,0:T(8,128)(2,1)}, u32[]{:S(2)}, u32[]{:S(2)}) collective-permute-start(bf16[8,96,768]{2,1,0:T(8,128)(2,1)} %bitcast.19), channel_id=1, source_target_pairs={{0,2},{2,0},{4,6},{6,4},{1,3},{3,1},{5,7},{7,5},{8,10},{10,8},{12,... | collective-permute-start | bytes 3538952 | tf_op jit(solution)/shard_map/ppermute | solution.py:34
  74.6 10.5 %collective-permute-start.8 = (bf16[160,1120]{1,0:T(8,128)(2,1)S(1)}, bf16[160,1120]{1,0:T(8,128)(2,1)S(1)}, u32[]{:S(2)}, u32[]{:S(2)}) collective-permute-start(bf16[160,1120]{1,0:T(8,128)(2,1)S(1)} %get-tuple-element.69), channel_id=1, source_target_pairs={{0,1},{1,0},{2,3},{3,2},{4,5},{5,4},{6,7},{7,6},{8,9},{9,8},{10,11... | collective-permute-start | bytes 1075208 | tf_op jit(solution)/shard_map/ppermute | solution.py:34
  75.3 11.1 %collective-permute-start.13 = (bf16[2,2,96,384]{3,2,1,0:T(8,128)(2,1)S(1)}, bf16[2,2,96,384]{3,2,1,0:T(8,128)(2,1)S(1)}, u32[]{:S(2)}, u32[]{:S(2)}) collective-permute-start(bf16[2,2,96,384]{3,2,1,0:T(8,128)(2,1)S(1)} %fusion.12), channel_id=1, source_target_pairs={{0,2},{2,0},{4,6},{6,4},{1,3},{3,1},{5,7},{7,5},{8,10},{10,8},{12,... | collective-permute-start | bytes 884744 | tf_op jit(solution)/shard_map/ppermute | solution.py:34
  77.1 22.7 %collective-permute-start.15 = (bf16[2,2,96,384]{3,2,0,1:T(8,128)(2,1)S(1)}, bf16[2,2,96,384]{3,2,0,1:T(8,128)(2,1)S(1)}, u32[]{:S(2)}, u32[]{:S(2)}) collective-permute-start(bf16[2,2,96,384]{3,2,0,1:T(8,128)(2,1)S(1)} %fusion.13), channel_id=1, source_target_pairs={{0,8},{8,0},{16,24},{24,16},{1,9},{9,1},{17,25},{25,17},{2,10},{10... | collective-permute-start | bytes 884744 | tf_op jit(solution)/shard_map/ppermute | solution.py:34
  82.0 16.2 %collective-permute-start.16 = (bf16[2,2,96,768]{3,2,0,1:T(8,128)(2,1)S(1)}, bf16[2,2,96,768]{3,2,0,1:T(8,128)(2,1)S(1)}, u32[]{:S(2)}, u32[]{:S(2)}) collective-permute-start(bf16[2,2,96,768]{3,2,0,1:T(8,128)(2,1)S(1)} %fusion.9), channel_id=1, source_target_pairs={{0,4},{2,6},{4,0},{6,2},{1,5},{3,7},{5,1},{7,3},{8,12},{10,14},{12... | collective-permute-start | bytes 1769480 | tf_op jit(solution)/shard_map/ppermute | solution.py:34
  85.2 19.8 %collective-permute-start.12 = (bf16[5,32,1120]{2,1,0:T(8,128)(2,1)S(1)}, bf16[5,32,1120]{2,1,0:T(8,128)(2,1)S(1)}, u32[]{:S(2)}, u32[]{:S(2)}) collective-permute-start(bf16[5,32,1120]{2,1,0:T(8,128)(2,1)S(1)} %bitcast.140), channel_id=1, source_target_pairs={{0,8},{8,16},{16,24},{24,0},{1,9},{9,17},{17,25},{25,1},{2,10},{10... | collective-permute-start | bytes 1075208 | tf_op jit(solution)/shard_map/ppermute | solution.py:29
  87.6 17.4 %copy-start.25 = (s32[5]{0:T(128)S(1)}, s32[5]{0:T(128)}, u32[]{:S(2)}) copy-start(s32[5]{0:T(128)} %and_select_fusion.1.shifts) | copy-start | bytes 64
  87.7 13.7 %collective-permute-start.14 = (bf16[2,96,384]{2,1,0:T(8,128)(2,1)S(1)}, bf16[2,96,384]{2,1,0:T(8,128)(2,1)S(1)}, u32[]{:S(2)}, u32[]{:S(2)}) collective-permute-start(bf16[2,96,384]{2,1,0:T(8,128)(2,1)S(1)} %fusion.21), channel_id=1, source_target_pairs={{0,4},{2,6},{4,0},{6,2},{1,5},{3,7},{5,1},{7,3},{8,12},{10,14},{12... | collective-permute-start | bytes 442376 | tf_op jit(solution)/shard_map/ppermute | solution.py:34
  98.3 10.3 %collective-permute-start.17 = (bf16[2,96,768]{2,1,0:T(8,128)(2,1)S(1)}, bf16[2,96,768]{2,1,0:T(8,128)(2,1)S(1)}, u32[]{:S(2)}, u32[]{:S(2)}) collective-permute-start(bf16[2,96,768]{2,1,0:T(8,128)(2,1)S(1)} %get-tuple-element.94), channel_id=1, source_target_pairs={{0,8},{8,0},{16,24},{24,16},{1,9},{9,1},{17,25},{25,17},{2,10},{10... | collective-permute-start | bytes 884744 | tf_op jit(solution)/shard_map/ppermute | solution.py:34
  99.8 6.8 %collective-permute-start.18 = (bf16[2,96,384]{2,1,0:T(8,128)(2,1)S(1)}, bf16[2,96,384]{2,1,0:T(8,128)(2,1)S(1)}, u32[]{:S(2)}, u32[]{:S(2)}) collective-permute-start(bf16[2,96,384]{2,1,0:T(8,128)(2,1)S(1)} %get-tuple-element.100), channel_id=1, source_target_pairs={{0,4},{2,6},{4,0},{6,2},{1,5},{3,7},{5,1},{7,3},{8,12},{10,14},{12... | collective-permute-start | bytes 442376 | tf_op jit(solution)/shard_map/ppermute | solution.py:34
  101.4 8.5 %collective-permute-start.21 = (bf16[96,384]{1,0:T(8,128)(2,1)S(1)}, bf16[96,384]{1,0:T(8,128)(2,1)S(1)}, u32[]{:S(2)}, u32[]{:S(2)}) collective-permute-start(bf16[96,384]{1,0:T(8,128)(2,1)S(1)} %fusion.30), channel_id=1, source_target_pairs={{0,16},{8,24},{16,0},{24,8},{1,17},{9,25},{17,1},{25,9},{2,18},{10... | collective-permute-start | bytes 221192 | tf_op jit(solution)/shard_map/ppermute | solution.py:34
  106.7 9.8 %collective-permute-start.20 = (bf16[96,384]{1,0:T(8,128)(2,1)S(1)}, bf16[96,384]{1,0:T(8,128)(2,1)S(1)}, u32[]{:S(2)}, u32[]{:S(2)}) collective-permute-start(bf16[96,384]{1,0:T(8,128)(2,1)S(1)} %fusion.31), channel_id=1, source_target_pairs={{0,16},{8,24},{16,0},{24,8},{1,17},{9,25},{17,1},{25,9},{2,18},{10... | collective-permute-start | bytes 221192 | tf_op jit(solution)/shard_map/ppermute | solution.py:34
  108.7 10.0 %collective-permute-start.19 = (bf16[96,768]{1,0:T(8,128)(2,1)S(1)}, bf16[96,768]{1,0:T(8,128)(2,1)S(1)}, u32[]{:S(2)}, u32[]{:S(2)}) collective-permute-start(bf16[96,768]{1,0:T(8,128)(2,1)S(1)} %fusion.24), channel_id=1, source_target_pairs={{0,16},{8,24},{16,0},{24,8},{1,17},{9,25},{17,1},{25,9},{2,18},{10... | collective-permute-start | bytes 442376 | tf_op jit(solution)/shard_map/ppermute | solution.py:34
  (23 other events, 57.7 us)
